TPU v7x, 32 devices: a whole 2x2x4 slice. The times are simulated.
32 devices in a mesh: group: 2 (over y), adapter: 4 (over x, core), tensor: 4 (over z).
Axes of the slice: x: 2, y: 2, z: 4, core: 2. Of those that a mesh axis runs over, the one named last changes fastest.
Arguments:
- queries: bfloat16 [512, 2, 8192], P(('group', 'adapter'), None, 'tensor'), parts along dimension 0, may hold values from -240 to 240
- token_key_rows: bfloat16 [512, 2, 1024], P(('group', 'adapter'), None, 'tensor'), parts along dimension 0, may hold values from -4 to 4
- token_value_rows: bfloat16 [512, 2, 1024], P(('group', 'adapter'), None, 'tensor'), parts along dimension 0, may hold values from -4 to 4
- cached_key_rows: bfloat16 [512, 128, 1024], P(('group', 'adapter'), None, 'tensor'), parts along dimension 0, may hold values from -4 to 4
- cached_value_rows: bfloat16 [512, 128, 1024], P(('group', 'adapter'), None, 'tensor'), parts along dimension 0, may hold values from -4 to 4
- cache_length: int32 [512], P(('group', 'adapter')), parts along dimension 0, may hold values from 16 to 128
- request_adapter: int32 [512], P(('group', 'adapter')), parts along dimension 0, may hold values from 0 to 15, as said below
- output_weight_matrix: bfloat16 [8192, 4096], P('tensor'), may hold values from -0.0625 to 0.0625
- adapter_down_weight: bfloat16 [32, 64, 8192], P(('group', 'adapter'), None, 'tensor'), parts along dimension 0, may hold values from -0.0625 to 0.0625
- adapter_up_weight: bfloat16 [32, 64, 4096], P(('group', 'adapter'), None, 'tensor'), parts along dimension 0, may hold values from -0.75 to 0.75
Outputs:
- mixed: bfloat16 [512, 2, 4096], P(('group', 'adapter'), None, 'tensor'), parts along dimension 0
There are 2 independent parts, one for each index of `group`. A program takes and returns all parts, laid end to end along the dimension named above; an argument that names none is the same for every part. Nothing has to cross between parts.
Inputs may be any that keep to these rules, and one draw needn't show every extreme that they name: `request_adapter`: adapter a is resident on owner a // 4. In every aligned block of 64 requests at most 32 requests name adapters of one owner.
All inputs are finite; a program needn't handle non-finite values.
Results may differ from a plain program's by a relative error of at most 0.014.
Values may be sent and summed in bfloat16 or wider, within the bound.
No kernel may reach another device: no remote copies, remote signals or barrier semaphores. Data moves between devices by JAX's collectives and lax.ppermute only.
A program may use at most 128 MiB of HBM per device.

v0:
```python
import math

import jax
import jax.numpy as jnp
from jax import lax
from jax.sharding import PartitionSpec as P

HEAD_DIM = 128


NEGATIVE = -1e30


def attend(
    queries, token_key_rows, token_value_rows, cached_key_rows, cached_value_rows, cache_length
):
    row_count, step_count, query_width = queries.shape
    groups = cached_key_rows.shape[2] // HEAD_DIM
    sharing = query_width // HEAD_DIM // groups
    cache_size = cached_key_rows.shape[1]
    scaling = 1.0 / math.sqrt(HEAD_DIM)
    query_heads = queries.reshape(row_count, step_count, groups, sharing, HEAD_DIM)
    cache_k = cached_key_rows.reshape(row_count, cache_size, groups, HEAD_DIM)
    cache_v = cached_value_rows.reshape(row_count, cache_size, groups, HEAD_DIM)
    fresh_k = token_key_rows.reshape(row_count, step_count, groups, HEAD_DIM)
    fresh_v = token_value_rows.reshape(row_count, step_count, groups, HEAD_DIM)
    cache_scores = (
        jnp.einsum("rsgqd,rlgd->rsgql", query_heads, cache_k, preferred_element_type=jnp.float32)
        * scaling
    )
    fresh_scores = (
        jnp.einsum("rsgqd,rtgd->rsgqt", query_heads, fresh_k, preferred_element_type=jnp.float32)
        * scaling
    )
    positions = jnp.arange(cache_size, dtype=jnp.int32)
    live_cache = (positions[None, :] < cache_length[:, None])[:, None, None, None, :]
    tokens = jnp.arange(step_count, dtype=jnp.int32)
    live_fresh = (tokens[None, :] <= tokens[:, None])[None, :, None, None, :]
    cache_scores = jnp.where(live_cache, cache_scores, NEGATIVE)
    fresh_scores = jnp.where(live_fresh, fresh_scores, NEGATIVE)
    highest = jnp.maximum(jnp.max(cache_scores, axis=-1), jnp.max(fresh_scores, axis=-1))
    cache_weight = jnp.exp(cache_scores - highest[..., None])
    fresh_weight = jnp.exp(fresh_scores - highest[..., None])
    denominator = jnp.sum(cache_weight, axis=-1) + jnp.sum(fresh_weight, axis=-1)
    numerator = jnp.einsum(
        "rsgql,rlgd->rsgqd",
        cache_weight.astype(jnp.bfloat16),
        cache_v,
        preferred_element_type=jnp.float32,
    )
    numerator = numerator + jnp.einsum(
        "rsgqt,rtgd->rsgqd",
        fresh_weight.astype(jnp.bfloat16),
        fresh_v,
        preferred_element_type=jnp.float32,
    )
    attended = (numerator / denominator[..., None]).astype(jnp.bfloat16)
    return attended.reshape(row_count, step_count, query_width)


def adapter_contributions(
    incoming_rows, incoming_adapter_index, adapter_down_weight, adapter_up_weight
):
    request_count, step_count, feature_count = incoming_rows.shape
    resident_adapters, adapter_rank_width, leftover_width = adapter_down_weight.shape
    local_id = incoming_adapter_index - lax.axis_index("adapter") * resident_adapters
    picked = (local_id[:, None] == jnp.arange(resident_adapters, dtype=jnp.int32)[None, :]).astype(
        jnp.float32
    )
    partial_results = jnp.einsum(
        "bth,yph->btyp", incoming_rows, adapter_down_weight, preferred_element_type=jnp.float32
    )
    masked = (partial_results * picked[:, None, :, None]).reshape(
        request_count, step_count, resident_adapters * adapter_rank_width
    )
    low_rank = lax.psum(masked.astype(jnp.bfloat16), "tensor")
    spread_rows = low_rank.reshape(request_count, step_count, resident_adapters, adapter_rank_width)
    return jnp.einsum(
        "vhzp,zpg->vhg", spread_rows, adapter_up_weight, preferred_element_type=jnp.float32
    )


def body(
    queries,
    token_key_rows,
    token_value_rows,
    cached_key_rows,
    cached_value_rows,
    cache_length,
    request_adapter,
    output_weight_matrix,
    adapter_down_weight,
    adapter_up_weight,
):
    attended = attend(
        queries, token_key_rows, token_value_rows, cached_key_rows, cached_value_rows, cache_length
    )
    row_count, step_count, feature_count = attended.shape
    partial_out = jnp.dot(
        attended.reshape(row_count * step_count, feature_count),
        output_weight_matrix,
        preferred_element_type=jnp.float32,
    ).reshape(row_count, step_count, -1)
    base = lax.psum_scatter(
        partial_out.astype(jnp.bfloat16), "tensor", scatter_dimension=2, tiled=True
    ).astype(jnp.float32)
    owner_count = lax.axis_size("adapter")
    capacity = max(2, 2 * row_count // owner_count)
    resident_adapters = adapter_down_weight.shape[0]
    owner_of = request_adapter // resident_adapters
    member = (owner_of[:, None] == jnp.arange(owner_count, dtype=jnp.int32)[None, :]).astype(
        jnp.int32
    )
    earlier = jnp.cumsum(member, axis=0) - member
    slot_of = jnp.sum(earlier * member, axis=1)
    target = owner_of * capacity + slot_of
    placing = jnp.arange(owner_count * capacity, dtype=jnp.int32)[:, None] == target[None, :]
    send_rows = jnp.einsum(
        "cr,rsf->csf", placing.astype(jnp.bfloat16), attended, preferred_element_type=jnp.float32
    ).astype(jnp.bfloat16)
    send_ids = jnp.sum(jnp.where(placing, request_adapter[None, :] + 1, 0), axis=1) - 1
    send_rows = send_rows.reshape(owner_count, capacity, step_count, feature_count)
    send_ids = send_ids.reshape(owner_count, capacity)
    got_rows = lax.all_to_all(send_rows, "adapter", split_axis=0, concat_axis=0, tiled=True)
    got_ids = lax.all_to_all(send_ids, "adapter", split_axis=0, concat_axis=0, tiled=True)
    source_count, slot_count = got_ids.shape
    served = adapter_contributions(
        got_rows.reshape(source_count * slot_count, step_count, feature_count),
        got_ids.reshape(source_count * slot_count),
        adapter_down_weight,
        adapter_up_weight,
    )
    answered = served.reshape(source_count, slot_count, step_count, -1)
    returned = lax.all_to_all(
        answered.astype(jnp.bfloat16), "adapter", split_axis=0, concat_axis=0, tiled=True
    ).astype(answered.dtype)
    low_rank_update = jnp.take(
        returned.reshape(owner_count * capacity, step_count, -1), target, axis=0
    )
    return (base + low_rank_update).astype(jnp.bfloat16)


def solution(mesh):
    return jax.shard_map(
        body,
        mesh=mesh,
        in_specs=(
            P(("group", "adapter"), None, "tensor"),
            P(("group", "adapter"), None, "tensor"),
            P(("group", "adapter"), None, "tensor"),
            P(("group", "adapter"), None, "tensor"),
            P(("group", "adapter"), None, "tensor"),
            P(("group", "adapter")),
            P(("group", "adapter")),
            P("tensor", None),
            P(("group", "adapter"), None, "tensor"),
            P(("group", "adapter"), None, "tensor"),
        ),
        out_specs=P(("group", "adapter"), None, "tensor"),
        check_vma=False,
    )
```

profile of v0, /device:TPU:0, one launch (start us, length us, event | category | flops | bytes accessed | tf_op | source)
XLA Modules:
  0.0 136.4 jit_solution(15603949717665767445)
XLA Ops:
  6.5 0.8 broadcast_add_fusion.1
  7.8 0.7 sub.51
  8.4 4.2 %all-to-all-start.1 = ((s32[4,1,32]{2,1,0:T(1,128)}), s32[4,1,32]{2,1,0:T(1,128)S(1)}, u32[]{:S(2)}, u32[]{:S(2)}) async-start(s32[4,1,32]{2,1,0:T(1,128)} %bitcast.18), calls=%async_computation.2 | async-start | bytes 4096 | tf_op jit(solution)/shard_map/all_to_all | solution.py:125
  12.7 1.4 %reshape.133 = bf16[64,2,2,8,128]{4,3,2,1,0:T(8,128)(2,1)S(1)} reshape(bf16[64,2,2048]{2,1,0:T(2,128)(2,1)} %param.10) | data formatting | bytes 1048576 | tf_op jit(solution)/shard_map/reshape | solution.py:22
  14.0 6.9 %reshape.132 = bf16[64,128,2,128]{3,2,1,0:T(2,128)(2,1)} reshape(bf16[64,128,256]{2,1,0:T(8,128)(2,1)} %param.13) | data formatting | bytes 8388608 | tf_op jit(solution)/shard_map/reshape | solution.py:23
  21.1 4.6 %fusion.57 = (f32[64,2,2,8]{3,1,2,0:T(2,128)S(1)}, f32[64,2,2,8,128]{4,3,1,2,0:T(8,128)S(1)}) fusion(bf16[64,2,2,8,128]{4,3,2,1,0:T(8,128)(2,1)S(1)} %reshape.133, bf16[64,128,2,128,1]{3,2,1,0,4:T(2,128)(2,1)} %bitcast.71, pred[64,128]{1,0:T(8,128)(4,1)S(1)} %iota_compare_fusion.2), kind=kOutput, calls=%fused_computation.64 | convolution fusion | flops 67893248 | bytes 5783552 | tf_op jit(solution)/shard_map/rsgqd,rlgd->rsgql/dot_general | solution.py:28
  25.7 2.5 %fusion.58 = (f32[64,2,2,8]{3,1,2,0:T(2,128)S(1)}, f32[64,2,2,8,2]{3,4,1,2,0:T(2,128)S(1)}) fusion(bf16[64,2,2,8,128]{4,3,2,1,0:T(8,128)(2,1)S(1)} %reshape.133, bf16[64,2,256]{2,1,0:T(2,128)(2,1)S(1)} %copy-done.4, pred[2,2]{1,0:T(4,128)(4,1)S(1)} %iota_compare_fusion.4), kind=kOutput, calls=%fused_computation.65 | convolution fusion | flops 1058816 | bytes 614404 | tf_op jit(solution)/shard_map/rsgqd,rtgd->rsgqt/dot_general | solution.py:32
  28.2 0.8 fusion.36
  30.0 6.9 %reshape.135 = bf16[64,128,2,128]{3,2,1,0:T(2,128)(2,1)} reshape(bf16[64,128,256]{2,1,0:T(8,128)(2,1)} %param.14) | data formatting | bytes 8388608 | tf_op jit(solution)/shard_map/reshape | solution.py:24
  37.0 3.4 %fusion.32 = bf16[64,2,2,8,128]{4,3,1,2,0:T(8,128)(2,1)S(1)} fusion(f32[64,2,2,8,128]{4,3,2,1,0:T(8,128)S(1)} %fusion.47, bf16[64,128,2,128,1]{3,2,1,0,4:T(2,128)(2,1)} %bitcast.70, f32[64,2,2,8,128]{4,3,1,2,0:T(8,128)S(1)} %get-tuple-element.10, f32[64,2,2,8]{3,1,2,0:T(2,128)S(1)} %add.49, f32[64,2,2,8]{3,1,2,0:T(2,128)S(1)} %max.7), kind=kOutput, calls=%fused_computation.23 | convolution fusion | flops 68419584 | bytes 6832128 | tf_op jit(solution)/shard_map/rsgql,rlgd->rsgqd/dot_general | solution.py:45
  41.3 1.1 copy.39
  42.3 3.5 %all-to-all-start = ((bf16[4,32,2,2048]{3,1,2,0:T(8,128)(2,1)}), bf16[4,32,2,2048]{3,1,2,0:T(8,128)(2,1)S(1)}, u32[]{:S(2)}, u32[]{:S(2)}) async-start(bf16[4,32,2,2048]{3,1,2,0:T(8,128)(2,1)} %copy.39), calls=%async_computation.1 | async-start | bytes 2097152 | tf_op jit(solution)/shard_map/all_to_all | solution.py:124
  46.0 14.3 %all-to-all-done = bf16[4,32,2,2048]{3,1,2,0:T(8,128)(2,1)S(1)} async-done(((bf16[4,32,2,2048]{3,1,2,0:T(8,128)(2,1)}), bf16[4,32,2,2048]{3,1,2,0:T(8,128)(2,1)S(1)}, u32[]{:S(2)}, u32[]{:S(2)}) %all-to-all-start) | async-done | bytes 1048608 | tf_op jit(solution)/shard_map/all_to_all | solution.py:124
  61.1 0.7 copy.43
  61.9 9.2 %fusion.2 = bf16[64,2,4096]{2,0,1:T(8,128)(2,1)} fusion(bf16[64,2,2048]{2,0,1:T(8,128)(2,1)S(1)} %dot_general.34, bf16[2048,4096]{1,0:T(8,128)(2,1)} %param.17), kind=kOutput, calls=%fused_computation.3 | convolution fusion | flops 2148007936 | bytes 18350080 | tf_op jit(solution)/shard_map/dot_general | solution.py:99
  71.1 27.0 %all-reduce.2.cloned.1.call-done = bf16[4,32,2,64,4]{3,1,4,2,0:T(8,128)(2,1)} async-done(((bf16[4,32,2,64,4]{3,1,4,2,0:T(8,128)(2,1)}), bf16[4,32,2,64,4]{3,1,4,2,0:T(8,128)(2,1)}) %all-reduce.2.cloned.1.call-update) | async-done | bytes 131088 | tf_op jit(solution)/shard_map/psum | solution.py:76
  98.1 2.1 %fusion.18 = bf16[4,32,2,1024]{3,1,2,0:T(8,128)(2,1)} fusion(bf16[4,32,2,64,4]{3,1,4,2,0:T(8,128)(2,1)} %all-reduce.2.cloned.1.call-done, bf16[4,64,1024]{2,1,0:T(8,128)(2,1)S(1)} %copy-done.3), kind=kOutput, calls=%fused_computation.13 | convolution fusion | flops 134479872 | bytes 1179648 | tf_op jit(solution)/shard_map/vhzp,zpg->vhg/dot_general | solution.py:78
  100.2 3.5 %all-to-all-start.2 = ((bf16[4,32,2,1024]{3,1,2,0:T(8,128)(2,1)}), bf16[4,32,2,1024]{3,1,2,0:T(8,128)(2,1)S(1)}, u32[]{:S(2)}, u32[]{:S(2)}) async-start(bf16[4,32,2,1024]{3,1,2,0:T(8,128)(2,1)} %fusion.18), calls=%async_computation.3 | async-start | bytes 1048576 | tf_op jit(solution)/shard_map/all_to_all | solution.py:134
  103.7 8.8 %all-to-all-done.2 = bf16[4,32,2,1024]{3,1,2,0:T(8,128)(2,1)S(1)} async-done(((bf16[4,32,2,1024]{3,1,2,0:T(8,128)(2,1)}), bf16[4,32,2,1024]{3,1,2,0:T(8,128)(2,1)S(1)}, u32[]{:S(2)}, u32[]{:S(2)}) %all-to-all-start.2) | async-done | bytes 524320 | tf_op jit(solution)/shard_map/all_to_all | solution.py:134
  112.6 0.8 copy.45
  113.5 1.1 gather_fusion
  114.6 12.9 %reduce-scatter.2.cloned.1.call-done = bf16[64,2,1024]{2,0,1:T(8,128)(2,1)} async-done(((bf16[64,2,4096]{2,0,1:T(8,128)(2,1)}), bf16[64,2,1024]{2,0,1:T(8,128)(2,1)}) %reduce-scatter.2.cloned.1.call-update) | async-done | bytes 262160 | tf_op jit(solution)/shard_map/reduce_scatter | solution.py:104
  127.4 1.2 fusion.41
  128.6 1.0 copy.47
  (39 shorter events, 3.6 us)
Async XLA Ops:
  6.5 53.9 %copy-start = (bf16[4,64,2048]{2,1,0:T(8,128)(2,1)S(1)}, bf16[4,64,2048]{2,1,0:T(8,128)(2,1)}, u32[]{:S(2)}) copy-start(bf16[4,64,2048]{2,1,0:T(8,128)(2,1)} %param.18) | copy-start | bytes 3145732
  8.4 33.9 %all-to-all-start.1 = ((s32[4,1,32]{2,1,0:T(1,128)}), s32[4,1,32]{2,1,0:T(1,128)S(1)}, u32[]{:S(2)}, u32[]{:S(2)}) async-start(s32[4,1,32]{2,1,0:T(1,128)} %bitcast.18), calls=%async_computation.2 | async-start | bytes 4096 | tf_op jit(solution)/shard_map/all_to_all | solution.py:125
  14.0 6.9 %copy-start.2 = (s32[64]{0:T(128)S(1)}, s32[64]{0:T(128)}, u32[]{:S(2)}) copy-start(s32[64]{0:T(128)} %param.15) | copy-start | bytes 772
  21.0 4.7 %copy-start.4 = (bf16[64,2,256]{2,1,0:T(2,128)(2,1)S(1)}, bf16[64,2,256]{2,1,0:T(2,128)(2,1)}, u32[]{:S(2)}) copy-start(bf16[64,2,256]{2,1,0:T(2,128)(2,1)} %param.11) | copy-start | bytes 196612
  21.1 8.5 %copy-start.1 = (bf16[64,2,256]{2,1,0:T(2,128)(2,1)S(1)}, bf16[64,2,256]{2,1,0:T(2,128)(2,1)}, u32[]{:S(2)}) copy-start(bf16[64,2,256]{2,1,0:T(2,128)(2,1)} %param.12) | copy-start | bytes 196612
  42.3 18.0 %all-to-all-start = ((bf16[4,32,2,2048]{3,1,2,0:T(8,128)(2,1)}), bf16[4,32,2,2048]{3,1,2,0:T(8,128)(2,1)S(1)}, u32[]{:S(2)}, u32[]{:S(2)}) async-start(bf16[4,32,2,2048]{3,1,2,0:T(8,128)(2,1)} %copy.39), calls=%async_computation.1 | async-start | bytes 2097152 | tf_op jit(solution)/shard_map/all_to_all | solution.py:124
  45.9 52.3 %all-reduce.2.cloned.1.call-start = ((), (), s32[]{:S(2)}) async-start(), calls=%async_computation.5 | async-start | bytes 524288 | tf_op jit(solution)/shard_map/psum | solution.py:76
  61.8 36.3 %copy-start.3 = (bf16[4,64,1024]{2,1,0:T(8,128)(2,1)S(1)}, bf16[4,64,1024]{2,1,0:T(8,128)(2,1)}, u32[]{:S(2)}) copy-start(bf16[4,64,1024]{2,1,0:T(8,128)(2,1)} %param.19) | copy-start | bytes 1572868
  61.9 65.6 %reduce-scatter.2.cloned.1.call-start = ((), (), s32[]{:S(2)}) async-start(), calls=%async_computation.4 | async-start | bytes 1310720 | tf_op jit(solution)/shard_map/reduce_scatter | solution.py:104
  100.2 12.3 %all-to-all-start.2 = ((bf16[4,32,2,1024]{3,1,2,0:T(8,128)(2,1)}), bf16[4,32,2,1024]{3,1,2,0:T(8,128)(2,1)S(1)}, u32[]{:S(2)}, u32[]{:S(2)}) async-start(bf16[4,32,2,1024]{3,1,2,0:T(8,128)(2,1)} %fusion.18), calls=%async_computation.3 | async-start | bytes 1048576 | tf_op jit(solution)/shard_map/all_to_all | solution.py:134
Sparse Core Ops, SparseCore 0:
  62.0 36.1 all-reduce.1
  100.5 26.8 reduce-scatter.1
where the time goes:
time: 137 us; the launch traced here: 136 us
  waiting for transfers between devices  63 us (46%)
  matrix products  23.2 us (17%)
  local copies, waits for them, and re-layouts  21.4 us (16%)
  between operations  13.6 us (10%)
  starting transfers between devices  11.3 us (8%)
  other arithmetic  3.92 us (3%)
    psum x1, waiting for transfers between devices, adapter_contributions(): low_rank = lax.psum(masked.astype(jnp.bfloat16), 'tensor')  27 us
    all_to_all x1, waiting for transfers between devices, body(): lax.all_to_all(send_rows, 'adapter', split_axis=0, concat_axis=0, tiled=T...  14.3 us
    reduce_scatter x1, waiting for transfers between devices, body(): lax.psum_scatter(partial_out.astype(jnp.bfloat16), 'tensor', scatter_dime...  12.9 us
    dot_general x1, matrix products, body(): jnp.dot(attended.reshape(row_count * step_count, feature_count), output_w...  9.15 us
    all_to_all x1, waiting for transfers between devices, body(): lax.all_to_all(answered.astype(jnp.bfloat16), 'adapter', split_axis=0, co...  8.79 us
    reshape x1, local copies, waits for them, and re-layouts, attend(): cache_k = cached_key_rows.reshape(row_count, cache_size, groups, HEAD_DIM)  6.93 us
    reshape x1, local copies, waits for them, and re-layouts, attend(): cache_v = cached_value_rows.reshape(row_count, cache_size, groups, HEAD_DIM)  6.93 us
    dot_general x1, matrix products, attend(): jnp.einsum('rsgqd,rlgd->rsgql', query_heads, cache_k, preferred_element_t...  4.63 us
  transfers between devices with their start and end apart: 5, of which 4 were waited for; matrix products, arithmetic and copies ran while one was open for 32% of the time, Pallas kernels for 0%

commit v1 on v0

v1 whole, which is shorter than its diff:
```python
import functools
import math

import jax
import jax.numpy as jnp
from jax import lax
from jax.experimental import pallas as pl
from jax.experimental.pallas import tpu as pltpu
from jax.sharding import PartitionSpec as P

HEAD_DIM = 128
NEGATIVE = -1e30
LANES = 128
VMEM_LIMIT = 56 * 1024 * 1024

F32 = jnp.float32
BF16 = jnp.bfloat16


def contract(a, b, a_dim, b_dim):
    return lax.dot_general(
        a, b, (((a_dim,), (b_dim,)), ((), ())), preferred_element_type=F32
    )


def attend_kernel(
    owners,
    resident,
    capacity,
    lengths,
    place,
    adapters,
    queries,
    fresh_k,
    fresh_v,
    cache_k,
    cache_v,
    attended,
    placing_out,
    *rest,
):
    packed = rest[:owners]
    query_scratch, result_scratch = rest[owners:]
    step = pl.program_id(0)
    block, steps, width = queries.shape
    heads = width // HEAD_DIM
    groups = cache_k.shape[2] // HEAD_DIM
    sharing = heads // groups
    cache_size = cache_k.shape[1]
    rows = block * steps
    total_rows = attended.shape[0]
    span = steps * sharing
    scaling = 1.0 / math.sqrt(HEAD_DIM)

    flat = queries[...].astype(F32).reshape(rows, width)
    for h in range(heads):
        query_scratch[h * rows : (h + 1) * rows, :] = flat[:, h * HEAD_DIM : (h + 1) * HEAD_DIM]
    new_k = fresh_k[...].reshape(rows, groups * HEAD_DIM)
    new_v = fresh_v[...].reshape(rows, groups * HEAD_DIM)

    positions = lax.broadcasted_iota(jnp.int32, (span, cache_size), 1)
    row_id = lax.broadcasted_iota(jnp.int32, (block * span, rows), 0)
    col_id = lax.broadcasted_iota(jnp.int32, (block * span, rows), 1)
    same = lax.div(row_id, span) == lax.div(col_id, steps)
    causal = lax.rem(col_id, steps) <= lax.div(lax.rem(row_id, span), sharing)
    live_fresh = jnp.logical_and(same, causal)

    for g in range(groups):
        lane = slice(g * HEAD_DIM, (g + 1) * HEAD_DIM)
        parts = []
        for r in range(block):
            for s in range(steps):
                start = g * sharing * rows + r * steps + s
                parts.append(query_scratch[pl.ds(start, sharing, stride=rows), :])
        q = jnp.concatenate(parts, axis=0).astype(BF16)
        fresh = contract(q, new_k[:, lane], 1, 1) * scaling
        fresh = jnp.where(live_fresh, fresh, NEGATIVE)
        cached = []
        for r in range(block):
            score = contract(q[r * span : (r + 1) * span], cache_k[r, :, lane], 1, 1) * scaling
            cached.append(jnp.where(positions < lengths[step * block + r], score, NEGATIVE))
        cached = jnp.concatenate(cached, axis=0)
        top = jnp.maximum(
            jnp.max(cached, axis=1, keepdims=True), jnp.max(fresh, axis=1, keepdims=True)
        )
        cached = jnp.exp(cached - top)
        fresh = jnp.exp(fresh - top)
        total = jnp.sum(cached, axis=1, keepdims=True) + jnp.sum(fresh, axis=1, keepdims=True)
        cached = cached.astype(BF16)
        out = contract(fresh.astype(BF16), new_v[:, lane], 1, 0)
        out_cached = [
            contract(cached[r * span : (r + 1) * span], cache_v[r, :, lane], 1, 0)
            for r in range(block)
        ]
        out = (out + jnp.concatenate(out_cached, axis=0)) / total
        for r in range(block):
            for s in range(steps):
                start = g * sharing * total_rows + (step * block + r) * steps + s
                piece = out[r * span + s * sharing : r * span + (s + 1) * sharing]
                result_scratch[pl.ds(start, sharing, stride=total_rows), :] = piece

    @pl.when(step == pl.num_programs(0) - 1)
    def _():
        for h in range(heads):
            attended[:, h * HEAD_DIM : (h + 1) * HEAD_DIM] = result_scratch[
                h * total_rows : (h + 1) * total_rows, :
            ].astype(BF16)
        requests = total_rows // steps
        named = adapters[...]
        owner = lax.div(named, resident)
        local = named - owner * resident
        relative = jnp.bitwise_xor(owner, place[0])
        owner_id = lax.broadcasted_iota(jnp.int32, (owners, requests), 0)
        member = (owner_id == relative).astype(F32)
        before = lax.broadcasted_iota(jnp.int32, (requests, requests), 0) < (
            lax.broadcasted_iota(jnp.int32, (requests, requests), 1)
        )
        earlier = contract(member.astype(BF16), before.astype(BF16), 1, 0)
        slot = jnp.sum(earlier * member, axis=0, keepdims=True)
        facts = jnp.concatenate(
            [relative.astype(F32), slot, local.astype(F32), jnp.zeros((5, requests), F32)], axis=0
        )
        spread = lax.broadcasted_iota(jnp.int32, (requests, total_rows), 0) == lax.div(
            lax.broadcasted_iota(jnp.int32, (requests, total_rows), 1), steps
        )
        facts = contract(facts.astype(BF16), spread.astype(BF16), 1, 0).astype(jnp.int32)
        token = lax.rem(lax.broadcasted_iota(jnp.int32, (1, total_rows), 1), steps)
        target = (facts[0:1] * capacity + facts[1:2]) * steps + token
        slots = owners * capacity * steps
        placing = (
            lax.broadcasted_iota(jnp.int32, (slots, total_rows), 0) == target
        ).astype(BF16)
        placing_out[...] = placing
        chosen = (
            lax.broadcasted_iota(jnp.int32, (LANES, total_rows), 0) == facts[2:3]
        ).astype(BF16)
        per = capacity * steps
        marks = contract(placing, chosen, 1, 1).astype(BF16)
        tile = 512
        for c in range(0, width, tile):
            moved = contract(placing, attended[:, c : c + tile], 1, 0).astype(BF16)
            for k in range(owners):
                packed[k][:, c : c + tile] = moved[k * per : (k + 1) * per]
        for k in range(owners):
            packed[k][:, width:] = marks[k * per : (k + 1) * per]


def attend(queries, fresh_k, fresh_v, cache_k, cache_v, lengths, place, adapters, owners, resident):
    requests, steps, width = queries.shape
    cache_size, kv_width = cache_k.shape[1:]
    capacity = max(2, 2 * requests // owners)
    block = 8
    heads = width // HEAD_DIM
    total_rows = requests * steps
    per = capacity * steps
    whole = lambda shape: pl.BlockSpec(shape, lambda i, *_: (0,) * len(shape))
    return pl.pallas_call(
        functools.partial(attend_kernel, owners, resident, capacity),
        grid_spec=pltpu.PrefetchScalarGridSpec(
            num_scalar_prefetch=2,
            grid=(requests // block,),
            in_specs=[
                whole((1, requests)),
                pl.BlockSpec((block, steps, width), lambda i, *_: (i, 0, 0)),
                pl.BlockSpec((block, steps, kv_width), lambda i, *_: (i, 0, 0)),
                pl.BlockSpec((block, steps, kv_width), lambda i, *_: (i, 0, 0)),
                pl.BlockSpec((block, cache_size, kv_width), lambda i, *_: (i, 0, 0)),
                pl.BlockSpec((block, cache_size, kv_width), lambda i, *_: (i, 0, 0)),
            ],
            out_specs=[whole((total_rows, width)), whole((owners * per, total_rows))]
            + [whole((per, width + LANES))] * owners,
            scratch_shapes=[
                pltpu.VMEM((heads * block * steps, HEAD_DIM), F32),
                pltpu.VMEM((heads * total_rows, HEAD_DIM), F32),
            ],
        ),
        out_shape=[
            jax.ShapeDtypeStruct((total_rows, width), BF16),
            jax.ShapeDtypeStruct((owners * per, total_rows), BF16),
        ]
        + [jax.ShapeDtypeStruct((per, width + LANES), BF16)] * owners,
        compiler_params=pltpu.CompilerParams(vmem_limit_bytes=VMEM_LIMIT),
        cost_estimate=pl.CostEstimate(
            flops=8 * total_rows * width * cache_size,
            bytes_accessed=4 * requests * cache_size * kv_width,
            transcendentals=0,
        ),
        name="attend",
    )(lengths, place, adapters.reshape(1, requests), queries, fresh_k, fresh_v, cache_k, cache_v)


def project_kernel(column, attended, weight, out):
    out[...] = contract(attended[...], weight[...], 1, 0).astype(BF16)


def project(attended, weight, column, tile, blocks):
    rows, depth = attended.shape
    columns = weight.shape[1] // blocks
    tiles = columns // tile
    return pl.pallas_call(
        project_kernel,
        grid_spec=pltpu.PrefetchScalarGridSpec(
            num_scalar_prefetch=1,
            grid=(tiles,),
            in_specs=[
                pl.BlockSpec((rows, depth), lambda i, c: (0, 0)),
                pl.BlockSpec((depth, tile), lambda i, c: (0, c[0] * tiles + i)),
            ],
            out_specs=pl.BlockSpec((rows, tile), lambda i, c: (0, i)),
        ),
        out_shape=jax.ShapeDtypeStruct((rows, columns), BF16),
        compiler_params=pltpu.CompilerParams(vmem_limit_bytes=VMEM_LIMIT),
        cost_estimate=pl.CostEstimate(
            flops=2 * rows * depth * columns,
            bytes_accessed=2 * depth * columns,
            transcendentals=0,
        ),
        name="project",
    )(column, attended, weight)


def low_kernel(owners, resident, down, *refs):
    packed = refs[:owners]
    low_out, marks_out = refs[owners:]
    depth = down.shape[1]
    rank = down.shape[0] // resident
    per = packed[0].shape[0]
    weight = down[...]
    lows = []
    for k in range(owners):
        every = contract(packed[k][:, :depth], weight, 1, 1)
        marks = packed[k][:, depth:]
        marks_out[k * per : (k + 1) * per, :] = marks
        marks = marks.astype(F32)
        low = every[:, :rank] * marks[:, 0:1]
        for y in range(1, resident):
            low = low + every[:, y * rank : (y + 1) * rank] * marks[:, y : y + 1]
        lows.append(low)
    half = owners // 2
    low_out[...] = jnp.concatenate(
        [jnp.concatenate(lows[:half], axis=0), jnp.concatenate(lows[half:], axis=0)], axis=1
    ).astype(BF16)


def low_partial(packed, down, owners):
    resident, rank, depth = down.shape
    per = packed[0].shape[0]
    slots = owners * per
    return pl.pallas_call(
        functools.partial(low_kernel, owners, resident),
        out_shape=[
            jax.ShapeDtypeStruct((slots // 2, 2 * rank), BF16),
            jax.ShapeDtypeStruct((slots, LANES), BF16),
        ],
        compiler_params=pltpu.CompilerParams(vmem_limit_bytes=VMEM_LIMIT),
        cost_estimate=pl.CostEstimate(
            flops=2 * slots * depth * resident * rank,
            bytes_accessed=2 * depth * resident * rank,
            transcendentals=0,
        ),
        name="low",
    )(down.reshape(resident * rank, depth), *packed)


def delta_kernel(owners, resident, marks, up, *refs):
    outs = refs[len(refs) - owners :]
    partials = refs[: len(refs) - owners]
    low = partials[0][...].astype(F32)
    for part in partials[1:]:
        low = low + part[...].astype(F32)
    rank = low.shape[1] // 2
    low = low.astype(BF16).astype(F32)
    low = jnp.concatenate([low[:, :rank], low[:, rank:]], axis=0)
    chosen = marks[...].astype(F32)
    spread = jnp.concatenate(
        [low * chosen[:, y : y + 1] for y in range(resident)], axis=1
    ).astype(BF16)
    answer = contract(spread, up[...], 1, 0).astype(BF16)
    per = answer.shape[0] // owners
    for k in range(owners):
        outs[k][...] = answer[k * per : (k + 1) * per]


def delta(marks, up, partials, owners):
    resident, rank, columns = up.shape
    slots = marks.shape[0]
    return pl.pallas_call(
        functools.partial(delta_kernel, owners, resident),
        out_shape=[jax.ShapeDtypeStruct((slots // owners, columns), BF16)] * owners,
        compiler_params=pltpu.CompilerParams(vmem_limit_bytes=VMEM_LIMIT),
        cost_estimate=pl.CostEstimate(
            flops=2 * slots * columns * resident * rank,
            bytes_accessed=2 * columns * resident * rank,
            transcendentals=0,
        ),
        name="delta",
    )(marks, up.reshape(resident * rank, columns), *partials)


def combine_kernel(owners, placing, *refs):
    answers = refs[:owners]
    partials = refs[owners:-1]
    out = refs[-1]
    base = partials[0][...].astype(F32)
    for part in partials[1:]:
        base = base + part[...].astype(F32)
    answer = jnp.concatenate([a[...] for a in answers], axis=0)
    base = base + contract(placing[...], answer, 0, 0)
    out[...] = base.astype(BF16)


def combine(placing, answers, partials):
    rows, columns = partials[0].shape
    return pl.pallas_call(
        functools.partial(combine_kernel, len(answers)),
        out_shape=jax.ShapeDtypeStruct((rows, columns), BF16),
        compiler_params=pltpu.CompilerParams(vmem_limit_bytes=VMEM_LIMIT),
        name="combine",
    )(placing, *answers, *partials)


def swap(value, axis, k):
    count = lax.axis_size(axis)
    return lax.ppermute(value, axis, [(i, i ^ k) for i in range(count)])


def body(
    queries,
    token_key_rows,
    token_value_rows,
    cached_key_rows,
    cached_value_rows,
    cache_length,
    request_adapter,
    output_weight_matrix,
    adapter_down_weight,
    adapter_up_weight,
):
    requests, steps, _ = queries.shape
    owners = lax.axis_size("adapter")
    blocks = lax.axis_size("tensor")
    resident = adapter_down_weight.shape[0]
    place = lax.axis_index("adapter").reshape(1)
    mine = lax.axis_index("tensor")

    attended, placing, *packed = attend(
        queries,
        token_key_rows,
        token_value_rows,
        cached_key_rows,
        cached_value_rows,
        cache_length,
        place,
        request_adapter,
        owners,
        resident,
    )
    columns = output_weight_matrix.shape[1] // blocks
    tile = min(512, columns)
    far_first = list(range(blocks - 1, 0, -1))
    partials = {}
    for k in far_first:
        column = jnp.bitwise_xor(mine, k).reshape(1)
        partials[k] = swap(
            project(attended, output_weight_matrix, column, tile, blocks), "tensor", k
        )
    arrived = {0: packed[0]}
    for k in range(owners - 1, 0, -1):
        arrived[k] = swap(packed[k], "adapter", k)
    own = project(attended, output_weight_matrix, mine.reshape(1), tile, blocks)
    low, marks = low_partial([arrived[k] for k in range(owners)], adapter_down_weight, owners)
    lows = [low] + [swap(low, "tensor", k) for k in far_first]
    answers = delta(marks, adapter_up_weight, lows, owners)
    returned = [answers[0]] + [None] * (owners - 1)
    for k in range(owners - 1, 0, -1):
        returned[k] = swap(answers[k], "adapter", k)
    mixed = combine(placing, returned, [own] + [partials[k] for k in far_first])
    return mixed.reshape(requests, steps, columns)


def solution(mesh):
    rows = P(("group", "adapter"), None, "tensor")
    return jax.shard_map(
        body,
        mesh=mesh,
        in_specs=(
            rows,
            rows,
            rows,
            rows,
            rows,
            P(("group", "adapter")),
            P(("group", "adapter")),
            P("tensor", None),
            rows,
            rows,
        ),
        out_specs=rows,
        check_vma=False,
    )
```

time: 137 us -> 67.4 us (0.49)
  waiting for transfers between devices: 63 us -> 8.74 us
  Pallas kernels: 0 us -> 34.6 us
  matrix products: 23.2 us -> 0 us
  local copies, waits for them, and re-layouts: 21.4 us -> 3.82 us
  between operations: 13.6 us -> 0.08 us
  starting transfers between devices: 11.3 us -> 19.7 us
  other arithmetic: 3.92 us -> 0 us
    pallas_call x0 -> x8, Pallas kernels: none -> 34.6 us  [the longest x4 14.1 us: project(): pl.pallas_call(project_kernel, grid_spec=pltpu.PrefetchScalarGridSpec(num...]
    psum x1 -> x0, waiting for transfers between devices: 27 us -> none  [adapter_contributions(): low_rank = lax.psum(masked.astype(jnp.bfloat16), 'tensor')]
    dot_general x8 -> x0, matrix products: 23.2 us -> none  [the longest x1 9.15 us: body(): jnp.dot(attended.reshape(row_count * step_count, feature_count), output_w...]
    all_to_all x3 -> x0, waiting for transfers between devices: 23.1 us -> none  [the longest x1 14.3 us: body(): lax.all_to_all(send_rows, 'adapter', split_axis=0, concat_axis=0, tiled=T...]
    ppermute x0 -> x12, starting transfers between devices: none -> 19.7 us  [swap(): return lax.ppermute(value, axis, [(i, i ^ k) for i in range(count)])]
    reshape x6 -> x1, local copies, waits for them, and re-layouts: 17.2 us -> 1.75 us  [body(): return mixed.reshape(requests, steps, columns)]
    reduce_scatter x1 -> x0, waiting for transfers between devices: 12.9 us -> none  [body(): lax.psum_scatter(partial_out.astype(jnp.bfloat16), 'tensor', scatter_dime...]
    all_to_all x3 -> x0, starting transfers between devices: 11.2 us -> none  [the longest x1 4.21 us: body(): lax.all_to_all(send_ids, 'adapter', split_axis=0, concat_axis=0, tiled=True)]
  transfers between devices with their start and end apart: 5 -> 12, of which waited for: 4 -> 4; matrix products, arithmetic and copies ran while one was open for 32% -> 0% of each run, Pallas kernels for 0% -> 30%
where the time goes in v1:
time: 67.4 us; the launch traced here: 67 us
  Pallas kernels  34.6 us (51%)
  starting transfers between devices  19.7 us (29%)
  waiting for transfers between devices  8.74 us (13%)
  local copies, waits for them, and re-layouts  3.82 us (6%)
    ppermute x12, starting transfers between devices, swap(): return lax.ppermute(value, axis, [(i, i ^ k) for i in range(count)])  19.7 us
    pallas_call x4, Pallas kernels, project(): pl.pallas_call(project_kernel, grid_spec=pltpu.PrefetchScalarGridSpec(num...  14.1 us
    pallas_call x1, Pallas kernels, attend(): pl.pallas_call(functools.partial(attend_kernel, owners, resident, capacit...  12.2 us
    ppermute x12, waiting for transfers between devices, swap(): return lax.ppermute(value, axis, [(i, i ^ k) for i in range(count)])  8.74 us
    pallas_call x1, Pallas kernels, low_partial(): pl.pallas_call(functools.partial(low_kernel, owners, resident), out_shape...  3.68 us
    pallas_call x1, Pallas kernels, combine(): pl.pallas_call(functools.partial(combine_kernel, len(answers)), out_shape...  2.4 us
    pallas_call x1, Pallas kernels, delta(): pl.pallas_call(functools.partial(delta_kernel, owners, resident), out_sha...  2.29 us
    unnamed x24, local copies, waits for them, and re-layouts  2.07 us
  transfers between devices with their start and end apart: 12, of which 4 were waited for; matrix products, arithmetic and copies ran while one was open for 0% of the time, Pallas kernels for 30%

profile of v1, /device:TPU:0, one launch (start us, length us, event | category | flops | bytes accessed | tf_op | source)
XLA Modules:
  0.0 67.0 jit_solution(1253360738941507598)
XLA Ops:
  0.0 12.2 %attend.1 = (bf16[128,2048]{1,0:T(8,128)(2,1)}, bf16[256,128]{1,0:T(8,128)(2,1)}, bf16[64,2176]{1,0:T(8,128)(2,1)}, bf16[64,2176]{1,0:T(8,128)(2,1)}, bf16[64,21...) custom-call(s32[64]{0:T(128)} %lengths.1, s32[1]{0:T(128)} %bitcast.place, s32[1,64]{1,0:T(1,128)} %bitcast.10, ...), custom_call_target="tpu_custom_call" | custom-call | flops 268435456 | bytes 8388608 | tf_op jit(solution)/shard_map/attend/pallas_call | solution.py:157
  12.2 0.5 collective-permute-start
  12.6 2.6 %collective-permute-start.1 = (bf16[64,2176]{1,0:T(8,128)(2,1)}, bf16[64,2176]{1,0:T(8,128)(2,1)S(1)}, u32[]{:S(2)}, u32[]{:S(2)}) collective-permute-start(bf16[64,2176]{1,0:T(8,128)(2,1)} %get-tuple-element.20), channel_id=1, source_target_pairs={{0,8},{4,12},{8,0},{12,4},{1,9},{5,13},{9,1},{13,5},{2,10},{6,14},... | collective-permute-start | bytes 835592 | tf_op jit(solution)/shard_map/ppermute | solution.py:324
  15.2 3.5 %project.5 = bf16[128,1024]{1,0:T(8,128)(2,1)} custom-call(s32[1]{0:T(128)} %bitcast.5.column, bf16[128,2048]{1,0:T(8,128)(2,1)} %get-tuple-element.28.attended, bf16[2048,4096]{1,0:T(8,128)(2,1)} %weight.7), custom_call_target="tpu_custom_call" | custom-call | flops 536870912 | bytes 4194304 | tf_op jit(solution)/shard_map/project/pallas_call | solution.py:200
  18.8 3.8 %collective-permute-start.9 = (bf16[128,1024]{1,0:T(8,128)(2,1)}, bf16[128,1024]{1,0:T(8,128)(2,1)S(1)}, u32[]{:S(2)}, u32[]{:S(2)}) collective-permute-start(bf16[128,1024]{1,0:T(8,128)(2,1)} %project.5), channel_id=1, source_target_pairs={{0,3},{1,2},{2,1},{3,0},{4,7},{5,6},{6,5},{7,4},{8,11},{9,10},{10,... | collective-permute-start | bytes 786440 | tf_op jit(solution)/shard_map/ppermute | solution.py:324
  22.6 3.5 %project.6 = bf16[128,1024]{1,0:T(8,128)(2,1)} custom-call(s32[1]{0:T(128)} %bitcast.6.column, bf16[128,2048]{1,0:T(8,128)(2,1)} %get-tuple-element.28.attended, bf16[2048,4096]{1,0:T(8,128)(2,1)} %weight.7), custom_call_target="tpu_custom_call" | custom-call | flops 536870912 | bytes 4194304 | tf_op jit(solution)/shard_map/project/pallas_call | solution.py:200
  26.1 3.5 %project.7 = bf16[128,1024]{1,0:T(8,128)(2,1)} custom-call(s32[1]{0:T(128)} %bitcast.7.column, bf16[128,2048]{1,0:T(8,128)(2,1)} %get-tuple-element.28.attended, bf16[2048,4096]{1,0:T(8,128)(2,1)} %weight.7), custom_call_target="tpu_custom_call" | custom-call | flops 536870912 | bytes 4194304 | tf_op jit(solution)/shard_map/project/pallas_call | solution.py:200
  29.6 0.6 collective-permute-start.11
  30.4 0.6 copy-done.1
  31.0 3.7 %low.1 = (bf16[128,128]{1,0:T(8,128)(2,1)}, bf16[256,128]{1,0:T(8,128)(2,1)}) custom-call(bf16[256,2048]{1,0:T(8,128)(2,1)} %bitcast.8, bf16[64,2176]{1,0:T(8,128)(2,1)} %get-tuple-element.18.refs_0_, bf16[64,2176]{1,0:T(8,128)(2,1)} %copy-done, bf16[64,2176]{1,0:T(8,128)(2,1)} %copy-done.1, bf16[64,2176]{1,0:T(8,128)(2,1)} %copy-done.2), custom_call_target="tpu_custom_call" | custom-call | flops 268435456 | bytes 1048576 | tf_op jit(solution)/shard_map/low/pallas_call | solution.py:249
  34.7 3.8 %collective-permute-start.3 = (bf16[128,128]{1,0:T(8,128)(2,1)}, bf16[128,128]{1,0:T(8,128)(2,1)S(1)}, u32[]{:S(2)}, u32[]{:S(2)}) collective-permute-start(bf16[128,128]{1,0:T(8,128)(2,1)} %get-tuple-element.23.refs_0_), channel_id=1, source_target_pairs={{0,3},{1,2},{2,1},{3,0},{4,7},{5,6},{6,5},{7,4},{8,11},{9,10},{10,... | collective-permute-start | bytes 98312 | tf_op jit(solution)/shard_map/ppermute | solution.py:324
  38.5 3.5 %collective-permute-done.3.refs_1_ = bf16[128,128]{1,0:T(8,128)(2,1)S(1)} collective-permute-done((bf16[128,128]{1,0:T(8,128)(2,1)}, bf16[128,128]{1,0:T(8,128)(2,1)S(1)}, u32[]{:S(2)}, u32[]{:S(2)}) %collective-permute-start.3) | collective-permute-done | bytes 32800 | tf_op jit(solution)/shard_map/ppermute | solution.py:324
  42.0 6.6 %collective-permute-start.5 = (bf16[128,128]{1,0:T(8,128)(2,1)}, bf16[128,128]{1,0:T(8,128)(2,1)S(1)}, u32[]{:S(2)}, u32[]{:S(2)}) collective-permute-start(bf16[128,128]{1,0:T(8,128)(2,1)} %get-tuple-element.23.refs_0_), channel_id=1, source_target_pairs={{0,1},{1,0},{2,3},{3,2},{4,5},{5,4},{6,7},{7,6},{8,9},{9,8},{10,11... | collective-permute-start | bytes 98312 | tf_op jit(solution)/shard_map/ppermute | solution.py:324
  48.6 2.1 %collective-permute-done.5.refs_3_ = bf16[128,128]{1,0:T(8,128)(2,1)S(1)} collective-permute-done((bf16[128,128]{1,0:T(8,128)(2,1)}, bf16[128,128]{1,0:T(8,128)(2,1)S(1)}, u32[]{:S(2)}, u32[]{:S(2)}) %collective-permute-start.5) | collective-permute-done | bytes 32800 | tf_op jit(solution)/shard_map/ppermute | solution.py:324
  50.7 0.6 copy-done.11
  51.3 2.3 %delta.1 = (bf16[64,1024]{1,0:T(8,128)(2,1)}, bf16[64,1024]{1,0:T(8,128)(2,1)}, bf16[64,1024]{1,0:T(8,128)(2,1)}, bf16[64,1024]{1,0:T(8,128)(2,1)}) custom-call(bf16[256,128]{1,0:T(8,128)(2,1)} %get-tuple-element.22.marks, bf16[256,1024]{1,0:T(8,128)(2,1)} %bitcast.9, bf16[128,128]{1,0:T(8,128)(2,1)} %get-tuple-element.23.refs_0_, ...), custom_call_target="tpu_custom_call" | custom-call | flops 134217728 | bytes 524288 | tf_op jit(solution)/shard_map/delta/pallas_call | solution.py:287
  53.6 1.5 %collective-permute-start.7 = (bf16[64,1024]{1,0:T(8,128)(2,1)}, bf16[64,1024]{1,0:T(8,128)(2,1)S(1)}, u32[]{:S(2)}, u32[]{:S(2)}) collective-permute-start(bf16[64,1024]{1,0:T(8,128)(2,1)} %get-tuple-element.26), channel_id=1, source_target_pairs={{0,8},{4,12},{8,0},{12,4},{1,9},{5,13},{9,1},{13,5},{2,10},{6,14},... | collective-permute-start | bytes 393224 | tf_op jit(solution)/shard_map/ppermute | solution.py:324
  55.1 0.4 collective-permute-start.8
  55.5 3.5 %project.4.refs_4_ = bf16[128,1024]{1,0:T(8,128)(2,1)} custom-call(s32[1]{0:T(128)} %bitcast.4.column, bf16[128,2048]{1,0:T(8,128)(2,1)} %get-tuple-element.28.attended, bf16[2048,4096]{1,0:T(8,128)(2,1)} %weight.7), custom_call_target="tpu_custom_call" | custom-call | flops 536870912 | bytes 4194304 | tf_op jit(solution)/shard_map/project/pallas_call | solution.py:200
  59.1 1.1 %collective-permute-done.7.refs_2_ = bf16[64,1024]{1,0:T(8,128)(2,1)S(1)} collective-permute-done((bf16[64,1024]{1,0:T(8,128)(2,1)}, bf16[64,1024]{1,0:T(8,128)(2,1)S(1)}, u32[]{:S(2)}, u32[]{:S(2)}) %collective-permute-start.7) | collective-permute-done | bytes 131104 | tf_op jit(solution)/shard_map/ppermute | solution.py:324
  60.1 2.0 %collective-permute-done.8.refs_3_ = bf16[64,1024]{1,0:T(8,128)(2,1)S(1)} collective-permute-done((bf16[64,1024]{1,0:T(8,128)(2,1)}, bf16[64,1024]{1,0:T(8,128)(2,1)S(1)}, u32[]{:S(2)}, u32[]{:S(2)}) %collective-permute-start.8) | collective-permute-done | bytes 131104 | tf_op jit(solution)/shard_map/ppermute | solution.py:324
  62.2 0.6 copy-done.8
  62.8 2.4 %combine.1 = bf16[128,1024]{1,0:T(8,128)(2,1)} custom-call(bf16[256,128]{1,0:T(8,128)(2,1)} %get-tuple-element.17.placing, bf16[64,1024]{1,0:T(8,128)(2,1)} %get-tuple-element.24.refs_0_, bf16[64,1024]{1,0:T(8,128)(2,1)} %copy-done.6, bf16[64,1024]{1,0:T(8,128)(2,1)} %copy-done.7, bf16[64,1024]{1,0:T(8,128)(2,1)} %copy-done.8, ...), custom_call_target="tpu_custom_call" | custom-call | tf_op jit(solution)/shard_map/combine/pallas_call | solution.py:314
  65.2 1.7 %reshape.35 = bf16[64,2,1024]{2,1,0:T(2,128)(2,1)} reshape(bf16[128,1024]{1,0:T(8,128)(2,1)} %combine.1) | data formatting | bytes 524288 | tf_op jit(solution)/shard_map/reshape | solution.py:378
  (33 shorter events, 0.4 us)
Async XLA Ops:
  12.2 17.5 %collective-permute-start = (bf16[64,2176]{1,0:T(8,128)(2,1)}, bf16[64,2176]{1,0:T(8,128)(2,1)S(1)}, u32[]{:S(2)}, u32[]{:S(2)}) collective-permute-start(bf16[64,2176]{1,0:T(8,128)(2,1)} %get-tuple-element.19), channel_id=1, source_target_pairs={{0,4},{4,0},{8,12},{12,8},{1,5},{5,1},{9,13},{13,9},{2,6},{6,2},{1... | collective-permute-start | bytes 835592 | tf_op jit(solution)/shard_map/ppermute | solution.py:324
  12.6 17.6 %collective-permute-start.1 = (bf16[64,2176]{1,0:T(8,128)(2,1)}, bf16[64,2176]{1,0:T(8,128)(2,1)S(1)}, u32[]{:S(2)}, u32[]{:S(2)}) collective-permute-start(bf16[64,2176]{1,0:T(8,128)(2,1)} %get-tuple-element.20), channel_id=1, source_target_pairs={{0,8},{4,12},{8,0},{12,4},{1,9},{5,13},{9,1},{13,5},{2,10},{6,14},... | collective-permute-start | bytes 835592 | tf_op jit(solution)/shard_map/ppermute | solution.py:324
  15.2 15.1 %collective-permute-start.2 = (bf16[64,2176]{1,0:T(8,128)(2,1)}, bf16[64,2176]{1,0:T(8,128)(2,1)S(1)}, u32[]{:S(2)}, u32[]{:S(2)}) collective-permute-start(bf16[64,2176]{1,0:T(8,128)(2,1)} %get-tuple-element.21), channel_id=1, source_target_pairs={{0,12},{4,8},{8,4},{12,0},{1,13},{5,9},{9,5},{13,1},{2,14},{6,10},... | collective-permute-start | bytes 835592 | tf_op jit(solution)/shard_map/ppermute | solution.py:324
  18.8 36.4 %collective-permute-start.9 = (bf16[128,1024]{1,0:T(8,128)(2,1)}, bf16[128,1024]{1,0:T(8,128)(2,1)S(1)}, u32[]{:S(2)}, u32[]{:S(2)}) collective-permute-start(bf16[128,1024]{1,0:T(8,128)(2,1)} %project.5), channel_id=1, source_target_pairs={{0,3},{1,2},{2,1},{3,0},{4,7},{5,6},{6,5},{7,4},{8,11},{9,10},{10,... | collective-permute-start | bytes 786440 | tf_op jit(solution)/shard_map/ppermute | solution.py:324
  26.1 32.9 %collective-permute-start.10 = (bf16[128,1024]{1,0:T(8,128)(2,1)}, bf16[128,1024]{1,0:T(8,128)(2,1)S(1)}, u32[]{:S(2)}, u32[]{:S(2)}) collective-permute-start(bf16[128,1024]{1,0:T(8,128)(2,1)} %project.6), channel_id=1, source_target_pairs={{0,2},{1,3},{2,0},{3,1},{4,6},{5,7},{6,4},{7,5},{8,10},{9,11},{10,... | collective-permute-start | bytes 786440 | tf_op jit(solution)/shard_map/ppermute | solution.py:324
  29.6 0.7 %copy-start = (bf16[64,2176]{1,0:T(8,128)(2,1)}, bf16[64,2176]{1,0:T(8,128)(2,1)S(1)}, u32[]{:S(2)}) copy-start(bf16[64,2176]{1,0:T(8,128)(2,1)S(1)} %collective-permute-done.refs_1_) | copy-start | bytes 835588
  29.6 29.4 %collective-permute-start.11 = (bf16[128,1024]{1,0:T(8,128)(2,1)}, bf16[128,1024]{1,0:T(8,128)(2,1)S(1)}, u32[]{:S(2)}, u32[]{:S(2)}) collective-permute-start(bf16[128,1024]{1,0:T(8,128)(2,1)} %project.7), channel_id=1, source_target_pairs={{0,1},{1,0},{2,3},{3,2},{4,5},{5,4},{6,7},{7,6},{8,9},{9,8},{10,11... | collective-permute-start | bytes 786440 | tf_op jit(solution)/shard_map/ppermute | solution.py:324
  30.2 0.7 %copy-start.1 = (bf16[64,2176]{1,0:T(8,128)(2,1)}, bf16[64,2176]{1,0:T(8,128)(2,1)S(1)}, u32[]{:S(2)}) copy-start(bf16[64,2176]{1,0:T(8,128)(2,1)S(1)} %collective-permute-done.1.refs_2_) | copy-start | bytes 835588
  30.2 0.8 %copy-start.2 = (bf16[64,2176]{1,0:T(8,128)(2,1)}, bf16[64,2176]{1,0:T(8,128)(2,1)S(1)}, u32[]{:S(2)}) copy-start(bf16[64,2176]{1,0:T(8,128)(2,1)S(1)} %collective-permute-done.2.refs_3_) | copy-start | bytes 835588
  34.7 7.3 %collective-permute-start.3 = (bf16[128,128]{1,0:T(8,128)(2,1)}, bf16[128,128]{1,0:T(8,128)(2,1)S(1)}, u32[]{:S(2)}, u32[]{:S(2)}) collective-permute-start(bf16[128,128]{1,0:T(8,128)(2,1)} %get-tuple-element.23.refs_0_), channel_id=1, source_target_pairs={{0,3},{1,2},{2,1},{3,0},{4,7},{5,6},{6,5},{7,4},{8,11},{9,10},{10,... | collective-permute-start | bytes 98312 | tf_op jit(solution)/shard_map/ppermute | solution.py:324
  38.5 10.1 %collective-permute-start.4 = (bf16[128,128]{1,0:T(8,128)(2,1)}, bf16[128,128]{1,0:T(8,128)(2,1)S(1)}, u32[]{:S(2)}, u32[]{:S(2)}) collective-permute-start(bf16[128,128]{1,0:T(8,128)(2,1)} %get-tuple-element.23.refs_0_), channel_id=1, source_target_pairs={{0,2},{1,3},{2,0},{3,1},{4,6},{5,7},{6,4},{7,5},{8,10},{9,11},{10,... | collective-permute-start | bytes 98312 | tf_op jit(solution)/shard_map/ppermute | solution.py:324
  42.0 8.7 %copy-start.9 = (bf16[128,128]{1,0:T(8,128)(2,1)}, bf16[128,128]{1,0:T(8,128)(2,1)S(1)}, u32[]{:S(2)}) copy-start(bf16[128,128]{1,0:T(8,128)(2,1)S(1)} %collective-permute-done.3.refs_1_) | copy-start | bytes 98308
  42.0 8.7 %collective-permute-start.5 = (bf16[128,128]{1,0:T(8,128)(2,1)}, bf16[128,128]{1,0:T(8,128)(2,1)S(1)}, u32[]{:S(2)}, u32[]{:S(2)}) collective-permute-start(bf16[128,128]{1,0:T(8,128)(2,1)} %get-tuple-element.23.refs_0_), channel_id=1, source_target_pairs={{0,1},{1,0},{2,3},{3,2},{4,5},{5,4},{6,7},{7,6},{8,9},{9,8},{10,11... | collective-permute-start | bytes 98312 | tf_op jit(solution)/shard_map/ppermute | solution.py:324
  48.6 2.1 %copy-start.10 = (bf16[128,128]{1,0:T(8,128)(2,1)}, bf16[128,128]{1,0:T(8,128)(2,1)S(1)}, u32[]{:S(2)}) copy-start(bf16[128,128]{1,0:T(8,128)(2,1)S(1)} %collective-permute-done.4.refs_2_) | copy-start | bytes 98308
  50.7 0.6 copy-start.11
  53.6 5.4 %collective-permute-start.6 = (bf16[64,1024]{1,0:T(8,128)(2,1)}, bf16[64,1024]{1,0:T(8,128)(2,1)S(1)}, u32[]{:S(2)}, u32[]{:S(2)}) collective-permute-start(bf16[64,1024]{1,0:T(8,128)(2,1)} %get-tuple-element.25), channel_id=1, source_target_pairs={{0,4},{4,0},{8,12},{12,8},{1,5},{5,1},{9,13},{13,9},{2,6},{6,2},{1... | collective-permute-start | bytes 393224 | tf_op jit(solution)/shard_map/ppermute | solution.py:324
  53.6 6.5 %collective-permute-start.7 = (bf16[64,1024]{1,0:T(8,128)(2,1)}, bf16[64,1024]{1,0:T(8,128)(2,1)S(1)}, u32[]{:S(2)}, u32[]{:S(2)}) collective-permute-start(bf16[64,1024]{1,0:T(8,128)(2,1)} %get-tuple-element.26), channel_id=1, source_target_pairs={{0,8},{4,12},{8,0},{12,4},{1,9},{5,13},{9,1},{13,5},{2,10},{6,14},... | collective-permute-start | bytes 393224 | tf_op jit(solution)/shard_map/ppermute | solution.py:324
  55.1 3.9 %copy-start.3 = (bf16[128,1024]{1,0:T(8,128)(2,1)}, bf16[128,1024]{1,0:T(8,128)(2,1)S(1)}, u32[]{:S(2)}) copy-start(bf16[128,1024]{1,0:T(8,128)(2,1)S(1)} %collective-permute-done.9.refs_5_) | copy-start | bytes 786436
  55.1 7.0 %collective-permute-start.8 = (bf16[64,1024]{1,0:T(8,128)(2,1)}, bf16[64,1024]{1,0:T(8,128)(2,1)S(1)}, u32[]{:S(2)}, u32[]{:S(2)}) collective-permute-start(bf16[64,1024]{1,0:T(8,128)(2,1)} %get-tuple-element.27), channel_id=1, source_target_pairs={{0,12},{4,8},{8,4},{12,0},{1,13},{5,9},{9,5},{13,1},{2,14},{6,10},... | collective-permute-start | bytes 393224 | tf_op jit(solution)/shard_map/ppermute | solution.py:324
  59.0 3.2 %copy-start.4 = (bf16[128,1024]{1,0:T(8,128)(2,1)}, bf16[128,1024]{1,0:T(8,128)(2,1)S(1)}, u32[]{:S(2)}) copy-start(bf16[128,1024]{1,0:T(8,128)(2,1)S(1)} %collective-permute-done.10.refs_6_) | copy-start | bytes 786436
  59.0 3.2 %copy-start.5 = (bf16[128,1024]{1,0:T(8,128)(2,1)}, bf16[128,1024]{1,0:T(8,128)(2,1)S(1)}, u32[]{:S(2)}) copy-start(bf16[128,1024]{1,0:T(8,128)(2,1)S(1)} %collective-permute-done.11.refs_7_) | copy-start | bytes 786436
  59.0 3.1 %copy-start.6 = (bf16[64,1024]{1,0:T(8,128)(2,1)}, bf16[64,1024]{1,0:T(8,128)(2,1)S(1)}, u32[]{:S(2)}) copy-start(bf16[64,1024]{1,0:T(8,128)(2,1)S(1)} %collective-permute-done.6.refs_1_) | copy-start | bytes 393220
  60.1 2.1 %copy-start.7 = (bf16[64,1024]{1,0:T(8,128)(2,1)}, bf16[64,1024]{1,0:T(8,128)(2,1)S(1)}, u32[]{:S(2)}) copy-start(bf16[64,1024]{1,0:T(8,128)(2,1)S(1)} %collective-permute-done.7.refs_2_) | copy-start | bytes 393220
  62.2 0.7 copy-start.8

commit v2 on v1

v2 whole, which is shorter than its diff:
```python
import functools
import math

import jax
import jax.numpy as jnp
from jax import lax
from jax.experimental import pallas as pl
from jax.experimental.pallas import tpu as pltpu
from jax.sharding import PartitionSpec as P

HEAD_DIM = 128
NEGATIVE = -1e30
LANES = 128
KERNEL_VMEM = 32 * 1024 * 1024
SMALL_VMEM = 12 * 1024 * 1024

F32 = jnp.float32
BF16 = jnp.bfloat16


def contract(a, b, a_dim, b_dim):
    return lax.dot_general(
        a, b, (((a_dim,), (b_dim,)), ((), ())), preferred_element_type=F32
    )


def attend_kernel(
    owners,
    resident,
    capacity,
    block,
    lengths,
    place,
    column,
    adapters,
    queries_hbm,
    fresh_k_hbm,
    fresh_v_hbm,
    cache_k_hbm,
    cache_v_hbm,
    weight_hbm,
    *rest,
):
    attended_hbm, placing_hbm, marks_hbm, partial_hbm = rest[:4]
    packed_hbm = rest[4 : 4 + owners]
    (
        queries,
        fresh_k,
        fresh_v,
        cache_k,
        cache_v,
        weight,
        new_k,
        new_v,
        query_scratch,
        result_scratch,
        attended,
        placing_out,
        marks_out,
        partial,
        packed,
        small_sem,
        cache_sem,
        weight_sem,
        out_sem,
    ) = rest[4 + owners :]
    requests, steps, width = queries.shape
    heads = width // HEAD_DIM
    groups = cache_k.shape[2] // HEAD_DIM
    sharing = heads // groups
    cache_size = cache_k.shape[1]
    rows = block * steps
    total_rows = requests * steps
    span = steps * sharing
    chunks = requests // block
    columns = partial.shape[1]

    def cache_copies(i):
        part = pl.ds(i * block, block)
        return (
            pltpu.make_async_copy(cache_k_hbm.at[part], cache_k.at[part], cache_sem.at[0, i]),
            pltpu.make_async_copy(cache_v_hbm.at[part], cache_v.at[part], cache_sem.at[1, i]),
        )

    small = [
        pltpu.make_async_copy(queries_hbm, queries, small_sem.at[0]),
        pltpu.make_async_copy(fresh_k_hbm, fresh_k, small_sem.at[1]),
        pltpu.make_async_copy(fresh_v_hbm, fresh_v, small_sem.at[2]),
    ]
    for copy in small:
        copy.start()
    for i in range(chunks):
        for copy in cache_copies(i):
            copy.start()
    weight_copy = pltpu.make_async_copy(
        weight_hbm.at[:, pl.ds(pl.multiple_of(column[0] * columns, LANES), columns)],
        weight,
        weight_sem.at[0],
    )
    weight_copy.start()

    named = adapters[...]
    owner = lax.div(named, resident)
    local = named - owner * resident
    relative = jnp.bitwise_xor(owner, place[0])
    owner_id = lax.broadcasted_iota(jnp.int32, (owners, requests), 0)
    member = (owner_id == relative).astype(F32)
    before = lax.broadcasted_iota(jnp.int32, (requests, requests), 0) < (
        lax.broadcasted_iota(jnp.int32, (requests, requests), 1)
    )
    earlier = contract(member.astype(BF16), before.astype(BF16), 1, 0)
    slot = jnp.sum(earlier * member, axis=0, keepdims=True)
    facts = jnp.concatenate(
        [relative.astype(F32), slot, local.astype(F32), jnp.zeros((5, requests), F32)], axis=0
    )
    spread = lax.broadcasted_iota(jnp.int32, (requests, total_rows), 0) == lax.div(
        lax.broadcasted_iota(jnp.int32, (requests, total_rows), 1), steps
    )
    facts = contract(facts.astype(BF16), spread.astype(BF16), 1, 0).astype(jnp.int32)
    token = lax.rem(lax.broadcasted_iota(jnp.int32, (1, total_rows), 1), steps)
    target = (facts[0:1] * capacity + facts[1:2]) * steps + token
    slots = owners * capacity * steps
    placing = (
        lax.broadcasted_iota(jnp.int32, (slots, total_rows), 0) == target
    ).astype(BF16)
    placing_out[...] = placing
    chosen = (
        lax.broadcasted_iota(jnp.int32, (LANES, total_rows), 0) == facts[2:3]
    ).astype(BF16)
    packed[:, width:] = contract(placing, chosen, 1, 1).astype(BF16)
    adapter_id = lax.broadcasted_iota(jnp.int32, (LANES, total_rows), 0)
    named_here = (adapter_id == facts[0:1] * resident + facts[2:3]).astype(BF16)
    identity = lax.broadcasted_iota(jnp.int32, (total_rows, total_rows), 0) == (
        lax.broadcasted_iota(jnp.int32, (total_rows, total_rows), 1)
    )
    marks_out[...] = contract(identity.astype(BF16), named_here, 1, 1).astype(BF16)

    positions = lax.broadcasted_iota(jnp.int32, (groups * span, cache_size), 1)
    row_id = lax.broadcasted_iota(jnp.int32, (block * groups * span, total_rows), 0)
    col_id = lax.broadcasted_iota(jnp.int32, (block * groups * span, total_rows), 1)
    distance = lax.div(row_id, groups * span) - lax.div(col_id, steps)
    causal = lax.rem(col_id, steps) <= lax.div(lax.rem(row_id, span), sharing)
    distance = jnp.where(causal, distance, requests)
    scaling = math.log2(math.e) / math.sqrt(HEAD_DIM)
    for copy in small:
        copy.wait()
    new_k[...] = fresh_k[...].reshape(total_rows, groups * HEAD_DIM)
    new_v[...] = fresh_v[...].reshape(total_rows, groups * HEAD_DIM)

    @pl.loop(0, chunks)
    def _(i):
        base = i * block
        flat = queries[pl.ds(base, block)].astype(F32).reshape(rows, width)
        for h in range(heads):
            query_scratch[h * rows : (h + 1) * rows, :] = flat[
                :, h * HEAD_DIM : (h + 1) * HEAD_DIM
            ]
        for copy in cache_copies(i):
            copy.wait()
        live_fresh = distance == -base
        empty = jnp.zeros((span, HEAD_DIM), BF16)
        wide = []
        for r in range(block):
            for g in range(groups):
                parts = []
                for s in range(steps):
                    start = g * sharing * rows + r * steps + s
                    parts.append(query_scratch[pl.ds(start, sharing, stride=rows), :])
                q = jnp.concatenate(parts, axis=0).astype(BF16)
                wide.append(
                    jnp.concatenate([q if o == g else empty for o in range(groups)], axis=1)
                )
        q = jnp.concatenate(wide, axis=0)
        fresh = jnp.where(live_fresh, contract(q, new_k[...], 1, 1), NEGATIVE)
        band = groups * span
        cached = []
        for r in range(block):
            score = contract(q[r * band : (r + 1) * band], cache_k[base + r], 1, 1)
            cached.append(jnp.where(positions < lengths[base + r], score, NEGATIVE))
        cached = jnp.concatenate(cached, axis=0)
        top = jnp.max(jnp.maximum(cached, fresh), axis=1, keepdims=True)
        cached = jnp.exp2((cached - top) * scaling)
        fresh = jnp.exp2((fresh - top) * scaling)
        scale = 1.0 / jnp.sum(cached + fresh, axis=1, keepdims=True)
        cached = cached.astype(BF16)
        out = contract(fresh.astype(BF16), new_v[...], 1, 0)
        for r in range(block):
            rows_r = slice(r * band, (r + 1) * band)
            both = (
                contract(cached[rows_r], cache_v[base + r], 1, 0) + out[rows_r]
            )
            for g in range(groups):
                for s in range(steps):
                    first = g * span + s * sharing
                    piece = both[
                        first : first + sharing, g * HEAD_DIM : (g + 1) * HEAD_DIM
                    ] * scale[r * band + first : r * band + first + sharing]
                    start = g * sharing * total_rows + (base + r) * steps + s
                    result_scratch[pl.ds(start, sharing, stride=total_rows), :] = piece

    for h in range(heads):
        attended[:, h * HEAD_DIM : (h + 1) * HEAD_DIM] = result_scratch[
            h * total_rows : (h + 1) * total_rows, :
        ].astype(BF16)
    attended_copy = pltpu.make_async_copy(attended, attended_hbm, out_sem.at[0])
    attended_copy.start()
    placing_copy = pltpu.make_async_copy(placing_out, placing_hbm, out_sem.at[1])
    placing_copy.start()
    marks_copy = pltpu.make_async_copy(marks_out, marks_hbm, out_sem.at[2])
    marks_copy.start()
    per = capacity * steps
    tile = min(512, width)
    for c in range(0, width, tile):
        packed[:, c : c + tile] = contract(
            placing_out[...], attended[:, c : c + tile], 1, 0
        ).astype(BF16)
    packed_copies = [
        pltpu.make_async_copy(
            packed.at[pl.ds(k * per, per)], packed_hbm[k], out_sem.at[4 + k]
        )
        for k in range(owners)
    ]
    for copy in packed_copies:
        copy.start()
    weight_copy.wait()
    tile = min(256, columns)
    for c in range(0, columns, tile):
        partial[:, c : c + tile] = contract(
            attended[...], weight[:, c : c + tile], 1, 0
        ).astype(BF16)
    partial_copy = pltpu.make_async_copy(partial, partial_hbm, out_sem.at[3])
    partial_copy.start()
    attended_copy.wait()
    placing_copy.wait()
    marks_copy.wait()
    for copy in packed_copies:
        copy.wait()
    partial_copy.wait()


def attend(
    queries,
    fresh_k,
    fresh_v,
    cache_k,
    cache_v,
    weight,
    lengths,
    place,
    column,
    adapters,
    owners,
    resident,
    columns,
):
    requests, steps, width = queries.shape
    cache_size, kv_width = cache_k.shape[1:]
    capacity = max(2, 2 * requests // owners)
    block = min(32, requests)
    heads = width // HEAD_DIM
    total_rows = requests * steps
    per = capacity * steps
    anywhere = pl.BlockSpec(memory_space=pl.ANY)
    return pl.pallas_call(
        functools.partial(attend_kernel, owners, resident, capacity, block),
        grid_spec=pltpu.PrefetchScalarGridSpec(
            num_scalar_prefetch=3,
            grid=(1,),
            in_specs=[pl.BlockSpec((1, requests), lambda i, *_: (0, 0))] + [anywhere] * 6,
            out_specs=[anywhere] * (4 + owners),
            scratch_shapes=[
                pltpu.VMEM((requests, steps, width), BF16),
                pltpu.VMEM((requests, steps, kv_width), BF16),
                pltpu.VMEM((requests, steps, kv_width), BF16),
                pltpu.VMEM((requests, cache_size, kv_width), BF16),
                pltpu.VMEM((requests, cache_size, kv_width), BF16),
                pltpu.VMEM((width, columns), BF16),
                pltpu.VMEM((total_rows, kv_width), BF16),
                pltpu.VMEM((total_rows, kv_width), BF16),
                pltpu.VMEM((heads * block * steps, HEAD_DIM), F32),
                pltpu.VMEM((heads * total_rows, HEAD_DIM), F32),
                pltpu.VMEM((total_rows, width), BF16),
                pltpu.VMEM((owners * per, total_rows), BF16),
                pltpu.VMEM((total_rows, LANES), BF16),
                pltpu.VMEM((total_rows, columns), BF16),
                pltpu.VMEM((owners * per, width + LANES), BF16),
                pltpu.SemaphoreType.DMA((3,)),
                pltpu.SemaphoreType.DMA((2, requests // block)),
                pltpu.SemaphoreType.DMA((1,)),
                pltpu.SemaphoreType.DMA((4 + owners,)),
            ],
        ),
        out_shape=[
            jax.ShapeDtypeStruct((total_rows, width), BF16),
            jax.ShapeDtypeStruct((owners * per, total_rows), BF16),
            jax.ShapeDtypeStruct((total_rows, LANES), BF16),
            jax.ShapeDtypeStruct((total_rows, columns), BF16),
        ]
        + [jax.ShapeDtypeStruct((per, width + LANES), BF16)] * owners,
        compiler_params=pltpu.CompilerParams(vmem_limit_bytes=KERNEL_VMEM),
        cost_estimate=pl.CostEstimate(
            flops=8 * total_rows * width * cache_size,
            bytes_accessed=4 * requests * cache_size * kv_width,
            transcendentals=0,
        ),
        name="attend",
    )(
        lengths,
        place,
        column,
        adapters.reshape(1, requests),
        queries,
        fresh_k,
        fresh_v,
        cache_k,
        cache_v,
        weight,
    )


def project_kernel(count, *refs):
    places = refs[:count]
    attended_hbm, weight_hbm = refs[count : count + 2]
    outs = refs[count + 2 : 2 * count + 2]
    attended, weight, results, in_sem, weight_sem, out_sem = refs[2 * count + 2 :]
    columns = results.shape[2]
    attended_copy = pltpu.make_async_copy(attended_hbm, attended, in_sem.at[0])
    attended_copy.start()
    copies = []
    for j in range(count):
        start = pl.multiple_of(places[j][0] * columns, LANES)
        copy = pltpu.make_async_copy(
            weight_hbm.at[:, pl.ds(start, columns)], weight.at[j], weight_sem.at[j]
        )
        copy.start()
        copies.append(copy)
    attended_copy.wait()
    tile = min(256, columns)
    writes = []
    for j in range(count):
        copies[j].wait()
        for c in range(0, columns, tile):
            results[j, :, c : c + tile] = contract(
                attended[...], weight[j, :, c : c + tile], 1, 0
            ).astype(BF16)
        write = pltpu.make_async_copy(results.at[j], outs[j], out_sem.at[j])
        write.start()
        writes.append(write)
    for write in writes:
        write.wait()


def project(attended, weight, places, blocks):
    rows, depth = attended.shape
    columns = weight.shape[1] // blocks
    count = len(places)
    anywhere = pl.BlockSpec(memory_space=pl.ANY)
    return pl.pallas_call(
        functools.partial(project_kernel, count),
        grid_spec=pltpu.PrefetchScalarGridSpec(
            num_scalar_prefetch=count,
            grid=(1,),
            in_specs=[anywhere] * 2,
            out_specs=[anywhere] * count,
            scratch_shapes=[
                pltpu.VMEM((rows, depth), BF16),
                pltpu.VMEM((count, depth, columns), BF16),
                pltpu.VMEM((count, rows, columns), BF16),
                pltpu.SemaphoreType.DMA((1,)),
                pltpu.SemaphoreType.DMA((count,)),
                pltpu.SemaphoreType.DMA((count,)),
            ],
        ),
        out_shape=[jax.ShapeDtypeStruct((rows, columns), BF16)] * count,
        compiler_params=pltpu.CompilerParams(vmem_limit_bytes=KERNEL_VMEM),
        cost_estimate=pl.CostEstimate(
            flops=2 * rows * depth * columns * count,
            bytes_accessed=2 * depth * columns * count,
            transcendentals=0,
        ),
        name="project",
    )(*places, attended, weight)


def low_kernel(owners, resident, down, *refs):
    packed = refs[:owners]
    outs = refs[owners:]
    depth = down.shape[1]
    rank = down.shape[0] // resident
    weight = down[...]
    for k in range(owners):
        every = contract(packed[k][:, :depth], weight, 1, 1)
        marks = packed[k][:, depth:].astype(F32)
        low = every[:, :rank] * marks[:, 0:1]
        for y in range(1, resident):
            low = low + every[:, y * rank : (y + 1) * rank] * marks[:, y : y + 1]
        outs[k][...] = jnp.concatenate([low, jnp.zeros_like(low)], axis=1).astype(BF16)


def low_partial(packed, down):
    resident, rank, depth = down.shape
    owners = len(packed)
    per = packed[0].shape[0]
    return pl.pallas_call(
        functools.partial(low_kernel, owners, resident),
        out_shape=[jax.ShapeDtypeStruct((per, 2 * rank), BF16)] * owners,
        compiler_params=pltpu.CompilerParams(vmem_limit_bytes=SMALL_VMEM),
        cost_estimate=pl.CostEstimate(
            flops=2 * owners * per * depth * resident * rank,
            bytes_accessed=2 * depth * resident * rank,
            transcendentals=0,
        ),
        name="low",
    )(down.reshape(resident * rank, depth), *packed)


def unpack_kernel(placing, *refs):
    out = refs[-1]
    slots = jnp.concatenate([part[...] for part in refs[:-1]], axis=0)
    low = contract(placing[...], slots, 0, 0)
    half = low.shape[0] // 2
    rank = low.shape[1] // 2
    out[...] = jnp.concatenate([low[:half, :rank], low[half:, :rank]], axis=1).astype(BF16)


def unpack(placing, slots):
    rows = placing.shape[1]
    return pl.pallas_call(
        unpack_kernel,
        out_shape=jax.ShapeDtypeStruct((rows // 2, slots[0].shape[1]), BF16),
        compiler_params=pltpu.CompilerParams(vmem_limit_bytes=SMALL_VMEM),
        cost_estimate=pl.CostEstimate(flops=2**20, bytes_accessed=2**18, transcendentals=0),
        name="unpack",
    )(placing, *slots)


def combine_kernel(blocks, resident, marks, *refs):
    partials = refs[:blocks]
    lows = refs[blocks : 2 * blocks]
    ups = refs[2 * blocks : -1]
    out = refs[-1]
    base = partials[0][...].astype(F32)
    low = lows[0][...].astype(F32)
    for part in partials[1:]:
        base = base + part[...].astype(F32)
    for part in lows[1:]:
        low = low + part[...].astype(F32)
    rank = low.shape[1] // 2
    low = low.astype(BF16).astype(F32)
    low = jnp.concatenate([low[:, :rank], low[:, rank:]], axis=0)
    chosen = marks[...].astype(F32)
    first = 0
    for up in ups:
        held = up.shape[0] // rank
        spread = jnp.concatenate(
            [low * chosen[:, y : y + 1] for y in range(first, first + held)], axis=1
        ).astype(BF16)
        base = base + contract(spread, up[...], 1, 0)
        first += held
    out[...] = base.reshape(out.shape).astype(BF16)


def combine(marks, partials, lows, ups, resident, steps):
    rows, columns = partials[0].shape
    return pl.pallas_call(
        functools.partial(combine_kernel, len(partials), resident),
        out_shape=jax.ShapeDtypeStruct((rows // steps, steps, columns), BF16),
        compiler_params=pltpu.CompilerParams(vmem_limit_bytes=SMALL_VMEM),
        cost_estimate=pl.CostEstimate(flops=2**28, bytes_accessed=2**22, transcendentals=0),
        name="combine",
    )(marks, *partials, *lows, *ups)


def swap(value, axis, k):
    count = lax.axis_size(axis)
    return lax.ppermute(value, axis, [(i, i ^ k) for i in range(count)])


def gather(value, axis):
    held = {0: value}
    bit = lax.axis_size(axis) // 2
    while bit:
        for k in list(held):
            held[k ^ bit] = swap(held[k], axis, bit)
        bit //= 2
    return held


def body(
    queries,
    token_key_rows,
    token_value_rows,
    cached_key_rows,
    cached_value_rows,
    cache_length,
    request_adapter,
    output_weight_matrix,
    adapter_down_weight,
    adapter_up_weight,
):
    requests, steps, _ = queries.shape
    owners = lax.axis_size("adapter")
    blocks = lax.axis_size("tensor")
    resident, rank, columns = adapter_up_weight.shape
    place = lax.axis_index("adapter").reshape(1)
    mine = lax.axis_index("tensor")
    columns_of = lambda k: jnp.bitwise_xor(mine, k).reshape(1)

    up_rows = adapter_up_weight.reshape(resident * rank, columns)
    cut = resident * rank // 2
    early, late = up_rows[:cut], up_rows[cut:]
    early_parts = gather(early, "adapter")

    far = blocks - 1
    attended, placing, marks, first_partial, *packed = attend(
        queries,
        token_key_rows,
        token_value_rows,
        cached_key_rows,
        cached_value_rows,
        output_weight_matrix,
        cache_length,
        place,
        columns_of(far),
        request_adapter,
        owners,
        resident,
        columns,
    )
    arrived = [packed[0]] + [None] * (owners - 1)
    for k in range(owners - 1, 0, -1):
        arrived[k] = swap(packed[k], "adapter", k)
    partials = {far: swap(first_partial, "tensor", far)}
    others = list(range(far - 1, 0, -1))
    made = project(attended, output_weight_matrix, [columns_of(k) for k in others], blocks)
    for k, part in zip(others, made):
        partials[k] = swap(part, "tensor", k)
    (own,) = project(attended, output_weight_matrix, [mine.reshape(1)], blocks)
    lows = low_partial(arrived, adapter_down_weight)
    returned = [lows[0]] + [swap(lows[k], "adapter", k) for k in range(1, owners)]
    late, _ = lax.optimization_barrier((late, lows[1]))
    late_parts = gather(late, "adapter")
    low = unpack(placing, returned)
    low_parts = [low] + [swap(low, "tensor", k) for k in range(1, blocks)]
    ups = []
    for k in range(owners):
        ups += [early_parts[k], late_parts[k]]
    return combine(
        marks,
        [own] + [partials[k] for k in range(1, blocks)],
        low_parts,
        ups,
        resident,
        steps,
    )


def solution(mesh):
    rows = P(("group", "adapter"), None, "tensor")
    return jax.shard_map(
        body,
        mesh=mesh,
        in_specs=(
            rows,
            rows,
            rows,
            rows,
            rows,
            P(("group", "adapter")),
            P(("group", "adapter")),
            P("tensor", None),
            rows,
            rows,
        ),
        out_specs=rows,
        check_vma=False,
    )
```

time: 67.4 us -> 67.6 us (level)
  Pallas kernels: 34.6 us -> 16 us
  local copies, waits for them, and re-layouts: 3.82 us -> 14.2 us
  waiting for transfers between devices: 8.74 us -> 18.4 us
  starting transfers between devices: 19.7 us -> 18.4 us
    unnamed x24 -> x20, local copies, waits for them, and re-layouts: 2.07 us -> 14.2 us
    pallas_call x6 -> x4, Pallas kernels: 18.8 us -> 7.08 us  [the longest x2 4.79 us: project(): pl.pallas_call(functools.partial(project_kernel, count), grid_spec=pltpu....]
    ppermute x12 -> x18, waiting for transfers between devices: 8.74 us -> 18.4 us  [swap(): return lax.ppermute(value, axis, [(i, i ^ k) for i in range(count)])]
    pallas_call x1, Pallas kernels: 12.2 us -> 7.48 us  [attend(): pl.pallas_call(functools.partial(attend_kernel, owners, resident, capacit...]
    pallas_call x1, Pallas kernels: 3.68 us -> 1.47 us  [low_partial(): pl.pallas_call(functools.partial(low_kernel, owners, resident), out_shape...]
    reshape x1 -> x0, local copies, waits for them, and re-layouts: 1.75 us -> none  [body(): return mixed.reshape(requests, steps, columns)]
    ppermute x12 -> x18, starting transfers between devices: 19.7 us -> 18.4 us  [swap(): return lax.ppermute(value, axis, [(i, i ^ k) for i in range(count)])]
  transfers between devices with their start and end apart: 12 -> 18, of which waited for: 4 -> 6; matrix products, arithmetic and copies ran while one was open for 0% -> 0% of each run, Pallas kernels for 30% -> 10%
where the time goes in v2:
time: 67.6 us; the launch traced here: 67.2 us
  starting transfers between devices  18.4 us (27%)
  waiting for transfers between devices  18.4 us (27%)
  Pallas kernels  16 us (24%)
  local copies, waits for them, and re-layouts  14.2 us (21%)
    ppermute x18, starting transfers between devices, swap(): return lax.ppermute(value, axis, [(i, i ^ k) for i in range(count)])  18.4 us
    ppermute x18, waiting for transfers between devices, swap(): return lax.ppermute(value, axis, [(i, i ^ k) for i in range(count)])  18.4 us
    unnamed x20, local copies, waits for them, and re-layouts  14.2 us
    pallas_call x1, Pallas kernels, attend(): pl.pallas_call(functools.partial(attend_kernel, owners, resident, capacit...  7.48 us
    pallas_call x2, Pallas kernels, project(): pl.pallas_call(functools.partial(project_kernel, count), grid_spec=pltpu....  4.79 us
    pallas_call x1, Pallas kernels, combine(): pl.pallas_call(functools.partial(combine_kernel, len(partials), resident)...  2.03 us
    pallas_call x1, Pallas kernels, low_partial(): pl.pallas_call(functools.partial(low_kernel, owners, resident), out_shape...  1.47 us
  transfers between devices with their start and end apart: 18, of which 6 were waited for; matrix products, arithmetic and copies ran while one was open for 0% of the time, Pallas kernels for 10%

profile of v2, /device:TPU:0, one launch (start us, length us, event | category | flops | bytes accessed | tf_op | source)
XLA Modules:
  0.0 67.2 jit_solution(2128298401361575123)
XLA Ops:
  0.0 2.2 %copy-done.1 = bf16[64,128,256]{2,1,0:T(8,128)(2,1)S(1)} copy-done((bf16[64,128,256]{2,1,0:T(8,128)(2,1)S(1)}, bf16[64,128,256]{2,1,0:T(8,128)(2,1)}, u32[]{:S(2)}) %copy-start.1) | copy-done | bytes 4194328
  2.2 2.2 %copy-done.2 = bf16[64,128,256]{2,1,0:T(8,128)(2,1)S(1)} copy-done((bf16[64,128,256]{2,1,0:T(8,128)(2,1)S(1)}, bf16[64,128,256]{2,1,0:T(8,128)(2,1)}, u32[]{:S(2)}) %copy-start.2) | copy-done | bytes 4194328
  4.4 1.0 %copy-done.4 = bf16[64,2,2048]{2,1,0:T(2,128)(2,1)S(1)} copy-done((bf16[64,2,2048]{2,1,0:T(2,128)(2,1)S(1)}, bf16[64,2,2048]{2,1,0:T(2,128)(2,1)}, u32[]{:S(2)}) %copy-start.4) | copy-done | bytes 524312
  5.4 0.8 %copy-done.5 = bf16[64,2,256]{2,1,0:T(2,128)(2,1)S(1)} copy-done((bf16[64,2,256]{2,1,0:T(2,128)(2,1)S(1)}, bf16[64,2,256]{2,1,0:T(2,128)(2,1)}, u32[]{:S(2)}) %copy-start.5) | copy-done | bytes 65560
  8.4 7.5 %attend.1 = (bf16[128,2048]{1,0:T(8,128)(2,1)S(1)}, bf16[256,128]{1,0:T(8,128)(2,1)S(1)}, bf16[128,128]{1,0:T(8,128)(2,1)S(1)}, bf16[128,1024]{1,0:T(8,128)(2,1)...) custom-call(s32[64]{0:T(128)S(1)} %copy-done.7, ...), custom_call_target="tpu_custom_call" | custom-call | flops 268435456 | bytes 8388608 | tf_op jit(solution)/shard_map/attend/pallas_call | solution.py:264
  16.4 2.6 %collective-permute-start.4 = (bf16[64,2176]{1,0:T(8,128)(2,1)S(1)}, bf16[64,2176]{1,0:T(8,128)(2,1)S(1)}, u32[]{:S(2)}, u32[]{:S(2)}) collective-permute-start(bf16[64,2176]{1,0:T(8,128)(2,1)S(1)} %get-tuple-element.28), channel_id=1, source_target_pairs={{0,8},{4,12},{8,0},{12,4},{1,9},{5,13},{9,1},{13,5},{2,10},{6,14},... | collective-permute-start | bytes 835592 | tf_op jit(solution)/shard_map/ppermute | solution.py:476
  19.1 5.8 %copy-done = bf16[2048,4096]{1,0:T(8,128)(2,1)S(1)} copy-done((bf16[2048,4096]{1,0:T(8,128)(2,1)S(1)}, bf16[2048,4096]{1,0:T(8,128)(2,1)}, u32[]{:S(2)}) %copy-start) | copy-done | bytes 16777240
  24.8 3.2 %project.3 = (bf16[128,1024]{1,0:T(8,128)(2,1)S(1)}, bf16[128,1024]{1,0:T(8,128)(2,1)S(1)}) custom-call(s32[1]{0:T(128)} %bitcast.4.refs_0_, s32[1]{0:T(128)} %bitcast.5.refs_1_, bf16[128,2048]{1,0:T(8,128)(2,1)S(1)} %get-tuple-element.21.refs_1_.refs_2_, bf16[2048,4096]{1,0:T(8,128)(2,1)S(1)} %copy-done), custom_call_target="tpu_custom_call" | custom-call | flops 1073741824 | bytes 8388608 | tf_op jit(solution)/shard_map/project/pallas_call | solution.py:358
  28.0 1.9 %collective-permute-start = (bf16[128,1024]{1,0:T(8,128)(2,1)S(1)}, bf16[128,1024]{1,0:T(8,128)(2,1)S(1)}, u32[]{:S(2)}, u32[]{:S(2)}) collective-permute-start(bf16[128,1024]{1,0:T(8,128)(2,1)S(1)} %get-tuple-element.22), channel_id=1, source_target_pairs={{0,1},{1,0},{2,3},{3,2},{4,5},{5,4},{6,7},{7,6},{8,9},{9,8},{10,11... | collective-permute-start | bytes 786440 | tf_op jit(solution)/shard_map/ppermute | solution.py:476
  29.9 2.6 %collective-permute-start.1 = (bf16[128,1024]{1,0:T(8,128)(2,1)S(1)}, bf16[128,1024]{1,0:T(8,128)(2,1)S(1)}, u32[]{:S(2)}, u32[]{:S(2)}) collective-permute-start(bf16[128,1024]{1,0:T(8,128)(2,1)S(1)} %get-tuple-element.23), channel_id=1, source_target_pairs={{0,2},{1,3},{2,0},{3,1},{4,6},{5,7},{6,4},{7,5},{8,10},{9,11},{10,... | collective-permute-start | bytes 786440 | tf_op jit(solution)/shard_map/ppermute | solution.py:476
  32.5 1.6 %collective-permute-start.14 = (bf16[128,1024]{1,0:T(8,128)(2,1)S(1)}, bf16[128,1024]{1,0:T(8,128)(2,1)S(1)}, u32[]{:S(2)}, u32[]{:S(2)}) collective-permute-start(bf16[128,1024]{1,0:T(8,128)(2,1)S(1)} %bitcast.13), channel_id=1, source_target_pairs={{0,8},{4,12},{8,0},{12,4},{1,9},{5,13},{9,1},{13,5},{2,10},{6,14},... | collective-permute-start | bytes 786440 | tf_op jit(solution)/shard_map/ppermute | solution.py:476
  34.1 1.5 %low.1 = (bf16[64,128]{1,0:T(8,128)(2,1)S(1)}, bf16[64,128]{1,0:T(8,128)(2,1)S(1)}, bf16[64,128]{1,0:T(8,128)(2,1)S(1)}, bf16[64,128]{1,0:T(8,128)(2,1)S(1)}) custom-call(bf16[256,2048]{1,0:T(8,128)(2,1)S(1)} %bitcast.9, bf16[64,2176]{1,0:T(8,128)(2,1)S(1)} %get-tuple-element.26.refs_0_, bf16[64,2176]{1,0:T(8,128)(2,1)S(1)} %collective-permute-done.3.refs_1_, ...), custom_call_target="tpu_custom_call" | custom-call | flops 268435456 | bytes 1048576 | tf_op jit(solution)/shard_map/low/pallas_call | solution.py:404
  36.2 2.5 %collective-permute-start.2 = (bf16[128,1024]{1,0:T(8,128)(2,1)S(1)}, bf16[128,1024]{1,0:T(8,128)(2,1)S(1)}, u32[]{:S(2)}, u32[]{:S(2)}) collective-permute-start(bf16[128,1024]{1,0:T(8,128)(2,1)S(1)} %get-tuple-element.24), channel_id=1, source_target_pairs={{0,3},{1,2},{2,1},{3,0},{4,7},{5,6},{6,5},{7,4},{8,11},{9,10},{10,... | collective-permute-start | bytes 786440 | tf_op jit(solution)/shard_map/ppermute | solution.py:476
  38.6 3.4 %collective-permute-done.refs_1_ = bf16[128,1024]{1,0:T(8,128)(2,1)S(1)} collective-permute-done((bf16[128,1024]{1,0:T(8,128)(2,1)S(1)}, bf16[128,1024]{1,0:T(8,128)(2,1)S(1)}, u32[]{:S(2)}, u32[]{:S(2)}) %collective-permute-start) | collective-permute-done | bytes 262176 | tf_op jit(solution)/shard_map/ppermute | solution.py:476
  42.1 8.7 %collective-permute-done.1.refs_2_ = bf16[128,1024]{1,0:T(8,128)(2,1)S(1)} collective-permute-done((bf16[128,1024]{1,0:T(8,128)(2,1)S(1)}, bf16[128,1024]{1,0:T(8,128)(2,1)S(1)}, u32[]{:S(2)}, u32[]{:S(2)}) %collective-permute-start.1) | collective-permute-done | bytes 262176 | tf_op jit(solution)/shard_map/ppermute | solution.py:476
  50.8 2.0 %collective-permute-start.7 = (bf16[64,128]{1,0:T(8,128)(2,1)S(1)}, bf16[64,128]{1,0:T(8,128)(2,1)S(1)}, u32[]{:S(2)}, u32[]{:S(2)}) collective-permute-start(bf16[64,128]{1,0:T(8,128)(2,1)S(1)} %get-tuple-element.32), channel_id=1, source_target_pairs={{0,8},{4,12},{8,0},{12,4},{1,9},{5,13},{9,1},{13,5},{2,10},{6,14},... | collective-permute-start | bytes 49160 | tf_op jit(solution)/shard_map/ppermute | solution.py:476
  52.7 0.9 %collective-permute-start.8 = (bf16[64,128]{1,0:T(8,128)(2,1)S(1)}, bf16[64,128]{1,0:T(8,128)(2,1)S(1)}, u32[]{:S(2)}, u32[]{:S(2)}) collective-permute-start(bf16[64,128]{1,0:T(8,128)(2,1)S(1)} %get-tuple-element.33), channel_id=1, source_target_pairs={{0,12},{4,8},{8,4},{12,0},{1,13},{5,9},{9,5},{13,1},{2,14},{6,10},... | collective-permute-start | bytes 49160 | tf_op jit(solution)/shard_map/ppermute | solution.py:476
  54.5 1.4 %collective-permute-done.8.refs_3_ = bf16[64,128]{1,0:T(8,128)(2,1)S(1)} collective-permute-done((bf16[64,128]{1,0:T(8,128)(2,1)S(1)}, bf16[64,128]{1,0:T(8,128)(2,1)S(1)}, u32[]{:S(2)}, u32[]{:S(2)}) %collective-permute-start.8) | collective-permute-done | bytes 16416 | tf_op jit(solution)/shard_map/ppermute | solution.py:476
  56.7 0.8 %collective-permute-start.10 = (bf16[64,128]{1,0:T(8,128)(2,1)S(1)}, bf16[64,128]{1,0:T(8,128)(2,1)S(1)}, u32[]{:S(2)}, u32[]{:S(2)}) collective-permute-start(bf16[64,128]{1,0:T(8,128)(2,1)S(1)} %unpack.1.refs_4_), channel_id=1, source_target_pairs={{0,2},{1,3},{2,0},{3,1},{4,6},{5,7},{6,4},{7,5},{8,10},{9,11},{10,... | collective-permute-start | bytes 49160 | tf_op jit(solution)/shard_map/ppermute | solution.py:476
  57.5 1.8 %collective-permute-start.11 = (bf16[64,128]{1,0:T(8,128)(2,1)S(1)}, bf16[64,128]{1,0:T(8,128)(2,1)S(1)}, u32[]{:S(2)}, u32[]{:S(2)}) collective-permute-start(bf16[64,128]{1,0:T(8,128)(2,1)S(1)} %unpack.1.refs_4_), channel_id=1, source_target_pairs={{0,3},{1,2},{2,1},{3,0},{4,7},{5,6},{6,5},{7,4},{8,11},{9,10},{10,... | collective-permute-start | bytes 49160 | tf_op jit(solution)/shard_map/ppermute | solution.py:476
  59.3 2.1 %collective-permute-done.10.refs_6_ = bf16[64,128]{1,0:T(8,128)(2,1)S(1)} collective-permute-done((bf16[64,128]{1,0:T(8,128)(2,1)S(1)}, bf16[64,128]{1,0:T(8,128)(2,1)S(1)}, u32[]{:S(2)}, u32[]{:S(2)}) %collective-permute-start.10) | collective-permute-done | bytes 16416 | tf_op jit(solution)/shard_map/ppermute | solution.py:476
  61.5 1.6 %project.2.refs_0_ = bf16[128,1024]{1,0:T(8,128)(2,1)S(1)} custom-call(s32[1]{0:T(128)} %bitcast.3.refs_0_, bf16[128,2048]{1,0:T(8,128)(2,1)S(1)} %get-tuple-element.21.refs_1_.refs_2_, bf16[2048,4096]{1,0:T(8,128)(2,1)S(1)} %copy-done), custom_call_target="tpu_custom_call" | custom-call | flops 536870912 | bytes 4194304 | tf_op jit(solution)/shard_map/project/pallas_call | solution.py:358
  63.2 2.0 %collective-permute-done.9.refs_5_ = bf16[64,128]{1,0:T(8,128)(2,1)S(1)} collective-permute-done((bf16[64,128]{1,0:T(8,128)(2,1)S(1)}, bf16[64,128]{1,0:T(8,128)(2,1)S(1)}, u32[]{:S(2)}, u32[]{:S(2)}) %collective-permute-start.9) | collective-permute-done | bytes 16416 | tf_op jit(solution)/shard_map/ppermute | solution.py:476
  65.1 2.0 %combine.1 = bf16[64,2,1024]{2,1,0:T(2,128)(2,1)} custom-call(bf16[128,128]{1,0:T(8,128)(2,1)S(1)} %get-tuple-element.20.marks, bf16[128,1024]{1,0:T(8,128)(2,1)S(1)} %project.2.refs_0_, bf16[128,1024]{1,0:T(8,128)(2,1)S(1)} %collective-permute-done.refs_1_, bf16[128,1024]{1,0:T(8,128)(2,1)S(1)} %collective-permute-done.1.refs_2_, ...), custom_call_target="tpu_custom_call" | custom-call | flops 268435456 | bytes 4194304 | tf_op jit(solution)/shard_map/combine/pallas_call | solution.py:465
  (39 shorter events, 5.2 us)
Async XLA Ops:
  0.0 2.2 %copy-start.1 = (bf16[64,128,256]{2,1,0:T(8,128)(2,1)S(1)}, bf16[64,128,256]{2,1,0:T(8,128)(2,1)}, u32[]{:S(2)}) copy-start(bf16[64,128,256]{2,1,0:T(8,128)(2,1)} %cache_k_hbm.1) | copy-start | bytes 12582916
  2.2 2.2 %copy-start.2 = (bf16[64,128,256]{2,1,0:T(8,128)(2,1)S(1)}, bf16[64,128,256]{2,1,0:T(8,128)(2,1)}, u32[]{:S(2)}) copy-start(bf16[64,128,256]{2,1,0:T(8,128)(2,1)} %cache_v_hbm.1) | copy-start | bytes 12582916
  4.4 1.0 %copy-start.4 = (bf16[64,2,2048]{2,1,0:T(2,128)(2,1)S(1)}, bf16[64,2,2048]{2,1,0:T(2,128)(2,1)}, u32[]{:S(2)}) copy-start(bf16[64,2,2048]{2,1,0:T(2,128)(2,1)} %queries_hbm.1) | copy-start | bytes 1572868
  15.9 16.6 %collective-permute-start.3 = (bf16[64,2176]{1,0:T(8,128)(2,1)S(1)}, bf16[64,2176]{1,0:T(8,128)(2,1)S(1)}, u32[]{:S(2)}, u32[]{:S(2)}) collective-permute-start(bf16[64,2176]{1,0:T(8,128)(2,1)S(1)} %get-tuple-element.27), channel_id=1, source_target_pairs={{0,4},{4,0},{8,12},{12,8},{1,5},{5,1},{9,13},{13,9},{2,6},{6,2},{1... | collective-permute-start | bytes 835592 | tf_op jit(solution)/shard_map/ppermute | solution.py:476
  16.4 17.7 %collective-permute-start.4 = (bf16[64,2176]{1,0:T(8,128)(2,1)S(1)}, bf16[64,2176]{1,0:T(8,128)(2,1)S(1)}, u32[]{:S(2)}, u32[]{:S(2)}) collective-permute-start(bf16[64,2176]{1,0:T(8,128)(2,1)S(1)} %get-tuple-element.28), channel_id=1, source_target_pairs={{0,8},{4,12},{8,0},{12,4},{1,9},{5,13},{9,1},{13,5},{2,10},{6,14},... | collective-permute-start | bytes 835592 | tf_op jit(solution)/shard_map/ppermute | solution.py:476
  19.0 15.1 %collective-permute-start.5 = (bf16[64,2176]{1,0:T(8,128)(2,1)S(1)}, bf16[64,2176]{1,0:T(8,128)(2,1)S(1)}, u32[]{:S(2)}, u32[]{:S(2)}) collective-permute-start(bf16[64,2176]{1,0:T(8,128)(2,1)S(1)} %get-tuple-element.29), channel_id=1, source_target_pairs={{0,12},{4,8},{8,4},{12,0},{1,13},{5,9},{9,5},{13,1},{2,14},{6,10},... | collective-permute-start | bytes 835592 | tf_op jit(solution)/shard_map/ppermute | solution.py:476
  19.1 5.8 %copy-start = (bf16[2048,4096]{1,0:T(8,128)(2,1)S(1)}, bf16[2048,4096]{1,0:T(8,128)(2,1)}, u32[]{:S(2)}) copy-start(bf16[2048,4096]{1,0:T(8,128)(2,1)} %refs_3_.1) | copy-start | bytes 50331652
  24.8 7.7 %copy-start.9 = (bf16[4,64,1024]{2,1,0:T(8,128)(2,1)S(1)}, bf16[4,64,1024]{2,1,0:T(8,128)(2,1)}, u32[]{:S(2)}) copy-start(bf16[4,64,1024]{2,1,0:T(8,128)(2,1)} %param.19) | copy-start | bytes 1572868
  24.8 9.3 %copy-start.3 = (bf16[4,64,2048]{2,1,0:T(8,128)(2,1)S(1)}, bf16[4,64,2048]{2,1,0:T(8,128)(2,1)}, u32[]{:S(2)}) copy-start(bf16[4,64,2048]{2,1,0:T(8,128)(2,1)} %param.18) | copy-start | bytes 3145732
  28.0 14.0 %collective-permute-start = (bf16[128,1024]{1,0:T(8,128)(2,1)S(1)}, bf16[128,1024]{1,0:T(8,128)(2,1)S(1)}, u32[]{:S(2)}, u32[]{:S(2)}) collective-permute-start(bf16[128,1024]{1,0:T(8,128)(2,1)S(1)} %get-tuple-element.22), channel_id=1, source_target_pairs={{0,1},{1,0},{2,3},{3,2},{4,5},{5,4},{6,7},{7,6},{8,9},{9,8},{10,11... | collective-permute-start | bytes 786440 | tf_op jit(solution)/shard_map/ppermute | solution.py:476
  29.9 20.9 %collective-permute-start.1 = (bf16[128,1024]{1,0:T(8,128)(2,1)S(1)}, bf16[128,1024]{1,0:T(8,128)(2,1)S(1)}, u32[]{:S(2)}, u32[]{:S(2)}) collective-permute-start(bf16[128,1024]{1,0:T(8,128)(2,1)S(1)} %get-tuple-element.23), channel_id=1, source_target_pairs={{0,2},{1,3},{2,0},{3,1},{4,6},{5,7},{6,4},{7,5},{8,10},{9,11},{10,... | collective-permute-start | bytes 786440 | tf_op jit(solution)/shard_map/ppermute | solution.py:476
  32.5 18.2 %collective-permute-start.14 = (bf16[128,1024]{1,0:T(8,128)(2,1)S(1)}, bf16[128,1024]{1,0:T(8,128)(2,1)S(1)}, u32[]{:S(2)}, u32[]{:S(2)}) collective-permute-start(bf16[128,1024]{1,0:T(8,128)(2,1)S(1)} %bitcast.13), channel_id=1, source_target_pairs={{0,8},{4,12},{8,0},{12,4},{1,9},{5,13},{9,1},{13,5},{2,10},{6,14},... | collective-permute-start | bytes 786440 | tf_op jit(solution)/shard_map/ppermute | solution.py:476
  35.6 20.6 %collective-permute-start.15 = (bf16[128,1024]{1,0:T(8,128)(2,1)S(1)}, bf16[128,1024]{1,0:T(8,128)(2,1)S(1)}, u32[]{:S(2)}, u32[]{:S(2)}) collective-permute-start(bf16[128,1024]{1,0:T(8,128)(2,1)S(1)} %bitcast.10), channel_id=1, source_target_pairs={{0,8},{4,12},{8,0},{12,4},{1,9},{5,13},{9,1},{13,5},{2,10},{6,14},... | collective-permute-start | bytes 786440 | tf_op jit(solution)/shard_map/ppermute | solution.py:476
  36.2 20.5 %collective-permute-start.2 = (bf16[128,1024]{1,0:T(8,128)(2,1)S(1)}, bf16[128,1024]{1,0:T(8,128)(2,1)S(1)}, u32[]{:S(2)}, u32[]{:S(2)}) collective-permute-start(bf16[128,1024]{1,0:T(8,128)(2,1)S(1)} %get-tuple-element.24), channel_id=1, source_target_pairs={{0,3},{1,2},{2,1},{3,0},{4,7},{5,6},{6,5},{7,4},{8,11},{9,10},{10,... | collective-permute-start | bytes 786440 | tf_op jit(solution)/shard_map/ppermute | solution.py:476
  42.1 15.5 %collective-permute-start.12 = (bf16[128,1024]{1,0:T(8,128)(2,1)S(1)}, bf16[128,1024]{1,0:T(8,128)(2,1)S(1)}, u32[]{:S(2)}, u32[]{:S(2)}) collective-permute-start(bf16[128,1024]{1,0:T(8,128)(2,1)S(1)} %bitcast.14), channel_id=1, source_target_pairs={{0,4},{4,0},{8,12},{12,8},{1,5},{5,1},{9,13},{13,9},{2,6},{6,2},{1... | collective-permute-start | bytes 786440 | tf_op jit(solution)/shard_map/ppermute | solution.py:476
  50.7 2.0 %collective-permute-start.6 = (bf16[64,128]{1,0:T(8,128)(2,1)S(1)}, bf16[64,128]{1,0:T(8,128)(2,1)S(1)}, u32[]{:S(2)}, u32[]{:S(2)}) collective-permute-start(bf16[64,128]{1,0:T(8,128)(2,1)S(1)} %get-tuple-element.31), channel_id=1, source_target_pairs={{0,4},{4,0},{8,12},{12,8},{1,5},{5,1},{9,13},{13,9},{2,6},{6,2},{1... | collective-permute-start | bytes 49160 | tf_op jit(solution)/shard_map/ppermute | solution.py:476
  50.8 3.7 %collective-permute-start.7 = (bf16[64,128]{1,0:T(8,128)(2,1)S(1)}, bf16[64,128]{1,0:T(8,128)(2,1)S(1)}, u32[]{:S(2)}, u32[]{:S(2)}) collective-permute-start(bf16[64,128]{1,0:T(8,128)(2,1)S(1)} %get-tuple-element.32), channel_id=1, source_target_pairs={{0,8},{4,12},{8,0},{12,4},{1,9},{5,13},{9,1},{13,5},{2,10},{6,14},... | collective-permute-start | bytes 49160 | tf_op jit(solution)/shard_map/ppermute | solution.py:476
  52.7 3.2 %collective-permute-start.8 = (bf16[64,128]{1,0:T(8,128)(2,1)S(1)}, bf16[64,128]{1,0:T(8,128)(2,1)S(1)}, u32[]{:S(2)}, u32[]{:S(2)}) collective-permute-start(bf16[64,128]{1,0:T(8,128)(2,1)S(1)} %get-tuple-element.33), channel_id=1, source_target_pairs={{0,12},{4,8},{8,4},{12,0},{1,13},{5,9},{9,5},{13,1},{2,14},{6,10},... | collective-permute-start | bytes 49160 | tf_op jit(solution)/shard_map/ppermute | solution.py:476
  54.5 10.6 %collective-permute-start.16 = (bf16[128,1024]{1,0:T(8,128)(2,1)S(1)}, bf16[128,1024]{1,0:T(8,128)(2,1)S(1)}, u32[]{:S(2)}, u32[]{:S(2)}) collective-permute-start(bf16[128,1024]{1,0:T(8,128)(2,1)S(1)} %collective-permute-done.14.refs_12_), channel_id=1, source_target_pairs={{0,4},{4,0},{8,12},{12,8},{1,5},{5,1},{9,13},{13,9},{2,6},{6,2},{1... | collective-permute-start | bytes 786440 | tf_op jit(solution)/shard_map/ppermute | solution.py:476
  55.9 9.2 %collective-permute-start.13 = (bf16[128,1024]{1,0:T(8,128)(2,1)S(1)}, bf16[128,1024]{1,0:T(8,128)(2,1)S(1)}, u32[]{:S(2)}, u32[]{:S(2)}) collective-permute-start(bf16[128,1024]{1,0:T(8,128)(2,1)S(1)} %bitcast.11), channel_id=1, source_target_pairs={{0,4},{4,0},{8,12},{12,8},{1,5},{5,1},{9,13},{13,9},{2,6},{6,2},{1... | collective-permute-start | bytes 786440 | tf_op jit(solution)/shard_map/ppermute | solution.py:476
  56.1 9.0 %collective-permute-start.17 = (bf16[128,1024]{1,0:T(8,128)(2,1)S(1)}, bf16[128,1024]{1,0:T(8,128)(2,1)S(1)}, u32[]{:S(2)}, u32[]{:S(2)}) collective-permute-start(bf16[128,1024]{1,0:T(8,128)(2,1)S(1)} %collective-permute-done.15.refs_13_), channel_id=1, source_target_pairs={{0,4},{4,0},{8,12},{12,8},{1,5},{5,1},{9,13},{13,9},{2,6},{6,2},{1... | collective-permute-start | bytes 786440 | tf_op jit(solution)/shard_map/ppermute | solution.py:476
  56.7 4.7 %collective-permute-start.10 = (bf16[64,128]{1,0:T(8,128)(2,1)S(1)}, bf16[64,128]{1,0:T(8,128)(2,1)S(1)}, u32[]{:S(2)}, u32[]{:S(2)}) collective-permute-start(bf16[64,128]{1,0:T(8,128)(2,1)S(1)} %unpack.1.refs_4_), channel_id=1, source_target_pairs={{0,2},{1,3},{2,0},{3,1},{4,6},{5,7},{6,4},{7,5},{8,10},{9,11},{10,... | collective-permute-start | bytes 49160 | tf_op jit(solution)/shard_map/ppermute | solution.py:476
  57.5 5.6 %collective-permute-start.11 = (bf16[64,128]{1,0:T(8,128)(2,1)S(1)}, bf16[64,128]{1,0:T(8,128)(2,1)S(1)}, u32[]{:S(2)}, u32[]{:S(2)}) collective-permute-start(bf16[64,128]{1,0:T(8,128)(2,1)S(1)} %unpack.1.refs_4_), channel_id=1, source_target_pairs={{0,3},{1,2},{2,1},{3,0},{4,7},{5,6},{6,5},{7,4},{8,11},{9,10},{10,... | collective-permute-start | bytes 49160 | tf_op jit(solution)/shard_map/ppermute | solution.py:476
  61.4 3.7 %collective-permute-start.9 = (bf16[64,128]{1,0:T(8,128)(2,1)S(1)}, bf16[64,128]{1,0:T(8,128)(2,1)S(1)}, u32[]{:S(2)}, u32[]{:S(2)}) collective-permute-start(bf16[64,128]{1,0:T(8,128)(2,1)S(1)} %unpack.1.refs_4_), channel_id=1, source_target_pairs={{0,1},{1,0},{2,3},{3,2},{4,5},{5,4},{6,7},{7,6},{8,9},{9,8},{10,11... | collective-permute-start | bytes 49160 | tf_op jit(solution)/shard_map/ppermute | solution.py:476
  (4 other events, 3.0 us)

commit v3 on v2

--- a/solution.py
+++ b/solution.py
@@ -11,7 +11,8 @@
 HEAD_DIM = 128
 NEGATIVE = -1e30
 LANES = 128
-KERNEL_VMEM = 32 * 1024 * 1024
+KERNEL_VMEM = 56 * 1024 * 1024
+SMALL_COST = pl.CostEstimate(flops=1024, bytes_accessed=1024, transcendentals=0)
 SMALL_VMEM = 12 * 1024 * 1024
 
 F32 = jnp.float32
@@ -298,11 +299,7 @@
         ]
         + [jax.ShapeDtypeStruct((per, width + LANES), BF16)] * owners,
         compiler_params=pltpu.CompilerParams(vmem_limit_bytes=KERNEL_VMEM),
-        cost_estimate=pl.CostEstimate(
-            flops=8 * total_rows * width * cache_size,
-            bytes_accessed=4 * requests * cache_size * kv_width,
-            transcendentals=0,
-        ),
+        cost_estimate=SMALL_COST,
         name="attend",
     )(
         lengths,
@@ -373,11 +370,7 @@
         ),
         out_shape=[jax.ShapeDtypeStruct((rows, columns), BF16)] * count,
         compiler_params=pltpu.CompilerParams(vmem_limit_bytes=KERNEL_VMEM),
-        cost_estimate=pl.CostEstimate(
-            flops=2 * rows * depth * columns * count,
-            bytes_accessed=2 * depth * columns * count,
-            transcendentals=0,
-        ),
+        cost_estimate=SMALL_COST,
         name="project",
     )(*places, attended, weight)
 
@@ -405,11 +398,7 @@
         functools.partial(low_kernel, owners, resident),
         out_shape=[jax.ShapeDtypeStruct((per, 2 * rank), BF16)] * owners,
         compiler_params=pltpu.CompilerParams(vmem_limit_bytes=SMALL_VMEM),
-        cost_estimate=pl.CostEstimate(
-            flops=2 * owners * per * depth * resident * rank,
-            bytes_accessed=2 * depth * resident * rank,
-            transcendentals=0,
-        ),
+        cost_estimate=SMALL_COST,
         name="low",
     )(down.reshape(resident * rank, depth), *packed)
 
@@ -429,7 +418,7 @@
         unpack_kernel,
         out_shape=jax.ShapeDtypeStruct((rows // 2, slots[0].shape[1]), BF16),
         compiler_params=pltpu.CompilerParams(vmem_limit_bytes=SMALL_VMEM),
-        cost_estimate=pl.CostEstimate(flops=2**20, bytes_accessed=2**18, transcendentals=0),
+        cost_estimate=SMALL_COST,
         name="unpack",
     )(placing, *slots)
 
@@ -466,7 +455,7 @@
         functools.partial(combine_kernel, len(partials), resident),
         out_shape=jax.ShapeDtypeStruct((rows // steps, steps, columns), BF16),
         compiler_params=pltpu.CompilerParams(vmem_limit_bytes=SMALL_VMEM),
-        cost_estimate=pl.CostEstimate(flops=2**28, bytes_accessed=2**22, transcendentals=0),
+        cost_estimate=SMALL_COST,
         name="combine",
     )(marks, *partials, *lows, *ups)
 
@@ -476,14 +465,12 @@
     return lax.ppermute(value, axis, [(i, i ^ k) for i in range(count)])
 
 
-def gather(value, axis):
-    held = {0: value}
-    bit = lax.axis_size(axis) // 2
+def forward(held, axis, bit):
     while bit:
         for k in list(held):
-            held[k ^ bit] = swap(held[k], axis, bit)
+            if k ^ bit not in held:
+                held[k ^ bit] = swap(held[k], axis, bit)
         bit //= 2
-    return held
 
 
 def body(
@@ -507,9 +494,10 @@
     columns_of = lambda k: jnp.bitwise_xor(mine, k).reshape(1)
 
     up_rows = adapter_up_weight.reshape(resident * rank, columns)
-    cut = resident * rank // 2
-    early, late = up_rows[:cut], up_rows[cut:]
-    early_parts = gather(early, "adapter")
+    top_bit = owners // 2
+    ups = {0: up_rows}
+    ups[top_bit] = swap(up_rows, "adapter", top_bit)
+    ups[1] = swap(up_rows, "adapter", 1)
 
     far = blocks - 1
     attended, placing, marks, first_partial, *packed = attend(
@@ -527,29 +515,34 @@
         resident,
         columns,
     )
+    ups[1], attended, first_partial, packed = lax.optimization_barrier(
+        (ups[1], attended, first_partial, packed)
+    )
     arrived = [packed[0]] + [None] * (owners - 1)
     for k in range(owners - 1, 0, -1):
         arrived[k] = swap(packed[k], "adapter", k)
     partials = {far: swap(first_partial, "tensor", far)}
     others = list(range(far - 1, 0, -1))
     made = project(attended, output_weight_matrix, [columns_of(k) for k in others], blocks)
+    made, arrived[1], ups[top_bit] = lax.optimization_barrier(
+        (made, arrived[1], ups[top_bit])
+    )
     for k, part in zip(others, made):
         partials[k] = swap(part, "tensor", k)
     (own,) = project(attended, output_weight_matrix, [mine.reshape(1)], blocks)
+    arrived, partials[far], own = lax.optimization_barrier((arrived, partials[far], own))
     lows = low_partial(arrived, adapter_down_weight)
     returned = [lows[0]] + [swap(lows[k], "adapter", k) for k in range(1, owners)]
-    late, _ = lax.optimization_barrier((late, lows[1]))
-    late_parts = gather(late, "adapter")
+    returned, partials = lax.optimization_barrier((returned, partials))
     low = unpack(placing, returned)
+    ups, low = lax.optimization_barrier((ups, low))
     low_parts = [low] + [swap(low, "tensor", k) for k in range(1, blocks)]
-    ups = []
-    for k in range(owners):
-        ups += [early_parts[k], late_parts[k]]
+    forward(ups, "adapter", top_bit // 2)
     return combine(
         marks,
         [own] + [partials[k] for k in range(1, blocks)],
         low_parts,
-        ups,
+        [ups[k] for k in range(owners)],
         resident,
         steps,
     )

time: 67.6 us -> 53.6 us (0.79)
  local copies, waits for them, and re-layouts: 14.2 us -> 0.96 us
  Pallas kernels: 16 us -> 22.6 us
  waiting for transfers between devices: 18.4 us -> 14 us
  starting transfers between devices: 18.4 us -> 15.8 us
    unnamed x20 -> x12, local copies, waits for them, and re-layouts: 14.2 us -> 0.96 us
    ppermute x18 -> x15, waiting for transfers between devices: 18.4 us -> 14 us  [swap(): return lax.ppermute(value, axis, [(i, i ^ k) for i in range(count)])]
    pallas_call x2, Pallas kernels: 4.79 us -> 9.04 us  [project(): pl.pallas_call(functools.partial(project_kernel, count), grid_spec=pltpu....]
    ppermute x18 -> x15, starting transfers between devices: 18.4 us -> 15.8 us  [swap(): return lax.ppermute(value, axis, [(i, i ^ k) for i in range(count)])]
    pallas_call x1, Pallas kernels: 7.48 us -> 10.1 us  [attend(): pl.pallas_call(functools.partial(attend_kernel, owners, resident, capacit...]
  transfers between devices with their start and end apart: 18 -> 15, of which waited for: 6 -> 5; matrix products, arithmetic and copies ran while one was open for 0% -> 0% of each run, Pallas kernels for 10% -> 39%
where the time goes in v3:
time: 53.6 us; the launch traced here: 53.5 us
  Pallas kernels  22.6 us (42%)
  starting transfers between devices  15.8 us (29%)
  waiting for transfers between devices  14 us (26%)
  local copies, waits for them, and re-layouts  0.96 us (2%)
    ppermute x15, starting transfers between devices, swap(): return lax.ppermute(value, axis, [(i, i ^ k) for i in range(count)])  15.8 us
    ppermute x15, waiting for transfers between devices, swap(): return lax.ppermute(value, axis, [(i, i ^ k) for i in range(count)])  14 us
    pallas_call x1, Pallas kernels, attend(): pl.pallas_call(functools.partial(attend_kernel, owners, resident, capacit...  10.1 us
    pallas_call x2, Pallas kernels, project(): pl.pallas_call(functools.partial(project_kernel, count), grid_spec=pltpu....  9.04 us
    pallas_call x1, Pallas kernels, combine(): pl.pallas_call(functools.partial(combine_kernel, len(partials), resident)...  1.72 us
    pallas_call x1, Pallas kernels, low_partial(): pl.pallas_call(functools.partial(low_kernel, owners, resident), out_shape...  1.47 us
  transfers between devices with their start and end apart: 15, of which 5 were waited for; matrix products, arithmetic and copies ran while one was open for 0% of the time, Pallas kernels for 39%

profile of v3, /device:TPU:0, one launch (start us, length us, event | category | flops | bytes accessed | tf_op | source)
XLA Modules:
  0.0 53.5 jit_solution(13939217989560170781)
XLA Ops:
  0.0 0.5 collective-permute-start
  0.5 2.5 %collective-permute-start.2 = (bf16[256,1024]{1,0:T(8,128)(2,1)}, bf16[256,1024]{1,0:T(8,128)(2,1)S(1)}, u32[]{:S(2)}, u32[]{:S(2)}) collective-permute-start(bf16[256,1024]{1,0:T(8,128)(2,1)} %bitcast.10), channel_id=1, source_target_pairs={{0,8},{4,12},{8,0},{12,4},{1,9},{5,13},{9,1},{13,5},{2,10},{6,14},... | collective-permute-start | bytes 1572872 | tf_op jit(solution)/shard_map/ppermute | solution.py:465
  2.9 10.1 %attend.1 = (bf16[128,2048]{1,0:T(8,128)(2,1)}, bf16[256,128]{1,0:T(8,128)(2,1)}, bf16[128,128]{1,0:T(8,128)(2,1)}, bf16[128,1024]{1,0:T(8,128)(2,1)}, bf16[64,2...) custom-call(s32[64]{0:T(128)} %lengths.1, s32[1]{0:T(128)} %bitcast.place, ...), custom_call_target="tpu_custom_call" | custom-call | flops 1024 | bytes 1024 | tf_op jit(solution)/shard_map/attend/pallas_call | solution.py:265
  13.1 0.3 collective-permute-start.1
  13.4 0.3 collective-permute-start.3
  13.6 1.4 %collective-permute-start.4 = (bf16[64,2176]{1,0:T(8,128)(2,1)}, bf16[64,2176]{1,0:T(8,128)(2,1)S(1)}, u32[]{:S(2)}, u32[]{:S(2)}) collective-permute-start(bf16[64,2176]{1,0:T(8,128)(2,1)} %get-tuple-element.61), channel_id=1, source_target_pairs={{0,12},{4,8},{8,4},{12,0},{1,13},{5,9},{9,5},{13,1},{2,14},{6,10},... | collective-permute-start | bytes 835592 | tf_op jit(solution)/shard_map/ppermute | solution.py:465
  15.0 3.6 %collective-permute-start.5 = (bf16[128,1024]{1,0:T(8,128)(2,1)}, bf16[128,1024]{1,0:T(8,128)(2,1)S(1)}, u32[]{:S(2)}, u32[]{:S(2)}) collective-permute-start(bf16[128,1024]{1,0:T(8,128)(2,1)} %get-tuple-element.62), channel_id=1, source_target_pairs={{0,3},{1,2},{2,1},{3,0},{4,7},{5,6},{6,5},{7,4},{8,11},{9,10},{10,... | collective-permute-start | bytes 786440 | tf_op jit(solution)/shard_map/ppermute | solution.py:465
  18.6 5.1 %project.2 = (bf16[128,1024]{1,0:T(8,128)(2,1)}, bf16[128,1024]{1,0:T(8,128)(2,1)}) custom-call(s32[1]{0:T(128)} %bitcast.4.refs_0_, s32[1]{0:T(128)} %bitcast.5.refs_1_, bf16[128,2048]{1,0:T(8,128)(2,1)} %get-tuple-element.55.refs_2_.refs_1_, bf16[2048,4096]{1,0:T(8,128)(2,1)} %refs_2_.1), custom_call_target="tpu_custom_call" | custom-call | flops 1024 | bytes 1024 | tf_op jit(solution)/shard_map/project/pallas_call | solution.py:355
  23.8 0.8 %collective-permute-start.9 = (bf16[128,1024]{1,0:T(8,128)(2,1)}, bf16[128,1024]{1,0:T(8,128)(2,1)S(1)}, u32[]{:S(2)}, u32[]{:S(2)}) collective-permute-start(bf16[128,1024]{1,0:T(8,128)(2,1)} %get-tuple-element.72), channel_id=1, source_target_pairs={{0,1},{1,0},{2,3},{3,2},{4,5},{5,4},{6,7},{7,6},{8,9},{9,8},{10,11... | collective-permute-start | bytes 786440 | tf_op jit(solution)/shard_map/ppermute | solution.py:465
  24.6 3.9 %project.3.refs_0_ = bf16[128,1024]{1,0:T(8,128)(2,1)} custom-call(s32[1]{0:T(128)} %bitcast.6.refs_0_, bf16[128,2048]{1,0:T(8,128)(2,1)} %get-tuple-element.55.refs_2_.refs_1_, bf16[2048,4096]{1,0:T(8,128)(2,1)} %refs_2_.1), custom_call_target="tpu_custom_call" | custom-call | flops 1024 | bytes 1024 | tf_op jit(solution)/shard_map/project/pallas_call | solution.py:355
  28.6 1.5 %low.1 = (bf16[64,128]{1,0:T(8,128)(2,1)S(1)}, bf16[64,128]{1,0:T(8,128)(2,1)S(1)}, bf16[64,128]{1,0:T(8,128)(2,1)S(1)}, bf16[64,128]{1,0:T(8,128)(2,1)S(1)}) custom-call(bf16[256,2048]{1,0:T(8,128)(2,1)S(1)} %bitcast.8, bf16[64,2176]{1,0:T(8,128)(2,1)S(1)} %copy-done.3, bf16[64,2176]{1,0:T(8,128)(2,1)S(1)} %collective-permute-done.1.refs_1_, ...), custom_call_target="tpu_custom_call" | custom-call | flops 1024 | bytes 1024 | tf_op jit(solution)/shard_map/low/pallas_call | solution.py:397
  30.2 0.9 %collective-permute-start.7 = (bf16[64,128]{1,0:T(8,128)(2,1)S(1)}, bf16[64,128]{1,0:T(8,128)(2,1)S(1)}, u32[]{:S(2)}, u32[]{:S(2)}) collective-permute-start(bf16[64,128]{1,0:T(8,128)(2,1)S(1)} %get-tuple-element.70), channel_id=1, source_target_pairs={{0,8},{4,12},{8,0},{12,4},{1,9},{5,13},{9,1},{13,5},{2,10},{6,14},... | collective-permute-start | bytes 49160 | tf_op jit(solution)/shard_map/ppermute | solution.py:465
  31.1 0.9 %collective-permute-start.8 = (bf16[64,128]{1,0:T(8,128)(2,1)S(1)}, bf16[64,128]{1,0:T(8,128)(2,1)S(1)}, u32[]{:S(2)}, u32[]{:S(2)}) collective-permute-start(bf16[64,128]{1,0:T(8,128)(2,1)S(1)} %get-tuple-element.71), channel_id=1, source_target_pairs={{0,12},{4,8},{8,4},{12,0},{1,13},{5,9},{9,5},{13,1},{2,14},{6,10},... | collective-permute-start | bytes 49160 | tf_op jit(solution)/shard_map/ppermute | solution.py:465
  32.0 1.9 %collective-permute-done.7.refs_2_ = bf16[64,128]{1,0:T(8,128)(2,1)S(1)} collective-permute-done((bf16[64,128]{1,0:T(8,128)(2,1)S(1)}, bf16[64,128]{1,0:T(8,128)(2,1)S(1)}, u32[]{:S(2)}, u32[]{:S(2)}) %collective-permute-start.7) | collective-permute-done | bytes 16416 | tf_op jit(solution)/shard_map/ppermute | solution.py:465
  34.0 0.4 collective-permute-done.8.refs_3_
  34.4 7.4 %collective-permute-done.10.refs_2_ = bf16[128,1024]{1,0:T(8,128)(2,1)S(1)} collective-permute-done((bf16[128,1024]{1,0:T(8,128)(2,1)}, bf16[128,1024]{1,0:T(8,128)(2,1)S(1)}, u32[]{:S(2)}, u32[]{:S(2)}) %collective-permute-start.10) | collective-permute-done | bytes 262176 | tf_op jit(solution)/shard_map/ppermute | solution.py:465
  41.8 0.3 unpack.1.refs_4_
  42.1 1.0 %collective-permute-start.11 = (bf16[64,128]{1,0:T(8,128)(2,1)S(1)}, bf16[64,128]{1,0:T(8,128)(2,1)S(1)}, u32[]{:S(2)}, u32[]{:S(2)}) collective-permute-start(bf16[64,128]{1,0:T(8,128)(2,1)S(1)} %unpack.1.refs_4_), channel_id=1, source_target_pairs={{0,1},{1,0},{2,3},{3,2},{4,5},{5,4},{6,7},{7,6},{8,9},{9,8},{10,11... | collective-permute-start | bytes 49160 | tf_op jit(solution)/shard_map/ppermute | solution.py:465
  43.1 2.1 %collective-permute-start.12 = (bf16[64,128]{1,0:T(8,128)(2,1)S(1)}, bf16[64,128]{1,0:T(8,128)(2,1)S(1)}, u32[]{:S(2)}, u32[]{:S(2)}) collective-permute-start(bf16[64,128]{1,0:T(8,128)(2,1)S(1)} %unpack.1.refs_4_), channel_id=1, source_target_pairs={{0,2},{1,3},{2,0},{3,1},{4,6},{5,7},{6,4},{7,5},{8,10},{9,11},{10,... | collective-permute-start | bytes 49160 | tf_op jit(solution)/shard_map/ppermute | solution.py:465
  45.2 1.3 %collective-permute-start.13 = (bf16[64,128]{1,0:T(8,128)(2,1)S(1)}, bf16[64,128]{1,0:T(8,128)(2,1)S(1)}, u32[]{:S(2)}, u32[]{:S(2)}) collective-permute-start(bf16[64,128]{1,0:T(8,128)(2,1)S(1)} %unpack.1.refs_4_), channel_id=1, source_target_pairs={{0,3},{1,2},{2,1},{3,0},{4,7},{5,6},{6,5},{7,4},{8,11},{9,10},{10,... | collective-permute-start | bytes 49160 | tf_op jit(solution)/shard_map/ppermute | solution.py:465
  46.6 1.1 %collective-permute-done.12.refs_6_ = bf16[64,128]{1,0:T(8,128)(2,1)S(1)} collective-permute-done((bf16[64,128]{1,0:T(8,128)(2,1)S(1)}, bf16[64,128]{1,0:T(8,128)(2,1)S(1)}, u32[]{:S(2)}, u32[]{:S(2)}) %collective-permute-start.12) | collective-permute-done | bytes 16416 | tf_op jit(solution)/shard_map/ppermute | solution.py:465
  47.7 3.0 %collective-permute-done.13.refs_7_ = bf16[64,128]{1,0:T(8,128)(2,1)S(1)} collective-permute-done((bf16[64,128]{1,0:T(8,128)(2,1)S(1)}, bf16[64,128]{1,0:T(8,128)(2,1)S(1)}, u32[]{:S(2)}, u32[]{:S(2)}) %collective-permute-start.13) | collective-permute-done | bytes 16416 | tf_op jit(solution)/shard_map/ppermute | solution.py:465
  50.8 0.9 %copy-done = bf16[128,1024]{1,0:T(8,128)(2,1)S(1)} copy-done((bf16[128,1024]{1,0:T(8,128)(2,1)S(1)}, bf16[128,1024]{1,0:T(8,128)(2,1)}, u32[]{:S(2)}) %copy-start) | copy-done | bytes 262168
  51.7 1.7 %combine.1 = bf16[64,2,1024]{2,1,0:T(2,128)(2,1)} custom-call(bf16[128,128]{1,0:T(8,128)(2,1)S(1)} %copy-done.5, bf16[128,1024]{1,0:T(8,128)(2,1)S(1)} %copy-done, bf16[128,1024]{1,0:T(8,128)(2,1)S(1)} %collective-permute-done.9.refs_1_, bf16[128,1024]{1,0:T(8,128)(2,1)S(1)} %collective-permute-done.10.refs_2_, ...), custom_call_target="tpu_custom_call" | custom-call | flops 1024 | bytes 1024 | tf_op jit(solution)/shard_map/combine/pallas_call | solution.py:454
  (24 shorter events, 0.3 us)
Async XLA Ops:
  0.0 13.1 %collective-permute-start = (bf16[256,1024]{1,0:T(8,128)(2,1)}, bf16[256,1024]{1,0:T(8,128)(2,1)S(1)}, u32[]{:S(2)}, u32[]{:S(2)}) collective-permute-start(bf16[256,1024]{1,0:T(8,128)(2,1)} %bitcast.9), channel_id=1, source_target_pairs={{0,4},{4,0},{8,12},{12,8},{1,5},{5,1},{9,13},{13,9},{2,6},{6,2},{1... | collective-permute-start | bytes 1572872 | tf_op jit(solution)/shard_map/ppermute | solution.py:465
  0.5 23.3 %collective-permute-start.2 = (bf16[256,1024]{1,0:T(8,128)(2,1)}, bf16[256,1024]{1,0:T(8,128)(2,1)S(1)}, u32[]{:S(2)}, u32[]{:S(2)}) collective-permute-start(bf16[256,1024]{1,0:T(8,128)(2,1)} %bitcast.10), channel_id=1, source_target_pairs={{0,8},{4,12},{8,0},{12,4},{1,9},{5,13},{9,1},{13,5},{2,10},{6,14},... | collective-permute-start | bytes 1572872 | tf_op jit(solution)/shard_map/ppermute | solution.py:465
  13.1 10.6 %collective-permute-start.1 = (bf16[64,2176]{1,0:T(8,128)(2,1)}, bf16[64,2176]{1,0:T(8,128)(2,1)S(1)}, u32[]{:S(2)}, u32[]{:S(2)}) collective-permute-start(bf16[64,2176]{1,0:T(8,128)(2,1)} %get-tuple-element.58), channel_id=1, source_target_pairs={{0,4},{4,0},{8,12},{12,8},{1,5},{5,1},{9,13},{13,9},{2,6},{6,2},{1... | collective-permute-start | bytes 835592 | tf_op jit(solution)/shard_map/ppermute | solution.py:465
  13.4 15.2 %collective-permute-start.3 = (bf16[64,2176]{1,0:T(8,128)(2,1)}, bf16[64,2176]{1,0:T(8,128)(2,1)S(1)}, u32[]{:S(2)}, u32[]{:S(2)}) collective-permute-start(bf16[64,2176]{1,0:T(8,128)(2,1)} %get-tuple-element.60), channel_id=1, source_target_pairs={{0,8},{4,12},{8,0},{12,4},{1,9},{5,13},{9,1},{13,5},{2,10},{6,14},... | collective-permute-start | bytes 835592 | tf_op jit(solution)/shard_map/ppermute | solution.py:465
  13.6 14.9 %collective-permute-start.4 = (bf16[64,2176]{1,0:T(8,128)(2,1)}, bf16[64,2176]{1,0:T(8,128)(2,1)S(1)}, u32[]{:S(2)}, u32[]{:S(2)}) collective-permute-start(bf16[64,2176]{1,0:T(8,128)(2,1)} %get-tuple-element.61), channel_id=1, source_target_pairs={{0,12},{4,8},{8,4},{12,0},{1,13},{5,9},{9,5},{13,1},{2,14},{6,10},... | collective-permute-start | bytes 835592 | tf_op jit(solution)/shard_map/ppermute | solution.py:465
  15.0 13.6 %collective-permute-start.5 = (bf16[128,1024]{1,0:T(8,128)(2,1)}, bf16[128,1024]{1,0:T(8,128)(2,1)S(1)}, u32[]{:S(2)}, u32[]{:S(2)}) collective-permute-start(bf16[128,1024]{1,0:T(8,128)(2,1)} %get-tuple-element.62), channel_id=1, source_target_pairs={{0,3},{1,2},{2,1},{3,0},{4,7},{5,6},{6,5},{7,4},{8,11},{9,10},{10,... | collective-permute-start | bytes 786440 | tf_op jit(solution)/shard_map/ppermute | solution.py:465
  23.7 18.1 %collective-permute-start.10 = (bf16[128,1024]{1,0:T(8,128)(2,1)}, bf16[128,1024]{1,0:T(8,128)(2,1)S(1)}, u32[]{:S(2)}, u32[]{:S(2)}) collective-permute-start(bf16[128,1024]{1,0:T(8,128)(2,1)} %get-tuple-element.73), channel_id=1, source_target_pairs={{0,2},{1,3},{2,0},{3,1},{4,6},{5,7},{6,4},{7,5},{8,10},{9,11},{10,... | collective-permute-start | bytes 786440 | tf_op jit(solution)/shard_map/ppermute | solution.py:465
  23.8 18.0 %collective-permute-start.9 = (bf16[128,1024]{1,0:T(8,128)(2,1)}, bf16[128,1024]{1,0:T(8,128)(2,1)S(1)}, u32[]{:S(2)}, u32[]{:S(2)}) collective-permute-start(bf16[128,1024]{1,0:T(8,128)(2,1)} %get-tuple-element.72), channel_id=1, source_target_pairs={{0,1},{1,0},{2,3},{3,2},{4,5},{5,4},{6,7},{7,6},{8,9},{9,8},{10,11... | collective-permute-start | bytes 786440 | tf_op jit(solution)/shard_map/ppermute | solution.py:465
  24.6 4.0 %copy-start.1 = (bf16[4,64,2048]{2,1,0:T(8,128)(2,1)S(1)}, bf16[4,64,2048]{2,1,0:T(8,128)(2,1)}, u32[]{:S(2)}) copy-start(bf16[4,64,2048]{2,1,0:T(8,128)(2,1)} %param.18) | copy-start | bytes 3145732
  24.6 4.0 %copy-start.3 = (bf16[64,2176]{1,0:T(8,128)(2,1)S(1)}, bf16[64,2176]{1,0:T(8,128)(2,1)}, u32[]{:S(2)}) copy-start(bf16[64,2176]{1,0:T(8,128)(2,1)} %get-tuple-element.64.refs_0_) | copy-start | bytes 835588
  24.6 17.2 %copy-start.4 = (bf16[256,128]{1,0:T(8,128)(2,1)S(1)}, bf16[256,128]{1,0:T(8,128)(2,1)}, u32[]{:S(2)}) copy-start(bf16[256,128]{1,0:T(8,128)(2,1)} %get-tuple-element.80.placing) | copy-start | bytes 196612
  24.6 26.2 %copy-start.2 = (bf16[4,64,1024]{2,1,0:T(8,128)(2,1)S(1)}, bf16[4,64,1024]{2,1,0:T(8,128)(2,1)}, u32[]{:S(2)}) copy-start(bf16[4,64,1024]{2,1,0:T(8,128)(2,1)} %param.19) | copy-start | bytes 1572868
  24.6 26.2 %copy-start.5 = (bf16[128,128]{1,0:T(8,128)(2,1)S(1)}, bf16[128,128]{1,0:T(8,128)(2,1)}, u32[]{:S(2)}) copy-start(bf16[128,128]{1,0:T(8,128)(2,1)} %get-tuple-element.47.marks) | copy-start | bytes 98308
  30.1 1.9 %collective-permute-start.6 = (bf16[64,128]{1,0:T(8,128)(2,1)S(1)}, bf16[64,128]{1,0:T(8,128)(2,1)S(1)}, u32[]{:S(2)}, u32[]{:S(2)}) collective-permute-start(bf16[64,128]{1,0:T(8,128)(2,1)S(1)} %get-tuple-element.69), channel_id=1, source_target_pairs={{0,4},{4,0},{8,12},{12,8},{1,5},{5,1},{9,13},{13,9},{2,6},{6,2},{1... | collective-permute-start | bytes 49160 | tf_op jit(solution)/shard_map/ppermute | solution.py:465
  30.2 3.8 %collective-permute-start.7 = (bf16[64,128]{1,0:T(8,128)(2,1)S(1)}, bf16[64,128]{1,0:T(8,128)(2,1)S(1)}, u32[]{:S(2)}, u32[]{:S(2)}) collective-permute-start(bf16[64,128]{1,0:T(8,128)(2,1)S(1)} %get-tuple-element.70), channel_id=1, source_target_pairs={{0,8},{4,12},{8,0},{12,4},{1,9},{5,13},{9,1},{13,5},{2,10},{6,14},... | collective-permute-start | bytes 49160 | tf_op jit(solution)/shard_map/ppermute | solution.py:465
  31.1 3.3 %collective-permute-start.8 = (bf16[64,128]{1,0:T(8,128)(2,1)S(1)}, bf16[64,128]{1,0:T(8,128)(2,1)S(1)}, u32[]{:S(2)}, u32[]{:S(2)}) collective-permute-start(bf16[64,128]{1,0:T(8,128)(2,1)S(1)} %get-tuple-element.71), channel_id=1, source_target_pairs={{0,12},{4,8},{8,4},{12,0},{1,13},{5,9},{9,5},{13,1},{2,14},{6,10},... | collective-permute-start | bytes 49160 | tf_op jit(solution)/shard_map/ppermute | solution.py:465
  42.1 8.7 %collective-permute-start.14 = (bf16[256,1024]{1,0:T(8,128)(2,1)S(1)}, bf16[256,1024]{1,0:T(8,128)(2,1)S(1)}, u32[]{:S(2)}, u32[]{:S(2)}) collective-permute-start(bf16[256,1024]{1,0:T(8,128)(2,1)S(1)} %collective-permute-done.2.refs_10_), channel_id=1, source_target_pairs={{0,4},{4,0},{8,12},{12,8},{1,5},{5,1},{9,13},{13,9},{2,6},{6,2},{1... | collective-permute-start | bytes 1572872 | tf_op jit(solution)/shard_map/ppermute | solution.py:465
  42.1 4.5 %collective-permute-start.11 = (bf16[64,128]{1,0:T(8,128)(2,1)S(1)}, bf16[64,128]{1,0:T(8,128)(2,1)S(1)}, u32[]{:S(2)}, u32[]{:S(2)}) collective-permute-start(bf16[64,128]{1,0:T(8,128)(2,1)S(1)} %unpack.1.refs_4_), channel_id=1, source_target_pairs={{0,1},{1,0},{2,3},{3,2},{4,5},{5,4},{6,7},{7,6},{8,9},{9,8},{10,11... | collective-permute-start | bytes 49160 | tf_op jit(solution)/shard_map/ppermute | solution.py:465
  43.1 4.6 %collective-permute-start.12 = (bf16[64,128]{1,0:T(8,128)(2,1)S(1)}, bf16[64,128]{1,0:T(8,128)(2,1)S(1)}, u32[]{:S(2)}, u32[]{:S(2)}) collective-permute-start(bf16[64,128]{1,0:T(8,128)(2,1)S(1)} %unpack.1.refs_4_), channel_id=1, source_target_pairs={{0,2},{1,3},{2,0},{3,1},{4,6},{5,7},{6,4},{7,5},{8,10},{9,11},{10,... | collective-permute-start | bytes 49160 | tf_op jit(solution)/shard_map/ppermute | solution.py:465
  45.2 5.5 %collective-permute-start.13 = (bf16[64,128]{1,0:T(8,128)(2,1)S(1)}, bf16[64,128]{1,0:T(8,128)(2,1)S(1)}, u32[]{:S(2)}, u32[]{:S(2)}) collective-permute-start(bf16[64,128]{1,0:T(8,128)(2,1)S(1)} %unpack.1.refs_4_), channel_id=1, source_target_pairs={{0,3},{1,2},{2,1},{3,0},{4,7},{5,6},{6,5},{7,4},{8,11},{9,10},{10,... | collective-permute-start | bytes 49160 | tf_op jit(solution)/shard_map/ppermute | solution.py:465
  50.8 1.0 %copy-start = (bf16[128,1024]{1,0:T(8,128)(2,1)S(1)}, bf16[128,1024]{1,0:T(8,128)(2,1)}, u32[]{:S(2)}) copy-start(bf16[128,1024]{1,0:T(8,128)(2,1)} %project.3.refs_0_) | copy-start | bytes 786436

commit v4 on v3

--- a/solution.py
+++ b/solution.py
@@ -27,6 +27,7 @@
 
 def attend_kernel(
     owners,
+    blocks,
     resident,
     capacity,
     block,
@@ -42,8 +43,9 @@
     weight_hbm,
     *rest,
 ):
-    attended_hbm, placing_hbm, marks_hbm, partial_hbm = rest[:4]
-    packed_hbm = rest[4 : 4 + owners]
+    placing_out, marks_out = rest[:2]
+    partials = rest[2 : 2 + blocks]
+    packed = rest[2 + blocks : 2 + blocks + owners]
     (
         queries,
         fresh_k,
@@ -56,15 +58,10 @@
         query_scratch,
         result_scratch,
         attended,
-        placing_out,
-        marks_out,
-        partial,
-        packed,
         small_sem,
         cache_sem,
         weight_sem,
-        out_sem,
-    ) = rest[4 + owners :]
+    ) = rest[2 + blocks + owners :]
     requests, steps, width = queries.shape
     heads = width // HEAD_DIM
     groups = cache_k.shape[2] // HEAD_DIM
@@ -74,7 +71,7 @@
     total_rows = requests * steps
     span = steps * sharing
     chunks = requests // block
-    columns = partial.shape[1]
+    columns = weight.shape[2]
 
     def cache_copies(i):
         part = pl.ds(i * block, block)
@@ -93,12 +90,14 @@
     for i in range(chunks):
         for copy in cache_copies(i):
             copy.start()
-    weight_copy = pltpu.make_async_copy(
-        weight_hbm.at[:, pl.ds(pl.multiple_of(column[0] * columns, LANES), columns)],
-        weight,
-        weight_sem.at[0],
-    )
-    weight_copy.start()
+    weight_copies = []
+    for k in range(blocks - 1, -1, -1):
+        start = pl.multiple_of(jnp.bitwise_xor(column[0], k) * columns, LANES)
+        copy = pltpu.make_async_copy(
+            weight_hbm.at[:, pl.ds(start, columns)], weight.at[k], weight_sem.at[k]
+        )
+        copy.start()
+        weight_copies.append((k, copy))
 
     named = adapters[...]
     owner = lax.div(named, resident)
@@ -128,7 +127,10 @@
     chosen = (
         lax.broadcasted_iota(jnp.int32, (LANES, total_rows), 0) == facts[2:3]
     ).astype(BF16)
-    packed[:, width:] = contract(placing, chosen, 1, 1).astype(BF16)
+    per = capacity * steps
+    carried = contract(placing, chosen, 1, 1).astype(BF16)
+    for k in range(owners):
+        packed[k][:, width:] = carried[k * per : (k + 1) * per]
     adapter_id = lax.broadcasted_iota(jnp.int32, (LANES, total_rows), 0)
     named_here = (adapter_id == facts[0:1] * resident + facts[2:3]).astype(BF16)
     identity = lax.broadcasted_iota(jnp.int32, (total_rows, total_rows), 0) == (
@@ -203,40 +205,18 @@
         attended[:, h * HEAD_DIM : (h + 1) * HEAD_DIM] = result_scratch[
             h * total_rows : (h + 1) * total_rows, :
         ].astype(BF16)
-    attended_copy = pltpu.make_async_copy(attended, attended_hbm, out_sem.at[0])
-    attended_copy.start()
-    placing_copy = pltpu.make_async_copy(placing_out, placing_hbm, out_sem.at[1])
-    placing_copy.start()
-    marks_copy = pltpu.make_async_copy(marks_out, marks_hbm, out_sem.at[2])
-    marks_copy.start()
-    per = capacity * steps
     tile = min(512, width)
     for c in range(0, width, tile):
-        packed[:, c : c + tile] = contract(
-            placing_out[...], attended[:, c : c + tile], 1, 0
-        ).astype(BF16)
-    packed_copies = [
-        pltpu.make_async_copy(
-            packed.at[pl.ds(k * per, per)], packed_hbm[k], out_sem.at[4 + k]
-        )
-        for k in range(owners)
-    ]
-    for copy in packed_copies:
-        copy.start()
-    weight_copy.wait()
+        moved = contract(placing_out[...], attended[:, c : c + tile], 1, 0).astype(BF16)
+        for k in range(owners):
+            packed[k][:, c : c + tile] = moved[k * per : (k + 1) * per]
     tile = min(256, columns)
-    for c in range(0, columns, tile):
-        partial[:, c : c + tile] = contract(
-            attended[...], weight[:, c : c + tile], 1, 0
-        ).astype(BF16)
-    partial_copy = pltpu.make_async_copy(partial, partial_hbm, out_sem.at[3])
-    partial_copy.start()
-    attended_copy.wait()
-    placing_copy.wait()
-    marks_copy.wait()
-    for copy in packed_copies:
+    for k, copy in weight_copies:
         copy.wait()
-    partial_copy.wait()
+        for c in range(0, columns, tile):
+            partials[k][:, c : c + tile] = contract(
+                attended[...], weight[k, :, c : c + tile], 1, 0
+            ).astype(BF16)
 
 
 def attend(
@@ -252,6 +232,7 @@
     adapters,
     owners,
     resident,
+    blocks,
     columns,
 ):
     requests, steps, width = queries.shape
@@ -262,41 +243,35 @@
     total_rows = requests * steps
     per = capacity * steps
     anywhere = pl.BlockSpec(memory_space=pl.ANY)
+    local = pl.BlockSpec(memory_space=pltpu.VMEM)
     return pl.pallas_call(
-        functools.partial(attend_kernel, owners, resident, capacity, block),
+        functools.partial(attend_kernel, owners, blocks, resident, capacity, block),
         grid_spec=pltpu.PrefetchScalarGridSpec(
             num_scalar_prefetch=3,
-            grid=(1,),
-            in_specs=[pl.BlockSpec((1, requests), lambda i, *_: (0, 0))] + [anywhere] * 6,
-            out_specs=[anywhere] * (4 + owners),
+            in_specs=[local] + [anywhere] * 6,
+            out_specs=[local] * (2 + blocks + owners),
             scratch_shapes=[
                 pltpu.VMEM((requests, steps, width), BF16),
                 pltpu.VMEM((requests, steps, kv_width), BF16),
                 pltpu.VMEM((requests, steps, kv_width), BF16),
                 pltpu.VMEM((requests, cache_size, kv_width), BF16),
                 pltpu.VMEM((requests, cache_size, kv_width), BF16),
-                pltpu.VMEM((width, columns), BF16),
+                pltpu.VMEM((blocks, width, columns), BF16),
                 pltpu.VMEM((total_rows, kv_width), BF16),
                 pltpu.VMEM((total_rows, kv_width), BF16),
                 pltpu.VMEM((heads * block * steps, HEAD_DIM), F32),
                 pltpu.VMEM((heads * total_rows, HEAD_DIM), F32),
                 pltpu.VMEM((total_rows, width), BF16),
-                pltpu.VMEM((owners * per, total_rows), BF16),
-                pltpu.VMEM((total_rows, LANES), BF16),
-                pltpu.VMEM((total_rows, columns), BF16),
-                pltpu.VMEM((owners * per, width + LANES), BF16),
                 pltpu.SemaphoreType.DMA((3,)),
                 pltpu.SemaphoreType.DMA((2, requests // block)),
-                pltpu.SemaphoreType.DMA((1,)),
-                pltpu.SemaphoreType.DMA((4 + owners,)),
+                pltpu.SemaphoreType.DMA((blocks,)),
             ],
         ),
         out_shape=[
-            jax.ShapeDtypeStruct((total_rows, width), BF16),
             jax.ShapeDtypeStruct((owners * per, total_rows), BF16),
             jax.ShapeDtypeStruct((total_rows, LANES), BF16),
-            jax.ShapeDtypeStruct((total_rows, columns), BF16),
         ]
+        + [jax.ShapeDtypeStruct((total_rows, columns), BF16)] * blocks
         + [jax.ShapeDtypeStruct((per, width + LANES), BF16)] * owners,
         compiler_params=pltpu.CompilerParams(vmem_limit_bytes=KERNEL_VMEM),
         cost_estimate=SMALL_COST,
@@ -315,66 +290,6 @@
     )
 
 
-def project_kernel(count, *refs):
-    places = refs[:count]
-    attended_hbm, weight_hbm = refs[count : count + 2]
-    outs = refs[count + 2 : 2 * count + 2]
-    attended, weight, results, in_sem, weight_sem, out_sem = refs[2 * count + 2 :]
-    columns = results.shape[2]
-    attended_copy = pltpu.make_async_copy(attended_hbm, attended, in_sem.at[0])
-    attended_copy.start()
-    copies = []
-    for j in range(count):
-        start = pl.multiple_of(places[j][0] * columns, LANES)
-        copy = pltpu.make_async_copy(
-            weight_hbm.at[:, pl.ds(start, columns)], weight.at[j], weight_sem.at[j]
-        )
-        copy.start()
-        copies.append(copy)
-    attended_copy.wait()
-    tile = min(256, columns)
-    writes = []
-    for j in range(count):
-        copies[j].wait()
-        for c in range(0, columns, tile):
-            results[j, :, c : c + tile] = contract(
-                attended[...], weight[j, :, c : c + tile], 1, 0
-            ).astype(BF16)
-        write = pltpu.make_async_copy(results.at[j], outs[j], out_sem.at[j])
-        write.start()
-        writes.append(write)
-    for write in writes:
-        write.wait()
-
-
-def project(attended, weight, places, blocks):
-    rows, depth = attended.shape
-    columns = weight.shape[1] // blocks
-    count = len(places)
-    anywhere = pl.BlockSpec(memory_space=pl.ANY)
-    return pl.pallas_call(
-        functools.partial(project_kernel, count),
-        grid_spec=pltpu.PrefetchScalarGridSpec(
-            num_scalar_prefetch=count,
-            grid=(1,),
-            in_specs=[anywhere] * 2,
-            out_specs=[anywhere] * count,
-            scratch_shapes=[
-                pltpu.VMEM((rows, depth), BF16),
-                pltpu.VMEM((count, depth, columns), BF16),
-                pltpu.VMEM((count, rows, columns), BF16),
-                pltpu.SemaphoreType.DMA((1,)),
-                pltpu.SemaphoreType.DMA((count,)),
-                pltpu.SemaphoreType.DMA((count,)),
-            ],
-        ),
-        out_shape=[jax.ShapeDtypeStruct((rows, columns), BF16)] * count,
-        compiler_params=pltpu.CompilerParams(vmem_limit_bytes=KERNEL_VMEM),
-        cost_estimate=SMALL_COST,
-        name="project",
-    )(*places, attended, weight)
-
-
 def low_kernel(owners, resident, down, *refs):
     packed = refs[:owners]
     outs = refs[owners:]
@@ -423,21 +338,26 @@
     )(placing, *slots)
 
 
-def combine_kernel(blocks, resident, marks, *refs):
-    partials = refs[:blocks]
-    lows = refs[blocks : 2 * blocks]
-    ups = refs[2 * blocks : -1]
+def combine_kernel(sums, pairs, blocks, marks, *refs):
+    partials = refs[:sums]
+    halves = refs[sums : sums + 2 * pairs]
+    refs = refs[:sums] + refs[sums + 2 * pairs :]
+    lows = refs[sums : sums + blocks]
+    ups = refs[sums + blocks : -1]
     out = refs[-1]
-    base = partials[0][...].astype(F32)
     low = lows[0][...].astype(F32)
-    for part in partials[1:]:
-        base = base + part[...].astype(F32)
     for part in lows[1:]:
         low = low + part[...].astype(F32)
     rank = low.shape[1] // 2
     low = low.astype(BF16).astype(F32)
     low = jnp.concatenate([low[:, :rank], low[:, rank:]], axis=0)
     chosen = marks[...].astype(F32)
+    base = partials[0][...].astype(F32)
+    for part in partials[1:]:
+        base = base + part[...].astype(F32)
+    for j in range(pairs):
+        both = jnp.concatenate([halves[2 * j][...], halves[2 * j + 1][...]], axis=0)
+        base = base + both.astype(F32)
     first = 0
     for up in ups:
         held = up.shape[0] // rank
@@ -449,15 +369,19 @@
     out[...] = base.reshape(out.shape).astype(BF16)
 
 
-def combine(marks, partials, lows, ups, resident, steps):
-    rows, columns = partials[0].shape
+def combine(marks, own, partials, halves, lows, ups, steps):
+    rows, columns = own.shape
+    split = [part for pair in halves for part in pair]
+    inputs = [marks, own, *partials, *split, *lows, *ups]
     return pl.pallas_call(
-        functools.partial(combine_kernel, len(partials), resident),
+        functools.partial(
+            combine_kernel, 1 + len(partials), len(halves), len(lows)
+        ),
         out_shape=jax.ShapeDtypeStruct((rows // steps, steps, columns), BF16),
         compiler_params=pltpu.CompilerParams(vmem_limit_bytes=SMALL_VMEM),
         cost_estimate=SMALL_COST,
         name="combine",
-    )(marks, *partials, *lows, *ups)
+    )(*inputs)
 
 
 def swap(value, axis, k):
@@ -490,8 +414,7 @@
     blocks = lax.axis_size("tensor")
     resident, rank, columns = adapter_up_weight.shape
     place = lax.axis_index("adapter").reshape(1)
-    mine = lax.axis_index("tensor")
-    columns_of = lambda k: jnp.bitwise_xor(mine, k).reshape(1)
+    mine = lax.axis_index("tensor").reshape(1)
 
     up_rows = adapter_up_weight.reshape(resident * rank, columns)
     top_bit = owners // 2
@@ -499,8 +422,7 @@
     ups[top_bit] = swap(up_rows, "adapter", top_bit)
     ups[1] = swap(up_rows, "adapter", 1)
 
-    far = blocks - 1
-    attended, placing, marks, first_partial, *packed = attend(
+    placing, marks, *made = attend(
         queries,
         token_key_rows,
         token_value_rows,
@@ -509,41 +431,45 @@
         output_weight_matrix,
         cache_length,
         place,
-        columns_of(far),
+        mine,
         request_adapter,
         owners,
         resident,
+        blocks,
         columns,
     )
-    ups[1], attended, first_partial, packed = lax.optimization_barrier(
-        (ups[1], attended, first_partial, packed)
-    )
+    ups[1], made = lax.optimization_barrier((ups[1], made))
+    partials, packed = made[:blocks], made[blocks:]
+    inward = {k: swap(partials[k], "tensor", 1) for k in range(blocks - 1, 1, -2)}
     arrived = [packed[0]] + [None] * (owners - 1)
     for k in range(owners - 1, 0, -1):
         arrived[k] = swap(packed[k], "adapter", k)
-    partials = {far: swap(first_partial, "tensor", far)}
-    others = list(range(far - 1, 0, -1))
-    made = project(attended, output_weight_matrix, [columns_of(k) for k in others], blocks)
-    made, arrived[1], ups[top_bit] = lax.optimization_barrier(
-        (made, arrived[1], ups[top_bit])
-    )
-    for k, part in zip(others, made):
-        partials[k] = swap(part, "tensor", k)
-    (own,) = project(attended, output_weight_matrix, [mine.reshape(1)], blocks)
-    arrived, partials[far], own = lax.optimization_barrier((arrived, partials[far], own))
+    partials, inward, arrived[1], ups[top_bit] = lax.optimization_barrier(
+        (partials, inward, arrived[1], ups[top_bit])
+    )
+    near = swap(partials[1], "tensor", 1)
+    half = requests * steps // 2
+    top, bottom = [], []
+    for k in range(2, blocks, 2):
+        pair = partials[k].astype(F32) + inward[k + 1].astype(F32)
+        pair = pair.astype(BF16)
+        top.append(swap(pair[:half], "tensor", k))
+        bottom.append(swap(pair[half:], "tensor", k))
+    arrived, near, top = lax.optimization_barrier((arrived, near, top))
+    forward(ups, "adapter", top_bit // 2)
     lows = low_partial(arrived, adapter_down_weight)
+
     returned = [lows[0]] + [swap(lows[k], "adapter", k) for k in range(1, owners)]
-    returned, partials = lax.optimization_barrier((returned, partials))
+    returned, bottom = lax.optimization_barrier((returned, bottom))
     low = unpack(placing, returned)
-    ups, low = lax.optimization_barrier((ups, low))
     low_parts = [low] + [swap(low, "tensor", k) for k in range(1, blocks)]
-    forward(ups, "adapter", top_bit // 2)
     return combine(
         marks,
-        [own] + [partials[k] for k in range(1, blocks)],
+        partials[0],
+        [near],
+        [*zip(top, bottom)],
         low_parts,
         [ups[k] for k in range(owners)],
-        resident,
         steps,
     )
 

time: 53.6 us -> 63.9 us (1.19)
  waiting for transfers between devices: 14 us -> 19.4 us
  starting transfers between devices: 15.8 us -> 20.1 us
  Pallas kernels: 22.6 us -> 19.4 us
  local copies, waits for them, and re-layouts: 0.96 us -> 3.53 us
  other arithmetic: 0 us -> 1.02 us
    ppermute x15 -> x16, waiting for transfers between devices: 14 us -> 19.4 us  [swap(): return lax.ppermute(value, axis, [(i, i ^ k) for i in range(count)])]
    ppermute x15 -> x16, starting transfers between devices: 15.8 us -> 20.1 us  [swap(): return lax.ppermute(value, axis, [(i, i ^ k) for i in range(count)])]
    pallas_call x4 -> x2, Pallas kernels: 20.9 us -> 17.7 us  [the longest x1 16 us: attend(): pl.pallas_call(functools.partial(attend_kernel, owners, blocks, resident,...]
    unnamed x12, local copies, waits for them, and re-layouts: 0.96 us -> 3.51 us
    convert_element_type x0 -> x1, other arithmetic: none -> 1.02 us  [body(): pair = pair.astype(BF16)]
  transfers between devices with their start and end apart: 15 -> 16, of which waited for: 5 -> 7; matrix products, arithmetic and copies ran while one was open for 0% -> 2% of each run, Pallas kernels for 39% -> 28%
where the time goes in v4:
time: 63.9 us; the launch traced here: 63.6 us
  starting transfers between devices  20.1 us (31%)
  Pallas kernels  19.4 us (30%)
  waiting for transfers between devices  19.4 us (30%)
  local copies, waits for them, and re-layouts  3.53 us (6%)
  other arithmetic  1.02 us (2%)
    ppermute x16, starting transfers between devices, swap(): return lax.ppermute(value, axis, [(i, i ^ k) for i in range(count)])  20.1 us
    ppermute x16, waiting for transfers between devices, swap(): return lax.ppermute(value, axis, [(i, i ^ k) for i in range(count)])  19.4 us
    pallas_call x1, Pallas kernels, attend(): pl.pallas_call(functools.partial(attend_kernel, owners, blocks, resident,...  16 us
    unnamed x12, local copies, waits for them, and re-layouts  3.51 us
    pallas_call x1, Pallas kernels, combine(): pl.pallas_call(functools.partial(combine_kernel, 1 + len(partials), len(h...  1.71 us
    pallas_call x1, Pallas kernels, low_partial(): pl.pallas_call(functools.partial(low_kernel, owners, resident), out_shape...  1.46 us
  transfers between devices with their start and end apart: 16, of which 7 were waited for; matrix products, arithmetic and copies ran while one was open for 2% of the time, Pallas kernels for 28%

profile of v4, /device:TPU:0, one launch (start us, length us, event | category | flops | bytes accessed | tf_op | source)
XLA Modules:
  0.0 63.6 jit_solution(8671571965542681421)
XLA Ops:
  0.5 2.5 %collective-permute-start.3 = (bf16[256,1024]{1,0:T(8,128)(2,1)}, bf16[256,1024]{1,0:T(8,128)(2,1)S(1)}, u32[]{:S(2)}, u32[]{:S(2)}) collective-permute-start(bf16[256,1024]{1,0:T(8,128)(2,1)} %bitcast.7), channel_id=1, source_target_pairs={{0,8},{4,12},{8,0},{12,4},{1,9},{5,13},{9,1},{13,5},{2,10},{6,14},... | collective-permute-start | bytes 1572872 | tf_op jit(solution)/shard_map/ppermute | solution.py:389
  2.9 16.0 %attend.1 = (bf16[256,128]{1,0:T(8,128)(2,1)}, bf16[128,128]{1,0:T(8,128)(2,1)}, bf16[128,1024]{1,0:T(8,128)(2,1)}, bf16[128,1024]{1,0:T(8,128)(2,1)}, bf16[128,...) custom-call(s32[64]{0:T(128)} %lengths.1, ...), custom_call_target="tpu_custom_call" | custom-call | flops 1024 | bytes 1024 | tf_op jit(solution)/shard_map/attend/pallas_call | solution.py:247
  19.3 1.6 %collective-permute-start.1 = (bf16[128,1024]{1,0:T(8,128)(2,1)}, bf16[128,1024]{1,0:T(8,128)(2,1)S(1)}, u32[]{:S(2)}, u32[]{:S(2)}) collective-permute-start(bf16[128,1024]{1,0:T(8,128)(2,1)} %get-tuple-element.57), channel_id=1, source_target_pairs={{0,1},{1,0},{2,3},{3,2},{4,5},{5,4},{6,7},{7,6},{8,9},{9,8},{10,11... | collective-permute-start | bytes 786440 | tf_op jit(solution)/shard_map/ppermute | solution.py:389
  20.8 0.5 collective-permute-start.4
  21.4 0.8 %collective-permute-start.5 = (bf16[64,2176]{1,0:T(8,128)(2,1)}, bf16[64,2176]{1,0:T(8,128)(2,1)S(1)}, u32[]{:S(2)}, u32[]{:S(2)}) collective-permute-start(bf16[64,2176]{1,0:T(8,128)(2,1)} %get-tuple-element.63), channel_id=1, source_target_pairs={{0,12},{4,8},{8,4},{12,0},{1,13},{5,9},{9,5},{13,1},{2,14},{6,10},... | collective-permute-start | bytes 835592 | tf_op jit(solution)/shard_map/ppermute | solution.py:389
  22.2 5.8 %collective-permute-done.1 = bf16[128,1024]{1,0:T(8,128)(2,1)S(1)} collective-permute-done((bf16[128,1024]{1,0:T(8,128)(2,1)}, bf16[128,1024]{1,0:T(8,128)(2,1)S(1)}, u32[]{:S(2)}, u32[]{:S(2)}) %collective-permute-start.1) | collective-permute-done | bytes 262176 | tf_op jit(solution)/shard_map/ppermute | solution.py:389
  28.0 1.6 %collective-permute-start.6 = (bf16[128,1024]{1,0:T(8,128)(2,1)}, bf16[128,1024]{1,0:T(8,128)(2,1)S(1)}, u32[]{:S(2)}, u32[]{:S(2)}) collective-permute-start(bf16[128,1024]{1,0:T(8,128)(2,1)} %get-tuple-element.64), channel_id=1, source_target_pairs={{0,1},{1,0},{2,3},{3,2},{4,5},{5,4},{6,7},{7,6},{8,9},{9,8},{10,11... | collective-permute-start | bytes 786440 | tf_op jit(solution)/shard_map/ppermute | solution.py:389
  29.6 1.0 %add_convert_fusion = bf16[128,1024]{1,0:T(8,128)(2,1)S(1)} fusion(bf16[128,1024]{1,0:T(8,128)(2,1)S(1)} %collective-permute-done.1, bf16[128,1024]{1,0:T(8,128)(2,1)} %get-tuple-element.65), kind=kLoop, calls=%fused_computation | loop fusion | flops 524288 | bytes 786432 | tf_op jit(solution)/shard_map/convert_element_type | solution.py:455
  30.6 2.7 %collective-permute-start.7 = (bf16[64,1024]{1,0:T(8,128)(2,1)S(1)}, bf16[64,1024]{1,0:T(8,128)(2,1)S(1)}, u32[]{:S(2)}, u32[]{:S(2)}) collective-permute-start(bf16[64,1024]{1,0:T(8,128)(2,1)S(1)} %get-tuple-element.86), channel_id=1, source_target_pairs={{0,2},{1,3},{2,0},{3,1},{4,6},{5,7},{6,4},{7,5},{8,10},{9,11},{10,... | collective-permute-start | bytes 393224 | tf_op jit(solution)/shard_map/ppermute | solution.py:389
  33.6 1.0 %collective-permute-done.5.refs_3_ = bf16[64,2176]{1,0:T(8,128)(2,1)S(1)} collective-permute-done((bf16[64,2176]{1,0:T(8,128)(2,1)}, bf16[64,2176]{1,0:T(8,128)(2,1)S(1)}, u32[]{:S(2)}, u32[]{:S(2)}) %collective-permute-start.5) | collective-permute-done | bytes 278560 | tf_op jit(solution)/shard_map/ppermute | solution.py:389
  34.6 4.8 %collective-permute-done.7.refs_2_ = bf16[64,1024]{1,0:T(8,128)(2,1)S(1)} collective-permute-done((bf16[64,1024]{1,0:T(8,128)(2,1)S(1)}, bf16[64,1024]{1,0:T(8,128)(2,1)S(1)}, u32[]{:S(2)}, u32[]{:S(2)}) %collective-permute-start.7) | collective-permute-done | bytes 131104 | tf_op jit(solution)/shard_map/ppermute | solution.py:389
  39.4 1.0 %copy-done.2 = bf16[64,2176]{1,0:T(8,128)(2,1)S(1)} copy-done((bf16[64,2176]{1,0:T(8,128)(2,1)S(1)}, bf16[64,2176]{1,0:T(8,128)(2,1)}, u32[]{:S(2)}) %copy-start.2) | copy-done | bytes 278552
  40.4 1.5 %low.1 = (bf16[64,128]{1,0:T(8,128)(2,1)S(1)}, bf16[64,128]{1,0:T(8,128)(2,1)S(1)}, bf16[64,128]{1,0:T(8,128)(2,1)S(1)}, bf16[64,128]{1,0:T(8,128)(2,1)S(1)}) custom-call(bf16[256,2048]{1,0:T(8,128)(2,1)S(1)} %bitcast.5, bf16[64,2176]{1,0:T(8,128)(2,1)S(1)} %copy-done.2, bf16[64,2176]{1,0:T(8,128)(2,1)S(1)} %collective-permute-done.2.refs_1_, ...), custom_call_target="tpu_custom_call" | custom-call | flops 1024 | bytes 1024 | tf_op jit(solution)/shard_map/low/pallas_call | solution.py:312
  41.9 0.7 %collective-permute-start.8 = (bf16[64,128]{1,0:T(8,128)(2,1)S(1)}, bf16[64,128]{1,0:T(8,128)(2,1)S(1)}, u32[]{:S(2)}, u32[]{:S(2)}) collective-permute-start(bf16[64,128]{1,0:T(8,128)(2,1)S(1)} %get-tuple-element.74), channel_id=1, source_target_pairs={{0,4},{4,0},{8,12},{12,8},{1,5},{5,1},{9,13},{13,9},{2,6},{6,2},{1... | collective-permute-start | bytes 49160 | tf_op jit(solution)/shard_map/ppermute | solution.py:389
  42.6 1.4 %collective-permute-start.9 = (bf16[64,128]{1,0:T(8,128)(2,1)S(1)}, bf16[64,128]{1,0:T(8,128)(2,1)S(1)}, u32[]{:S(2)}, u32[]{:S(2)}) collective-permute-start(bf16[64,128]{1,0:T(8,128)(2,1)S(1)} %get-tuple-element.75), channel_id=1, source_target_pairs={{0,8},{4,12},{8,0},{12,4},{1,9},{5,13},{9,1},{13,5},{2,10},{6,14},... | collective-permute-start | bytes 49160 | tf_op jit(solution)/shard_map/ppermute | solution.py:389
  44.1 1.9 %collective-permute-done.11.refs_3_ = bf16[64,1024]{1,0:T(8,128)(2,1)S(1)} collective-permute-done((bf16[64,1024]{1,0:T(8,128)(2,1)S(1)}, bf16[64,1024]{1,0:T(8,128)(2,1)S(1)}, u32[]{:S(2)}, u32[]{:S(2)}) %collective-permute-start.11) | collective-permute-done | bytes 131104 | tf_op jit(solution)/shard_map/ppermute | solution.py:389
  46.4 0.8 %copy-done.4 = bf16[256,128]{1,0:T(8,128)(2,1)S(1)} copy-done((bf16[256,128]{1,0:T(8,128)(2,1)S(1)}, bf16[256,128]{1,0:T(8,128)(2,1)}, u32[]{:S(2)}) %copy-start.4) | copy-done | bytes 65560
  47.5 3.8 %collective-permute-start.12 = (bf16[64,128]{1,0:T(8,128)(2,1)S(1)}, bf16[64,128]{1,0:T(8,128)(2,1)S(1)}, u32[]{:S(2)}, u32[]{:S(2)}) collective-permute-start(bf16[64,128]{1,0:T(8,128)(2,1)S(1)} %unpack.1.refs_4_), channel_id=1, source_target_pairs={{0,1},{1,0},{2,3},{3,2},{4,5},{5,4},{6,7},{7,6},{8,9},{9,8},{10,11... | collective-permute-start | bytes 49160 | tf_op jit(solution)/shard_map/ppermute | solution.py:389
  51.3 3.4 %collective-permute-start.13 = (bf16[64,128]{1,0:T(8,128)(2,1)S(1)}, bf16[64,128]{1,0:T(8,128)(2,1)S(1)}, u32[]{:S(2)}, u32[]{:S(2)}) collective-permute-start(bf16[64,128]{1,0:T(8,128)(2,1)S(1)} %unpack.1.refs_4_), channel_id=1, source_target_pairs={{0,2},{1,3},{2,0},{3,1},{4,6},{5,7},{6,4},{7,5},{8,10},{9,11},{10,... | collective-permute-start | bytes 49160 | tf_op jit(solution)/shard_map/ppermute | solution.py:389
  54.7 1.7 %collective-permute-done.13.refs_6_ = bf16[64,128]{1,0:T(8,128)(2,1)S(1)} collective-permute-done((bf16[64,128]{1,0:T(8,128)(2,1)S(1)}, bf16[64,128]{1,0:T(8,128)(2,1)S(1)}, u32[]{:S(2)}, u32[]{:S(2)}) %collective-permute-start.13) | collective-permute-done | bytes 16416 | tf_op jit(solution)/shard_map/ppermute | solution.py:389
  56.4 3.8 %collective-permute-done.14.refs_7_ = bf16[64,128]{1,0:T(8,128)(2,1)S(1)} collective-permute-done((bf16[64,128]{1,0:T(8,128)(2,1)S(1)}, bf16[64,128]{1,0:T(8,128)(2,1)S(1)}, u32[]{:S(2)}, u32[]{:S(2)}) %collective-permute-start.14) | collective-permute-done | bytes 16416 | tf_op jit(solution)/shard_map/ppermute | solution.py:389
  60.2 0.9 %copy-done.3 = bf16[128,1024]{1,0:T(8,128)(2,1)S(1)} copy-done((bf16[128,1024]{1,0:T(8,128)(2,1)S(1)}, bf16[128,1024]{1,0:T(8,128)(2,1)}, u32[]{:S(2)}) %copy-start.3) | copy-done | bytes 262168
  61.1 0.8 %copy-done.5 = bf16[128,128]{1,0:T(8,128)(2,1)S(1)} copy-done((bf16[128,128]{1,0:T(8,128)(2,1)S(1)}, bf16[128,128]{1,0:T(8,128)(2,1)}, u32[]{:S(2)}) %copy-start.5) | copy-done | bytes 32792
  61.9 1.7 %combine.1 = bf16[64,2,1024]{2,1,0:T(2,128)(2,1)} custom-call(bf16[128,128]{1,0:T(8,128)(2,1)S(1)} %copy-done.5, bf16[128,1024]{1,0:T(8,128)(2,1)S(1)} %copy-done.3, bf16[128,1024]{1,0:T(8,128)(2,1)S(1)} %collective-permute-done.6.refs_1_, bf16[64,1024]{1,0:T(8,128)(2,1)S(1)} %collective-permute-done.7.refs_2_, ...), custom_call_target="tpu_custom_call" | custom-call | flops 1024 | bytes 1024 | tf_op jit(solution)/shard_map/combine/pallas_call | solution.py:376
  (26 shorter events, 1.9 us)
Async XLA Ops:
  0.0 19.0 %collective-permute-start = (bf16[256,1024]{1,0:T(8,128)(2,1)}, bf16[256,1024]{1,0:T(8,128)(2,1)S(1)}, u32[]{:S(2)}, u32[]{:S(2)}) collective-permute-start(bf16[256,1024]{1,0:T(8,128)(2,1)} %bitcast.6), channel_id=1, source_target_pairs={{0,4},{4,0},{8,12},{12,8},{1,5},{5,1},{9,13},{13,9},{2,6},{6,2},{1... | collective-permute-start | bytes 1572872 | tf_op jit(solution)/shard_map/ppermute | solution.py:389
  0.5 21.8 %collective-permute-start.3 = (bf16[256,1024]{1,0:T(8,128)(2,1)}, bf16[256,1024]{1,0:T(8,128)(2,1)S(1)}, u32[]{:S(2)}, u32[]{:S(2)}) collective-permute-start(bf16[256,1024]{1,0:T(8,128)(2,1)} %bitcast.7), channel_id=1, source_target_pairs={{0,8},{4,12},{8,0},{12,4},{1,9},{5,13},{9,1},{13,5},{2,10},{6,14},... | collective-permute-start | bytes 1572872 | tf_op jit(solution)/shard_map/ppermute | solution.py:389
  2.9 36.5 %copy-start = (bf16[4,64,2048]{2,1,0:T(8,128)(2,1)S(1)}, bf16[4,64,2048]{2,1,0:T(8,128)(2,1)}, u32[]{:S(2)}) copy-start(bf16[4,64,2048]{2,1,0:T(8,128)(2,1)} %param.18) | copy-start | bytes 3145732
  2.9 57.2 %copy-start.1 = (bf16[4,64,1024]{2,1,0:T(8,128)(2,1)S(1)}, bf16[4,64,1024]{2,1,0:T(8,128)(2,1)}, u32[]{:S(2)}) copy-start(bf16[4,64,1024]{2,1,0:T(8,128)(2,1)} %param.19) | copy-start | bytes 1572868
  19.0 9.0 %collective-permute-start.2 = (bf16[64,2176]{1,0:T(8,128)(2,1)}, bf16[64,2176]{1,0:T(8,128)(2,1)S(1)}, u32[]{:S(2)}, u32[]{:S(2)}) collective-permute-start(bf16[64,2176]{1,0:T(8,128)(2,1)} %get-tuple-element.58), channel_id=1, source_target_pairs={{0,4},{4,0},{8,12},{12,8},{1,5},{5,1},{9,13},{13,9},{2,6},{6,2},{1... | collective-permute-start | bytes 835592 | tf_op jit(solution)/shard_map/ppermute | solution.py:389
  19.3 8.7 %collective-permute-start.1 = (bf16[128,1024]{1,0:T(8,128)(2,1)}, bf16[128,1024]{1,0:T(8,128)(2,1)S(1)}, u32[]{:S(2)}, u32[]{:S(2)}) collective-permute-start(bf16[128,1024]{1,0:T(8,128)(2,1)} %get-tuple-element.57), channel_id=1, source_target_pairs={{0,1},{1,0},{2,3},{3,2},{4,5},{5,4},{6,7},{7,6},{8,9},{9,8},{10,11... | collective-permute-start | bytes 786440 | tf_op jit(solution)/shard_map/ppermute | solution.py:389
  20.8 12.4 %collective-permute-start.4 = (bf16[64,2176]{1,0:T(8,128)(2,1)}, bf16[64,2176]{1,0:T(8,128)(2,1)S(1)}, u32[]{:S(2)}, u32[]{:S(2)}) collective-permute-start(bf16[64,2176]{1,0:T(8,128)(2,1)} %get-tuple-element.62), channel_id=1, source_target_pairs={{0,8},{4,12},{8,0},{12,4},{1,9},{5,13},{9,1},{13,5},{2,10},{6,14},... | collective-permute-start | bytes 835592 | tf_op jit(solution)/shard_map/ppermute | solution.py:389
  21.4 13.3 %collective-permute-start.5 = (bf16[64,2176]{1,0:T(8,128)(2,1)}, bf16[64,2176]{1,0:T(8,128)(2,1)S(1)}, u32[]{:S(2)}, u32[]{:S(2)}) collective-permute-start(bf16[64,2176]{1,0:T(8,128)(2,1)} %get-tuple-element.63), channel_id=1, source_target_pairs={{0,12},{4,8},{8,4},{12,0},{1,13},{5,9},{9,5},{13,1},{2,14},{6,10},... | collective-permute-start | bytes 835592 | tf_op jit(solution)/shard_map/ppermute | solution.py:389
  28.0 11.4 %collective-permute-start.6 = (bf16[128,1024]{1,0:T(8,128)(2,1)}, bf16[128,1024]{1,0:T(8,128)(2,1)S(1)}, u32[]{:S(2)}, u32[]{:S(2)}) collective-permute-start(bf16[128,1024]{1,0:T(8,128)(2,1)} %get-tuple-element.64), channel_id=1, source_target_pairs={{0,1},{1,0},{2,3},{3,2},{4,5},{5,4},{6,7},{7,6},{8,9},{9,8},{10,11... | collective-permute-start | bytes 786440 | tf_op jit(solution)/shard_map/ppermute | solution.py:389
  29.6 30.6 %collective-permute-start.15 = (bf16[256,1024]{1,0:T(8,128)(2,1)S(1)}, bf16[256,1024]{1,0:T(8,128)(2,1)S(1)}, u32[]{:S(2)}, u32[]{:S(2)}) collective-permute-start(bf16[256,1024]{1,0:T(8,128)(2,1)S(1)} %collective-permute-done.3.refs_10_), channel_id=1, source_target_pairs={{0,4},{4,0},{8,12},{12,8},{1,5},{5,1},{9,13},{13,9},{2,6},{6,2},{1... | collective-permute-start | bytes 1572872 | tf_op jit(solution)/shard_map/ppermute | solution.py:389
  30.6 8.8 %collective-permute-start.7 = (bf16[64,1024]{1,0:T(8,128)(2,1)S(1)}, bf16[64,1024]{1,0:T(8,128)(2,1)S(1)}, u32[]{:S(2)}, u32[]{:S(2)}) collective-permute-start(bf16[64,1024]{1,0:T(8,128)(2,1)S(1)} %get-tuple-element.86), channel_id=1, source_target_pairs={{0,2},{1,3},{2,0},{3,1},{4,6},{5,7},{6,4},{7,5},{8,10},{9,11},{10,... | collective-permute-start | bytes 393224 | tf_op jit(solution)/shard_map/ppermute | solution.py:389
  33.3 12.7 %collective-permute-start.11 = (bf16[64,1024]{1,0:T(8,128)(2,1)S(1)}, bf16[64,1024]{1,0:T(8,128)(2,1)S(1)}, u32[]{:S(2)}, u32[]{:S(2)}) collective-permute-start(bf16[64,1024]{1,0:T(8,128)(2,1)S(1)} %get-tuple-element.85), channel_id=1, source_target_pairs={{0,2},{1,3},{2,0},{3,1},{4,6},{5,7},{6,4},{7,5},{8,10},{9,11},{10,... | collective-permute-start | bytes 393224 | tf_op jit(solution)/shard_map/ppermute | solution.py:389
  39.4 1.0 %copy-start.2 = (bf16[64,2176]{1,0:T(8,128)(2,1)S(1)}, bf16[64,2176]{1,0:T(8,128)(2,1)}, u32[]{:S(2)}) copy-start(bf16[64,2176]{1,0:T(8,128)(2,1)} %get-tuple-element.69.refs_0_) | copy-start | bytes 835588
  41.9 4.1 %collective-permute-start.10 = (bf16[64,128]{1,0:T(8,128)(2,1)S(1)}, bf16[64,128]{1,0:T(8,128)(2,1)S(1)}, u32[]{:S(2)}, u32[]{:S(2)}) collective-permute-start(bf16[64,128]{1,0:T(8,128)(2,1)S(1)} %get-tuple-element.76), channel_id=1, source_target_pairs={{0,12},{4,8},{8,4},{12,0},{1,13},{5,9},{9,5},{13,1},{2,14},{6,10},... | collective-permute-start | bytes 49160 | tf_op jit(solution)/shard_map/ppermute | solution.py:389
  41.9 4.0 %collective-permute-start.8 = (bf16[64,128]{1,0:T(8,128)(2,1)S(1)}, bf16[64,128]{1,0:T(8,128)(2,1)S(1)}, u32[]{:S(2)}, u32[]{:S(2)}) collective-permute-start(bf16[64,128]{1,0:T(8,128)(2,1)S(1)} %get-tuple-element.74), channel_id=1, source_target_pairs={{0,4},{4,0},{8,12},{12,8},{1,5},{5,1},{9,13},{13,9},{2,6},{6,2},{1... | collective-permute-start | bytes 49160 | tf_op jit(solution)/shard_map/ppermute | solution.py:389
  42.6 3.7 %collective-permute-start.9 = (bf16[64,128]{1,0:T(8,128)(2,1)S(1)}, bf16[64,128]{1,0:T(8,128)(2,1)S(1)}, u32[]{:S(2)}, u32[]{:S(2)}) collective-permute-start(bf16[64,128]{1,0:T(8,128)(2,1)S(1)} %get-tuple-element.75), channel_id=1, source_target_pairs={{0,8},{4,12},{8,0},{12,4},{1,9},{5,13},{9,1},{13,5},{2,10},{6,14},... | collective-permute-start | bytes 49160 | tf_op jit(solution)/shard_map/ppermute | solution.py:389
  46.4 0.8 %copy-start.4 = (bf16[256,128]{1,0:T(8,128)(2,1)S(1)}, bf16[256,128]{1,0:T(8,128)(2,1)}, u32[]{:S(2)}) copy-start(bf16[256,128]{1,0:T(8,128)(2,1)} %get-tuple-element.78.placing) | copy-start | bytes 196612
  47.5 7.2 %collective-permute-start.12 = (bf16[64,128]{1,0:T(8,128)(2,1)S(1)}, bf16[64,128]{1,0:T(8,128)(2,1)S(1)}, u32[]{:S(2)}, u32[]{:S(2)}) collective-permute-start(bf16[64,128]{1,0:T(8,128)(2,1)S(1)} %unpack.1.refs_4_), channel_id=1, source_target_pairs={{0,1},{1,0},{2,3},{3,2},{4,5},{5,4},{6,7},{7,6},{8,9},{9,8},{10,11... | collective-permute-start | bytes 49160 | tf_op jit(solution)/shard_map/ppermute | solution.py:389
  51.3 5.1 %collective-permute-start.13 = (bf16[64,128]{1,0:T(8,128)(2,1)S(1)}, bf16[64,128]{1,0:T(8,128)(2,1)S(1)}, u32[]{:S(2)}, u32[]{:S(2)}) collective-permute-start(bf16[64,128]{1,0:T(8,128)(2,1)S(1)} %unpack.1.refs_4_), channel_id=1, source_target_pairs={{0,2},{1,3},{2,0},{3,1},{4,6},{5,7},{6,4},{7,5},{8,10},{9,11},{10,... | collective-permute-start | bytes 49160 | tf_op jit(solution)/shard_map/ppermute | solution.py:389
  54.6 5.5 %collective-permute-start.14 = (bf16[64,128]{1,0:T(8,128)(2,1)S(1)}, bf16[64,128]{1,0:T(8,128)(2,1)S(1)}, u32[]{:S(2)}, u32[]{:S(2)}) collective-permute-start(bf16[64,128]{1,0:T(8,128)(2,1)S(1)} %unpack.1.refs_4_), channel_id=1, source_target_pairs={{0,3},{1,2},{2,1},{3,0},{4,7},{5,6},{6,5},{7,4},{8,11},{9,10},{10,... | collective-permute-start | bytes 49160 | tf_op jit(solution)/shard_map/ppermute | solution.py:389
  60.2 1.0 %copy-start.3 = (bf16[128,1024]{1,0:T(8,128)(2,1)S(1)}, bf16[128,1024]{1,0:T(8,128)(2,1)}, u32[]{:S(2)}) copy-start(bf16[128,1024]{1,0:T(8,128)(2,1)} %get-tuple-element.59.refs_0_) | copy-start | bytes 786436
  61.1 0.8 %copy-start.5 = (bf16[128,128]{1,0:T(8,128)(2,1)S(1)}, bf16[128,128]{1,0:T(8,128)(2,1)}, u32[]{:S(2)}) copy-start(bf16[128,128]{1,0:T(8,128)(2,1)} %get-tuple-element.45.marks) | copy-start | bytes 98308

commit v5 on v4

--- a/solution.py
+++ b/solution.py
@@ -9,6 +9,7 @@
 from jax.sharding import PartitionSpec as P
 
 HEAD_DIM = 128
+AHEAD = 4
 NEGATIVE = -1e30
 LANES = 128
 KERNEL_VMEM = 56 * 1024 * 1024
@@ -27,7 +28,7 @@
 
 def attend_kernel(
     owners,
-    blocks,
+    made,
     resident,
     capacity,
     block,
@@ -43,9 +44,8 @@
     weight_hbm,
     *rest,
 ):
-    placing_out, marks_out = rest[:2]
-    partials = rest[2 : 2 + blocks]
-    packed = rest[2 + blocks : 2 + blocks + owners]
+    attended, placing_out, marks_out, partial = rest[:4]
+    packed = rest[4 : 4 + owners]
     (
         queries,
         fresh_k,
@@ -57,11 +57,10 @@
         new_v,
         query_scratch,
         result_scratch,
-        attended,
         small_sem,
         cache_sem,
         weight_sem,
-    ) = rest[2 + blocks + owners :]
+    ) = rest[4 + owners :]
     requests, steps, width = queries.shape
     heads = width // HEAD_DIM
     groups = cache_k.shape[2] // HEAD_DIM
@@ -71,7 +70,7 @@
     total_rows = requests * steps
     span = steps * sharing
     chunks = requests // block
-    columns = weight.shape[2]
+    columns = weight.shape[1]
 
     def cache_copies(i):
         part = pl.ds(i * block, block)
@@ -85,19 +84,12 @@
         pltpu.make_async_copy(fresh_k_hbm, fresh_k, small_sem.at[1]),
         pltpu.make_async_copy(fresh_v_hbm, fresh_v, small_sem.at[2]),
     ]
-    for copy in small:
+    start = pl.multiple_of(jnp.bitwise_xor(column[0], made) * columns, LANES)
+    weight_copy = pltpu.make_async_copy(
+        weight_hbm.at[:, pl.ds(start, columns)], weight, weight_sem.at[0]
+    )
+    for copy in (*small, *cache_copies(0)):
         copy.start()
-    for i in range(chunks):
-        for copy in cache_copies(i):
-            copy.start()
-    weight_copies = []
-    for k in range(blocks - 1, -1, -1):
-        start = pl.multiple_of(jnp.bitwise_xor(column[0], k) * columns, LANES)
-        copy = pltpu.make_async_copy(
-            weight_hbm.at[:, pl.ds(start, columns)], weight.at[k], weight_sem.at[k]
-        )
-        copy.start()
-        weight_copies.append((k, copy))
 
     named = adapters[...]
     owner = lax.div(named, resident)
@@ -147,6 +139,9 @@
     scaling = math.log2(math.e) / math.sqrt(HEAD_DIM)
     for copy in small:
         copy.wait()
+    for i in range(1, min(AHEAD, chunks)):
+        for copy in cache_copies(i):
+            copy.start()
     new_k[...] = fresh_k[...].reshape(total_rows, groups * HEAD_DIM)
     new_v[...] = fresh_v[...].reshape(total_rows, groups * HEAD_DIM)
 
@@ -160,6 +155,16 @@
             ]
         for copy in cache_copies(i):
             copy.wait()
+
+        @pl.when(i + AHEAD < chunks)
+        def _():
+            for copy in cache_copies(i + AHEAD):
+                copy.start()
+
+        @pl.when(i == min(1, chunks - 1))
+        def _():
+            weight_copy.start()
+
         live_fresh = distance == -base
         empty = jnp.zeros((span, HEAD_DIM), BF16)
         wide = []
@@ -210,13 +215,12 @@
         moved = contract(placing_out[...], attended[:, c : c + tile], 1, 0).astype(BF16)
         for k in range(owners):
             packed[k][:, c : c + tile] = moved[k * per : (k + 1) * per]
+    weight_copy.wait()
     tile = min(256, columns)
-    for k, copy in weight_copies:
-        copy.wait()
-        for c in range(0, columns, tile):
-            partials[k][:, c : c + tile] = contract(
-                attended[...], weight[k, :, c : c + tile], 1, 0
-            ).astype(BF16)
+    for c in range(0, columns, tile):
+        partial[:, c : c + tile] = contract(
+            attended[...], weight[:, c : c + tile], 1, 0
+        ).astype(BF16)
 
 
 def attend(
@@ -238,40 +242,40 @@
     requests, steps, width = queries.shape
     cache_size, kv_width = cache_k.shape[1:]
     capacity = max(2, 2 * requests // owners)
-    block = min(32, requests)
+    block = min(16, requests)
     heads = width // HEAD_DIM
     total_rows = requests * steps
     per = capacity * steps
     anywhere = pl.BlockSpec(memory_space=pl.ANY)
     local = pl.BlockSpec(memory_space=pltpu.VMEM)
     return pl.pallas_call(
-        functools.partial(attend_kernel, owners, blocks, resident, capacity, block),
+        functools.partial(attend_kernel, owners, blocks - 1, resident, capacity, block),
         grid_spec=pltpu.PrefetchScalarGridSpec(
             num_scalar_prefetch=3,
             in_specs=[local] + [anywhere] * 6,
-            out_specs=[local] * (2 + blocks + owners),
+            out_specs=[local] * (4 + owners),
             scratch_shapes=[
                 pltpu.VMEM((requests, steps, width), BF16),
                 pltpu.VMEM((requests, steps, kv_width), BF16),
                 pltpu.VMEM((requests, steps, kv_width), BF16),
                 pltpu.VMEM((requests, cache_size, kv_width), BF16),
                 pltpu.VMEM((requests, cache_size, kv_width), BF16),
-                pltpu.VMEM((blocks, width, columns), BF16),
+                pltpu.VMEM((width, columns), BF16),
                 pltpu.VMEM((total_rows, kv_width), BF16),
                 pltpu.VMEM((total_rows, kv_width), BF16),
                 pltpu.VMEM((heads * block * steps, HEAD_DIM), F32),
                 pltpu.VMEM((heads * total_rows, HEAD_DIM), F32),
-                pltpu.VMEM((total_rows, width), BF16),
                 pltpu.SemaphoreType.DMA((3,)),
                 pltpu.SemaphoreType.DMA((2, requests // block)),
-                pltpu.SemaphoreType.DMA((blocks,)),
+                pltpu.SemaphoreType.DMA((1,)),
             ],
         ),
         out_shape=[
+            jax.ShapeDtypeStruct((total_rows, width), BF16),
             jax.ShapeDtypeStruct((owners * per, total_rows), BF16),
             jax.ShapeDtypeStruct((total_rows, LANES), BF16),
+            jax.ShapeDtypeStruct((total_rows, columns), BF16),
         ]
-        + [jax.ShapeDtypeStruct((total_rows, columns), BF16)] * blocks
         + [jax.ShapeDtypeStruct((per, width + LANES), BF16)] * owners,
         compiler_params=pltpu.CompilerParams(vmem_limit_bytes=KERNEL_VMEM),
         cost_estimate=SMALL_COST,
@@ -288,6 +292,59 @@
         cache_v,
         weight,
     )
+
+
+def project_kernel(count, *refs):
+    column = refs[0]
+    refs = refs[1:]
+    attended_hbm, weight_hbm = refs[:2]
+    outs = refs[2 : 2 + count]
+    attended, weight, in_sem, weight_sem = refs[2 + count :]
+    columns = weight.shape[2]
+    attended_copy = pltpu.make_async_copy(attended_hbm, attended, in_sem.at[0])
+    attended_copy.start()
+    copies = []
+    for j in range(count):
+        start = pl.multiple_of(jnp.bitwise_xor(column[0], count - 1 - j) * columns, LANES)
+        copy = pltpu.make_async_copy(
+            weight_hbm.at[:, pl.ds(start, columns)], weight.at[j], weight_sem.at[j]
+        )
+        copy.start()
+        copies.append(copy)
+    attended_copy.wait()
+    tile = min(256, columns)
+    for j in range(count):
+        copies[j].wait()
+        for c in range(0, columns, tile):
+            outs[j][:, c : c + tile] = contract(
+                attended[...], weight[j, :, c : c + tile], 1, 0
+            ).astype(BF16)
+
+
+def project(attended, weight, column, blocks):
+    rows, depth = attended.shape
+    columns = weight.shape[1] // blocks
+    count = blocks - 1
+    local = pl.BlockSpec(memory_space=pltpu.VMEM)
+    anywhere = pl.BlockSpec(memory_space=pl.ANY)
+    return pl.pallas_call(
+        functools.partial(project_kernel, count),
+        grid_spec=pltpu.PrefetchScalarGridSpec(
+            num_scalar_prefetch=1,
+            in_specs=[anywhere] * 2,
+            out_specs=[local] * count,
+            scratch_shapes=[
+                pltpu.VMEM((rows, depth), BF16),
+                pltpu.VMEM((count, depth, columns), BF16),
+                pltpu.SemaphoreType.DMA((1,)),
+                pltpu.SemaphoreType.DMA((count,)),
+            ],
+        ),
+        out_shape=[jax.ShapeDtypeStruct((rows, columns), BF16)] * count,
+        compiler_params=pltpu.CompilerParams(vmem_limit_bytes=KERNEL_VMEM),
+        cost_estimate=SMALL_COST,
+        name="project",
+    )(column, attended, weight)
 
 
 def low_kernel(owners, resident, down, *refs):
@@ -422,7 +479,7 @@
     ups[top_bit] = swap(up_rows, "adapter", top_bit)
     ups[1] = swap(up_rows, "adapter", 1)
 
-    placing, marks, *made = attend(
+    attended, placing, marks, first, *packed = attend(
         queries,
         token_key_rows,
         token_value_rows,
@@ -438,36 +495,38 @@
         blocks,
         columns,
     )
-    ups[1], made = lax.optimization_barrier((ups[1], made))
-    partials, packed = made[:blocks], made[blocks:]
-    inward = {k: swap(partials[k], "tensor", 1) for k in range(blocks - 1, 1, -2)}
+    ups[1], attended, first, packed = lax.optimization_barrier(
+        (ups[1], attended, first, packed)
+    )
+    inward = {blocks - 1: swap(first, "tensor", 1)}
     arrived = [packed[0]] + [None] * (owners - 1)
     for k in range(owners - 1, 0, -1):
         arrived[k] = swap(packed[k], "adapter", k)
+    made = project(attended, output_weight_matrix, mine, blocks)
+    partials = {blocks - 2 - j: part for j, part in enumerate(made)}
+    for k in range(blocks - 3, 1, -2):
+        inward[k] = swap(partials[k], "tensor", 1)
     partials, inward, arrived[1], ups[top_bit] = lax.optimization_barrier(
         (partials, inward, arrived[1], ups[top_bit])
     )
-    near = swap(partials[1], "tensor", 1)
-    half = requests * steps // 2
-    top, bottom = [], []
+    outward = []
     for k in range(2, blocks, 2):
         pair = partials[k].astype(F32) + inward[k + 1].astype(F32)
-        pair = pair.astype(BF16)
-        top.append(swap(pair[:half], "tensor", k))
-        bottom.append(swap(pair[half:], "tensor", k))
-    arrived, near, top = lax.optimization_barrier((arrived, near, top))
+        outward.append(swap(pair.astype(BF16), "tensor", k))
+    near = swap(partials[1], "tensor", 1)
+    arrived, near, outward = lax.optimization_barrier((arrived, near, outward))
+    lows = low_partial(arrived, adapter_down_weight)
+    ups, lows = lax.optimization_barrier((ups, lows))
     forward(ups, "adapter", top_bit // 2)
-    lows = low_partial(arrived, adapter_down_weight)
-
     returned = [lows[0]] + [swap(lows[k], "adapter", k) for k in range(1, owners)]
-    returned, bottom = lax.optimization_barrier((returned, bottom))
+
     low = unpack(placing, returned)
     low_parts = [low] + [swap(low, "tensor", k) for k in range(1, blocks)]
     return combine(
         marks,
         partials[0],
-        [near],
-        [*zip(top, bottom)],
+        [near] + outward,
+        [],
         low_parts,
         [ups[k] for k in range(owners)],
         steps,

time: 63.9 us -> 56.9 us (0.89)
  starting transfers between devices: 20.1 us -> 16.4 us
  local copies, waits for them, and re-layouts: 3.53 us -> 0.98 us
  waiting for transfers between devices: 19.4 us -> 18.6 us
    ppermute x16 -> x15, starting transfers between devices: 20.1 us -> 16.4 us  [swap(): return lax.ppermute(value, axis, [(i, i ^ k) for i in range(count)])]
    unnamed x12 -> x16, local copies, waits for them, and re-layouts: 3.51 us -> 0.98 us
    ppermute x16 -> x15, waiting for transfers between devices: 19.4 us -> 18.6 us  [swap(): return lax.ppermute(value, axis, [(i, i ^ k) for i in range(count)])]
    pallas_call x1 -> x2, Pallas kernels: 16 us -> 16 us  [the longest x1 9.57 us: attend(): pl.pallas_call(functools.partial(attend_kernel, owners, blocks - 1, resid...]
  transfers between devices with their start and end apart: 16 -> 15, of which waited for: 7 -> 8; matrix products, arithmetic and copies ran while one was open for 2% -> 2% of each run, Pallas kernels for 28% -> 29%
where the time goes in v5:
time: 56.9 us; the launch traced here: 56.7 us
  Pallas kernels  19.5 us (34%)
  waiting for transfers between devices  18.6 us (33%)
  starting transfers between devices  16.4 us (29%)
  other arithmetic  1.02 us (2%)
  local copies, waits for them, and re-layouts  0.98 us (2%)
    ppermute x15, waiting for transfers between devices, swap(): return lax.ppermute(value, axis, [(i, i ^ k) for i in range(count)])  18.6 us
    ppermute x15, starting transfers between devices, swap(): return lax.ppermute(value, axis, [(i, i ^ k) for i in range(count)])  16.4 us
    pallas_call x1, Pallas kernels, attend(): pl.pallas_call(functools.partial(attend_kernel, owners, blocks - 1, resid...  9.57 us
    pallas_call x1, Pallas kernels, project(): pl.pallas_call(functools.partial(project_kernel, count), grid_spec=pltpu....  6.46 us
    pallas_call x1, Pallas kernels, combine(): pl.pallas_call(functools.partial(combine_kernel, 1 + len(partials), len(h...  1.7 us
    pallas_call x1, Pallas kernels, low_partial(): pl.pallas_call(functools.partial(low_kernel, owners, resident), out_shape...  1.47 us
  transfers between devices with their start and end apart: 15, of which 8 were waited for; matrix products, arithmetic and copies ran while one was open for 2% of the time, Pallas kernels for 29%

profile of v5, /device:TPU:0, one launch (start us, length us, event | category | flops | bytes accessed | tf_op | source)
XLA Modules:
  0.0 56.7 jit_solution(6644199430442590752)
XLA Ops:
  0.5 2.5 %collective-permute-start.3 = (bf16[256,1024]{1,0:T(8,128)(2,1)}, bf16[256,1024]{1,0:T(8,128)(2,1)S(1)}, u32[]{:S(2)}, u32[]{:S(2)}) collective-permute-start(bf16[256,1024]{1,0:T(8,128)(2,1)} %bitcast.7), channel_id=1, source_target_pairs={{0,8},{4,12},{8,0},{12,4},{1,9},{5,13},{9,1},{13,5},{2,10},{6,14},... | collective-permute-start | bytes 1572872 | tf_op jit(solution)/shard_map/ppermute | solution.py:446
  2.9 9.6 %attend.1 = (bf16[128,2048]{1,0:T(8,128)(2,1)}, bf16[256,128]{1,0:T(8,128)(2,1)}, bf16[128,128]{1,0:T(8,128)(2,1)}, bf16[128,1024]{1,0:T(8,128)(2,1)}, bf16[64,2...) custom-call(s32[64]{0:T(128)} %lengths.1, s32[1]{0:T(128)} %bitcast.place, ...), custom_call_target="tpu_custom_call" | custom-call | flops 1024 | bytes 1024 | tf_op jit(solution)/shard_map/attend/pallas_call | solution.py:251
  12.9 1.6 %collective-permute-start.1 = (bf16[128,1024]{1,0:T(8,128)(2,1)}, bf16[128,1024]{1,0:T(8,128)(2,1)S(1)}, u32[]{:S(2)}, u32[]{:S(2)}) collective-permute-start(bf16[128,1024]{1,0:T(8,128)(2,1)} %get-tuple-element.57), channel_id=1, source_target_pairs={{0,1},{1,0},{2,3},{3,2},{4,5},{5,4},{6,7},{7,6},{8,9},{9,8},{10,11... | collective-permute-start | bytes 786440 | tf_op jit(solution)/shard_map/ppermute | solution.py:446
  14.5 6.5 %project.1 = (bf16[128,1024]{1,0:T(8,128)(2,1)}, bf16[128,1024]{1,0:T(8,128)(2,1)}, bf16[128,1024]{1,0:T(8,128)(2,1)}) custom-call(s32[1]{0:T(128)} %bitcast.1.column.refs_0_, bf16[128,2048]{1,0:T(8,128)(2,1)} %get-tuple-element.53.refs_1_, bf16[2048,4096]{1,0:T(8,128)(2,1)} %refs_2_.1), custom_call_target="tpu_custom_call" | custom-call | flops 1024 | bytes 1024 | tf_op jit(solution)/shard_map/project/pallas_call | solution.py:330
  21.0 0.6 %collective-permute-start.4 = (bf16[64,2176]{1,0:T(8,128)(2,1)S(1)}, bf16[64,2176]{1,0:T(8,128)(2,1)S(1)}, u32[]{:S(2)}, u32[]{:S(2)}) collective-permute-start(bf16[64,2176]{1,0:T(8,128)(2,1)S(1)} %copy-done.7), channel_id=1, source_target_pairs={{0,8},{4,12},{8,0},{12,4},{1,9},{5,13},{9,1},{13,5},{2,10},{6,14},... | collective-permute-start | bytes 835592 | tf_op jit(solution)/shard_map/ppermute | solution.py:446
  21.6 0.8 %collective-permute-start.5 = (bf16[64,2176]{1,0:T(8,128)(2,1)S(1)}, bf16[64,2176]{1,0:T(8,128)(2,1)S(1)}, u32[]{:S(2)}, u32[]{:S(2)}) collective-permute-start(bf16[64,2176]{1,0:T(8,128)(2,1)S(1)} %copy-done.6), channel_id=1, source_target_pairs={{0,12},{4,8},{8,4},{12,0},{1,13},{5,9},{9,5},{13,1},{2,14},{6,10},... | collective-permute-start | bytes 835592 | tf_op jit(solution)/shard_map/ppermute | solution.py:446
  22.4 1.0 %add_convert_fusion = bf16[128,1024]{1,0:T(8,128)(2,1)S(1)} fusion(bf16[128,1024]{1,0:T(8,128)(2,1)S(1)} %collective-permute-done.1, bf16[128,1024]{1,0:T(8,128)(2,1)} %get-tuple-element.65), kind=kLoop, calls=%fused_computation | loop fusion | flops 524288 | bytes 786432 | tf_op jit(solution)/shard_map/convert_element_type | solution.py:515
  23.4 2.7 %collective-permute-start.7 = (bf16[128,1024]{1,0:T(8,128)(2,1)S(1)}, bf16[128,1024]{1,0:T(8,128)(2,1)S(1)}, u32[]{:S(2)}, u32[]{:S(2)}) collective-permute-start(bf16[128,1024]{1,0:T(8,128)(2,1)S(1)} %add_convert_fusion), channel_id=1, source_target_pairs={{0,2},{1,3},{2,0},{3,1},{4,6},{5,7},{6,4},{7,5},{8,10},{9,11},{10,... | collective-permute-start | bytes 786440 | tf_op jit(solution)/shard_map/ppermute | solution.py:446
  26.1 0.8 %collective-permute-start.6 = (bf16[128,1024]{1,0:T(8,128)(2,1)}, bf16[128,1024]{1,0:T(8,128)(2,1)S(1)}, u32[]{:S(2)}, u32[]{:S(2)}) collective-permute-start(bf16[128,1024]{1,0:T(8,128)(2,1)} %get-tuple-element.64), channel_id=1, source_target_pairs={{0,1},{1,0},{2,3},{3,2},{4,5},{5,4},{6,7},{7,6},{8,9},{9,8},{10,11... | collective-permute-start | bytes 786440 | tf_op jit(solution)/shard_map/ppermute | solution.py:446
  26.9 3.7 %collective-permute-done.4.refs_2_ = bf16[64,2176]{1,0:T(8,128)(2,1)S(1)} collective-permute-done((bf16[64,2176]{1,0:T(8,128)(2,1)S(1)}, bf16[64,2176]{1,0:T(8,128)(2,1)S(1)}, u32[]{:S(2)}, u32[]{:S(2)}) %collective-permute-start.4) | collective-permute-done | bytes 278560 | tf_op jit(solution)/shard_map/ppermute | solution.py:446
  30.6 4.0 %collective-permute-done.5.refs_3_ = bf16[64,2176]{1,0:T(8,128)(2,1)S(1)} collective-permute-done((bf16[64,2176]{1,0:T(8,128)(2,1)S(1)}, bf16[64,2176]{1,0:T(8,128)(2,1)S(1)}, u32[]{:S(2)}, u32[]{:S(2)}) %collective-permute-start.5) | collective-permute-done | bytes 278560 | tf_op jit(solution)/shard_map/ppermute | solution.py:446
  34.6 4.4 %collective-permute-done.7.refs_2_ = bf16[128,1024]{1,0:T(8,128)(2,1)S(1)} collective-permute-done((bf16[128,1024]{1,0:T(8,128)(2,1)S(1)}, bf16[128,1024]{1,0:T(8,128)(2,1)S(1)}, u32[]{:S(2)}, u32[]{:S(2)}) %collective-permute-start.7) | collective-permute-done | bytes 262176 | tf_op jit(solution)/shard_map/ppermute | solution.py:446
  39.0 1.5 %collective-permute-done.6.refs_1_ = bf16[128,1024]{1,0:T(8,128)(2,1)S(1)} collective-permute-done((bf16[128,1024]{1,0:T(8,128)(2,1)}, bf16[128,1024]{1,0:T(8,128)(2,1)S(1)}, u32[]{:S(2)}, u32[]{:S(2)}) %collective-permute-start.6) | collective-permute-done | bytes 262176 | tf_op jit(solution)/shard_map/ppermute | solution.py:446
  40.5 1.5 %low.1 = (bf16[64,128]{1,0:T(8,128)(2,1)S(1)}, bf16[64,128]{1,0:T(8,128)(2,1)S(1)}, bf16[64,128]{1,0:T(8,128)(2,1)S(1)}, bf16[64,128]{1,0:T(8,128)(2,1)S(1)}) custom-call(bf16[256,2048]{1,0:T(8,128)(2,1)S(1)} %bitcast.5, bf16[64,2176]{1,0:T(8,128)(2,1)S(1)} %copy-done.2, bf16[64,2176]{1,0:T(8,128)(2,1)S(1)} %collective-permute-done.2.refs_1_, ...), custom_call_target="tpu_custom_call" | custom-call | flops 1024 | bytes 1024 | tf_op jit(solution)/shard_map/low/pallas_call | solution.py:369
  42.1 0.6 %collective-permute-start.10 = (bf16[64,128]{1,0:T(8,128)(2,1)S(1)}, bf16[64,128]{1,0:T(8,128)(2,1)S(1)}, u32[]{:S(2)}, u32[]{:S(2)}) collective-permute-start(bf16[64,128]{1,0:T(8,128)(2,1)S(1)} %get-tuple-element.83), channel_id=1, source_target_pairs={{0,12},{4,8},{8,4},{12,0},{1,13},{5,9},{9,5},{13,1},{2,14},{6,10},... | collective-permute-start | bytes 49160 | tf_op jit(solution)/shard_map/ppermute | solution.py:446
  42.8 1.5 %collective-permute-start.9 = (bf16[64,128]{1,0:T(8,128)(2,1)S(1)}, bf16[64,128]{1,0:T(8,128)(2,1)S(1)}, u32[]{:S(2)}, u32[]{:S(2)}) collective-permute-start(bf16[64,128]{1,0:T(8,128)(2,1)S(1)} %get-tuple-element.82), channel_id=1, source_target_pairs={{0,8},{4,12},{8,0},{12,4},{1,9},{5,13},{9,1},{13,5},{2,10},{6,14},... | collective-permute-start | bytes 49160 | tf_op jit(solution)/shard_map/ppermute | solution.py:446
  44.3 1.0 %collective-permute-done.10.refs_3_ = bf16[64,128]{1,0:T(8,128)(2,1)S(1)} collective-permute-done((bf16[64,128]{1,0:T(8,128)(2,1)S(1)}, bf16[64,128]{1,0:T(8,128)(2,1)S(1)}, u32[]{:S(2)}, u32[]{:S(2)}) %collective-permute-start.10) | collective-permute-done | bytes 16416 | tf_op jit(solution)/shard_map/ppermute | solution.py:446
  45.3 1.2 %collective-permute-done.9.refs_2_ = bf16[64,128]{1,0:T(8,128)(2,1)S(1)} collective-permute-done((bf16[64,128]{1,0:T(8,128)(2,1)S(1)}, bf16[64,128]{1,0:T(8,128)(2,1)S(1)}, u32[]{:S(2)}, u32[]{:S(2)}) %collective-permute-start.9) | collective-permute-done | bytes 16416 | tf_op jit(solution)/shard_map/ppermute | solution.py:446
  47.1 1.4 %collective-permute-start.12 = (bf16[64,128]{1,0:T(8,128)(2,1)S(1)}, bf16[64,128]{1,0:T(8,128)(2,1)S(1)}, u32[]{:S(2)}, u32[]{:S(2)}) collective-permute-start(bf16[64,128]{1,0:T(8,128)(2,1)S(1)} %unpack.1.refs_3_), channel_id=1, source_target_pairs={{0,2},{1,3},{2,0},{3,1},{4,6},{5,7},{6,4},{7,5},{8,10},{9,11},{10,... | collective-permute-start | bytes 49160 | tf_op jit(solution)/shard_map/ppermute | solution.py:446
  48.5 2.8 %collective-permute-start.13 = (bf16[64,128]{1,0:T(8,128)(2,1)S(1)}, bf16[64,128]{1,0:T(8,128)(2,1)S(1)}, u32[]{:S(2)}, u32[]{:S(2)}) collective-permute-start(bf16[64,128]{1,0:T(8,128)(2,1)S(1)} %unpack.1.refs_3_), channel_id=1, source_target_pairs={{0,3},{1,2},{2,1},{3,0},{4,7},{5,6},{6,5},{7,4},{8,11},{9,10},{10,... | collective-permute-start | bytes 49160 | tf_op jit(solution)/shard_map/ppermute | solution.py:446
  51.3 0.5 collective-permute-done.12.refs_5_
  51.7 2.2 %collective-permute-done.13.refs_6_ = bf16[64,128]{1,0:T(8,128)(2,1)S(1)} collective-permute-done((bf16[64,128]{1,0:T(8,128)(2,1)S(1)}, bf16[64,128]{1,0:T(8,128)(2,1)S(1)}, u32[]{:S(2)}, u32[]{:S(2)}) %collective-permute-start.13) | collective-permute-done | bytes 16416 | tf_op jit(solution)/shard_map/ppermute | solution.py:446
  54.0 0.9 %copy-done.3 = bf16[128,1024]{1,0:T(8,128)(2,1)S(1)} copy-done((bf16[128,1024]{1,0:T(8,128)(2,1)S(1)}, bf16[128,1024]{1,0:T(8,128)(2,1)}, u32[]{:S(2)}) %copy-start.3) | copy-done | bytes 262168
  55.0 1.7 %combine.1 = bf16[64,2,1024]{2,1,0:T(2,128)(2,1)} custom-call(bf16[128,128]{1,0:T(8,128)(2,1)S(1)} %copy-done.5, bf16[128,1024]{1,0:T(8,128)(2,1)S(1)} %copy-done.3, bf16[128,1024]{1,0:T(8,128)(2,1)S(1)} %collective-permute-done.6.refs_1_, bf16[128,1024]{1,0:T(8,128)(2,1)S(1)} %collective-permute-done.7.refs_2_, bf16[64,128]{1,0:T(8,128)(2,1)S(1)} %unpack.1.refs_3_, ...), custom_call_target="tpu_custom_call" | custom-call | flops 1024 | bytes 1024 | tf_op jit(solution)/shard_map/combine/pallas_call | solution.py:433
  (28 shorter events, 1.5 us)
Async XLA Ops:
  0.0 12.5 %collective-permute-start = (bf16[256,1024]{1,0:T(8,128)(2,1)}, bf16[256,1024]{1,0:T(8,128)(2,1)S(1)}, u32[]{:S(2)}, u32[]{:S(2)}) collective-permute-start(bf16[256,1024]{1,0:T(8,128)(2,1)} %bitcast.6), channel_id=1, source_target_pairs={{0,4},{4,0},{8,12},{12,8},{1,5},{5,1},{9,13},{13,9},{2,6},{6,2},{1... | collective-permute-start | bytes 1572872 | tf_op jit(solution)/shard_map/ppermute | solution.py:446
  0.5 21.9 %collective-permute-start.3 = (bf16[256,1024]{1,0:T(8,128)(2,1)}, bf16[256,1024]{1,0:T(8,128)(2,1)S(1)}, u32[]{:S(2)}, u32[]{:S(2)}) collective-permute-start(bf16[256,1024]{1,0:T(8,128)(2,1)} %bitcast.7), channel_id=1, source_target_pairs={{0,8},{4,12},{8,0},{12,4},{1,9},{5,13},{9,1},{13,5},{2,10},{6,14},... | collective-permute-start | bytes 1572872 | tf_op jit(solution)/shard_map/ppermute | solution.py:446
  12.5 8.4 %copy-start.7 = (bf16[64,2176]{1,0:T(8,128)(2,1)S(1)}, bf16[64,2176]{1,0:T(8,128)(2,1)}, u32[]{:S(2)}) copy-start(bf16[64,2176]{1,0:T(8,128)(2,1)} %get-tuple-element.62) | copy-start | bytes 835588
  12.5 9.0 %copy-start.6 = (bf16[64,2176]{1,0:T(8,128)(2,1)S(1)}, bf16[64,2176]{1,0:T(8,128)(2,1)}, u32[]{:S(2)}) copy-start(bf16[64,2176]{1,0:T(8,128)(2,1)} %get-tuple-element.63) | copy-start | bytes 835588
  12.6 28.0 %copy-start = (bf16[4,64,2048]{2,1,0:T(8,128)(2,1)S(1)}, bf16[4,64,2048]{2,1,0:T(8,128)(2,1)}, u32[]{:S(2)}) copy-start(bf16[4,64,2048]{2,1,0:T(8,128)(2,1)} %param.18) | copy-start | bytes 3145732
  12.6 28.0 %copy-start.2 = (bf16[64,2176]{1,0:T(8,128)(2,1)S(1)}, bf16[64,2176]{1,0:T(8,128)(2,1)}, u32[]{:S(2)}) copy-start(bf16[64,2176]{1,0:T(8,128)(2,1)} %get-tuple-element.72.refs_0_) | copy-start | bytes 835588
  12.6 34.0 %copy-start.4 = (bf16[256,128]{1,0:T(8,128)(2,1)S(1)}, bf16[256,128]{1,0:T(8,128)(2,1)}, u32[]{:S(2)}) copy-start(bf16[256,128]{1,0:T(8,128)(2,1)} %get-tuple-element.69.placing) | copy-start | bytes 196612
  12.6 41.4 %copy-start.1 = (bf16[4,64,1024]{2,1,0:T(8,128)(2,1)S(1)}, bf16[4,64,1024]{2,1,0:T(8,128)(2,1)}, u32[]{:S(2)}) copy-start(bf16[4,64,1024]{2,1,0:T(8,128)(2,1)} %param.19) | copy-start | bytes 1572868
  12.6 41.4 %copy-start.5 = (bf16[128,128]{1,0:T(8,128)(2,1)S(1)}, bf16[128,128]{1,0:T(8,128)(2,1)}, u32[]{:S(2)}) copy-start(bf16[128,128]{1,0:T(8,128)(2,1)} %get-tuple-element.46.marks) | copy-start | bytes 98308
  12.6 9.8 %collective-permute-start.2 = (bf16[64,2176]{1,0:T(8,128)(2,1)}, bf16[64,2176]{1,0:T(8,128)(2,1)S(1)}, u32[]{:S(2)}, u32[]{:S(2)}) collective-permute-start(bf16[64,2176]{1,0:T(8,128)(2,1)} %get-tuple-element.58), channel_id=1, source_target_pairs={{0,4},{4,0},{8,12},{12,8},{1,5},{5,1},{9,13},{13,9},{2,6},{6,2},{1... | collective-permute-start | bytes 835592 | tf_op jit(solution)/shard_map/ppermute | solution.py:446
  12.9 9.5 %collective-permute-start.1 = (bf16[128,1024]{1,0:T(8,128)(2,1)}, bf16[128,1024]{1,0:T(8,128)(2,1)S(1)}, u32[]{:S(2)}, u32[]{:S(2)}) collective-permute-start(bf16[128,1024]{1,0:T(8,128)(2,1)} %get-tuple-element.57), channel_id=1, source_target_pairs={{0,1},{1,0},{2,3},{3,2},{4,5},{5,4},{6,7},{7,6},{8,9},{9,8},{10,11... | collective-permute-start | bytes 786440 | tf_op jit(solution)/shard_map/ppermute | solution.py:446
  21.0 9.6 %collective-permute-start.4 = (bf16[64,2176]{1,0:T(8,128)(2,1)S(1)}, bf16[64,2176]{1,0:T(8,128)(2,1)S(1)}, u32[]{:S(2)}, u32[]{:S(2)}) collective-permute-start(bf16[64,2176]{1,0:T(8,128)(2,1)S(1)} %copy-done.7), channel_id=1, source_target_pairs={{0,8},{4,12},{8,0},{12,4},{1,9},{5,13},{9,1},{13,5},{2,10},{6,14},... | collective-permute-start | bytes 835592 | tf_op jit(solution)/shard_map/ppermute | solution.py:446
  21.6 13.0 %collective-permute-start.5 = (bf16[64,2176]{1,0:T(8,128)(2,1)S(1)}, bf16[64,2176]{1,0:T(8,128)(2,1)S(1)}, u32[]{:S(2)}, u32[]{:S(2)}) collective-permute-start(bf16[64,2176]{1,0:T(8,128)(2,1)S(1)} %copy-done.6), channel_id=1, source_target_pairs={{0,12},{4,8},{8,4},{12,0},{1,13},{5,9},{9,5},{13,1},{2,14},{6,10},... | collective-permute-start | bytes 835592 | tf_op jit(solution)/shard_map/ppermute | solution.py:446
  23.4 15.6 %collective-permute-start.7 = (bf16[128,1024]{1,0:T(8,128)(2,1)S(1)}, bf16[128,1024]{1,0:T(8,128)(2,1)S(1)}, u32[]{:S(2)}, u32[]{:S(2)}) collective-permute-start(bf16[128,1024]{1,0:T(8,128)(2,1)S(1)} %add_convert_fusion), channel_id=1, source_target_pairs={{0,2},{1,3},{2,0},{3,1},{4,6},{5,7},{6,4},{7,5},{8,10},{9,11},{10,... | collective-permute-start | bytes 786440 | tf_op jit(solution)/shard_map/ppermute | solution.py:446
  26.1 14.4 %collective-permute-start.6 = (bf16[128,1024]{1,0:T(8,128)(2,1)}, bf16[128,1024]{1,0:T(8,128)(2,1)S(1)}, u32[]{:S(2)}, u32[]{:S(2)}) collective-permute-start(bf16[128,1024]{1,0:T(8,128)(2,1)} %get-tuple-element.64), channel_id=1, source_target_pairs={{0,1},{1,0},{2,3},{3,2},{4,5},{5,4},{6,7},{7,6},{8,9},{9,8},{10,11... | collective-permute-start | bytes 786440 | tf_op jit(solution)/shard_map/ppermute | solution.py:446
  42.0 12.0 %collective-permute-start.14 = (bf16[256,1024]{1,0:T(8,128)(2,1)S(1)}, bf16[256,1024]{1,0:T(8,128)(2,1)S(1)}, u32[]{:S(2)}, u32[]{:S(2)}) collective-permute-start(bf16[256,1024]{1,0:T(8,128)(2,1)S(1)} %collective-permute-done.3.refs_9_), channel_id=1, source_target_pairs={{0,4},{4,0},{8,12},{12,8},{1,5},{5,1},{9,13},{13,9},{2,6},{6,2},{1... | collective-permute-start | bytes 1572872 | tf_op jit(solution)/shard_map/ppermute | solution.py:446
  42.1 3.2 %collective-permute-start.10 = (bf16[64,128]{1,0:T(8,128)(2,1)S(1)}, bf16[64,128]{1,0:T(8,128)(2,1)S(1)}, u32[]{:S(2)}, u32[]{:S(2)}) collective-permute-start(bf16[64,128]{1,0:T(8,128)(2,1)S(1)} %get-tuple-element.83), channel_id=1, source_target_pairs={{0,12},{4,8},{8,4},{12,0},{1,13},{5,9},{9,5},{13,1},{2,14},{6,10},... | collective-permute-start | bytes 49160 | tf_op jit(solution)/shard_map/ppermute | solution.py:446
  42.7 2.6 %collective-permute-start.8 = (bf16[64,128]{1,0:T(8,128)(2,1)S(1)}, bf16[64,128]{1,0:T(8,128)(2,1)S(1)}, u32[]{:S(2)}, u32[]{:S(2)}) collective-permute-start(bf16[64,128]{1,0:T(8,128)(2,1)S(1)} %get-tuple-element.81), channel_id=1, source_target_pairs={{0,4},{4,0},{8,12},{12,8},{1,5},{5,1},{9,13},{13,9},{2,6},{6,2},{1... | collective-permute-start | bytes 49160 | tf_op jit(solution)/shard_map/ppermute | solution.py:446
  42.8 3.7 %collective-permute-start.9 = (bf16[64,128]{1,0:T(8,128)(2,1)S(1)}, bf16[64,128]{1,0:T(8,128)(2,1)S(1)}, u32[]{:S(2)}, u32[]{:S(2)}) collective-permute-start(bf16[64,128]{1,0:T(8,128)(2,1)S(1)} %get-tuple-element.82), channel_id=1, source_target_pairs={{0,8},{4,12},{8,0},{12,4},{1,9},{5,13},{9,1},{13,5},{2,10},{6,14},... | collective-permute-start | bytes 49160 | tf_op jit(solution)/shard_map/ppermute | solution.py:446
  46.8 4.5 %collective-permute-start.11 = (bf16[64,128]{1,0:T(8,128)(2,1)S(1)}, bf16[64,128]{1,0:T(8,128)(2,1)S(1)}, u32[]{:S(2)}, u32[]{:S(2)}) collective-permute-start(bf16[64,128]{1,0:T(8,128)(2,1)S(1)} %unpack.1.refs_3_), channel_id=1, source_target_pairs={{0,1},{1,0},{2,3},{3,2},{4,5},{5,4},{6,7},{7,6},{8,9},{9,8},{10,11... | collective-permute-start | bytes 49160 | tf_op jit(solution)/shard_map/ppermute | solution.py:446
  47.1 4.6 %collective-permute-start.12 = (bf16[64,128]{1,0:T(8,128)(2,1)S(1)}, bf16[64,128]{1,0:T(8,128)(2,1)S(1)}, u32[]{:S(2)}, u32[]{:S(2)}) collective-permute-start(bf16[64,128]{1,0:T(8,128)(2,1)S(1)} %unpack.1.refs_3_), channel_id=1, source_target_pairs={{0,2},{1,3},{2,0},{3,1},{4,6},{5,7},{6,4},{7,5},{8,10},{9,11},{10,... | collective-permute-start | bytes 49160 | tf_op jit(solution)/shard_map/ppermute | solution.py:446
  48.5 5.5 %collective-permute-start.13 = (bf16[64,128]{1,0:T(8,128)(2,1)S(1)}, bf16[64,128]{1,0:T(8,128)(2,1)S(1)}, u32[]{:S(2)}, u32[]{:S(2)}) collective-permute-start(bf16[64,128]{1,0:T(8,128)(2,1)S(1)} %unpack.1.refs_3_), channel_id=1, source_target_pairs={{0,3},{1,2},{2,1},{3,0},{4,7},{5,6},{6,5},{7,4},{8,11},{9,10},{10,... | collective-permute-start | bytes 49160 | tf_op jit(solution)/shard_map/ppermute | solution.py:446
  54.0 1.0 %copy-start.3 = (bf16[128,1024]{1,0:T(8,128)(2,1)S(1)}, bf16[128,1024]{1,0:T(8,128)(2,1)}, u32[]{:S(2)}) copy-start(bf16[128,1024]{1,0:T(8,128)(2,1)} %get-tuple-element.59.refs_0_) | copy-start | bytes 786436

commit v6 on v5

--- a/solution.py
+++ b/solution.py
@@ -14,7 +14,7 @@
 LANES = 128
 KERNEL_VMEM = 56 * 1024 * 1024
 SMALL_COST = pl.CostEstimate(flops=1024, bytes_accessed=1024, transcendentals=0)
-SMALL_VMEM = 12 * 1024 * 1024
+SMALL_VMEM = 16 * 1024 * 1024
 
 F32 = jnp.float32
 BF16 = jnp.bfloat16
@@ -27,10 +27,8 @@
 
 
 def attend_kernel(
-    owners,
     made,
     resident,
-    capacity,
     block,
     lengths,
     place,
@@ -44,8 +42,7 @@
     weight_hbm,
     *rest,
 ):
-    attended, placing_out, marks_out, partial = rest[:4]
-    packed = rest[4 : 4 + owners]
+    attended, marks_out, partial = rest[:3]
     (
         queries,
         fresh_k,
@@ -60,7 +57,7 @@
         small_sem,
         cache_sem,
         weight_sem,
-    ) = rest[4 + owners :]
+    ) = rest[3:]
     requests, steps, width = queries.shape
     heads = width // HEAD_DIM
     groups = cache_k.shape[2] // HEAD_DIM
@@ -94,37 +91,17 @@
     named = adapters[...]
     owner = lax.div(named, resident)
     local = named - owner * resident
-    relative = jnp.bitwise_xor(owner, place[0])
-    owner_id = lax.broadcasted_iota(jnp.int32, (owners, requests), 0)
-    member = (owner_id == relative).astype(F32)
-    before = lax.broadcasted_iota(jnp.int32, (requests, requests), 0) < (
-        lax.broadcasted_iota(jnp.int32, (requests, requests), 1)
-    )
-    earlier = contract(member.astype(BF16), before.astype(BF16), 1, 0)
-    slot = jnp.sum(earlier * member, axis=0, keepdims=True)
+    relative = jnp.bitwise_xor(owner, place[0]) * resident + local
     facts = jnp.concatenate(
-        [relative.astype(F32), slot, local.astype(F32), jnp.zeros((5, requests), F32)], axis=0
-    )
+        [relative.astype(F32), jnp.zeros((7, requests), F32)], axis=0
+    ).astype(BF16)
     spread = lax.broadcasted_iota(jnp.int32, (requests, total_rows), 0) == lax.div(
         lax.broadcasted_iota(jnp.int32, (requests, total_rows), 1), steps
     )
-    facts = contract(facts.astype(BF16), spread.astype(BF16), 1, 0).astype(jnp.int32)
-    token = lax.rem(lax.broadcasted_iota(jnp.int32, (1, total_rows), 1), steps)
-    target = (facts[0:1] * capacity + facts[1:2]) * steps + token
-    slots = owners * capacity * steps
-    placing = (
-        lax.broadcasted_iota(jnp.int32, (slots, total_rows), 0) == target
+    facts = contract(facts, spread.astype(BF16), 1, 0).astype(jnp.int32)
+    named_here = (
+        lax.broadcasted_iota(jnp.int32, (LANES, total_rows), 0) == facts[0:1]
     ).astype(BF16)
-    placing_out[...] = placing
-    chosen = (
-        lax.broadcasted_iota(jnp.int32, (LANES, total_rows), 0) == facts[2:3]
-    ).astype(BF16)
-    per = capacity * steps
-    carried = contract(placing, chosen, 1, 1).astype(BF16)
-    for k in range(owners):
-        packed[k][:, width:] = carried[k * per : (k + 1) * per]
-    adapter_id = lax.broadcasted_iota(jnp.int32, (LANES, total_rows), 0)
-    named_here = (adapter_id == facts[0:1] * resident + facts[2:3]).astype(BF16)
     identity = lax.broadcasted_iota(jnp.int32, (total_rows, total_rows), 0) == (
         lax.broadcasted_iota(jnp.int32, (total_rows, total_rows), 1)
     )
@@ -210,11 +187,6 @@
         attended[:, h * HEAD_DIM : (h + 1) * HEAD_DIM] = result_scratch[
             h * total_rows : (h + 1) * total_rows, :
         ].astype(BF16)
-    tile = min(512, width)
-    for c in range(0, width, tile):
-        moved = contract(placing_out[...], attended[:, c : c + tile], 1, 0).astype(BF16)
-        for k in range(owners):
-            packed[k][:, c : c + tile] = moved[k * per : (k + 1) * per]
     weight_copy.wait()
     tile = min(256, columns)
     for c in range(0, columns, tile):
@@ -234,26 +206,23 @@
     place,
     column,
     adapters,
-    owners,
     resident,
     blocks,
     columns,
 ):
     requests, steps, width = queries.shape
     cache_size, kv_width = cache_k.shape[1:]
-    capacity = max(2, 2 * requests // owners)
     block = min(16, requests)
     heads = width // HEAD_DIM
     total_rows = requests * steps
-    per = capacity * steps
     anywhere = pl.BlockSpec(memory_space=pl.ANY)
     local = pl.BlockSpec(memory_space=pltpu.VMEM)
     return pl.pallas_call(
-        functools.partial(attend_kernel, owners, blocks - 1, resident, capacity, block),
+        functools.partial(attend_kernel, blocks - 1, resident, block),
         grid_spec=pltpu.PrefetchScalarGridSpec(
             num_scalar_prefetch=3,
             in_specs=[local] + [anywhere] * 6,
-            out_specs=[local] * (4 + owners),
+            out_specs=[local] * 3,
             scratch_shapes=[
                 pltpu.VMEM((requests, steps, width), BF16),
                 pltpu.VMEM((requests, steps, kv_width), BF16),
@@ -272,11 +241,9 @@
         ),
         out_shape=[
             jax.ShapeDtypeStruct((total_rows, width), BF16),
-            jax.ShapeDtypeStruct((owners * per, total_rows), BF16),
             jax.ShapeDtypeStruct((total_rows, LANES), BF16),
             jax.ShapeDtypeStruct((total_rows, columns), BF16),
-        ]
-        + [jax.ShapeDtypeStruct((per, width + LANES), BF16)] * owners,
+        ],
         compiler_params=pltpu.CompilerParams(vmem_limit_bytes=KERNEL_VMEM),
         cost_estimate=SMALL_COST,
         name="attend",
@@ -347,58 +314,35 @@
     )(column, attended, weight)
 
 
-def low_kernel(owners, resident, down, *refs):
-    packed = refs[:owners]
-    outs = refs[owners:]
-    depth = down.shape[1]
-    rank = down.shape[0] // resident
-    weight = down[...]
-    for k in range(owners):
-        every = contract(packed[k][:, :depth], weight, 1, 1)
-        marks = packed[k][:, depth:].astype(F32)
-        low = every[:, :rank] * marks[:, 0:1]
-        for y in range(1, resident):
-            low = low + every[:, y * rank : (y + 1) * rank] * marks[:, y : y + 1]
-        outs[k][...] = jnp.concatenate([low, jnp.zeros_like(low)], axis=1).astype(BF16)
-
-
-def low_partial(packed, down):
-    resident, rank, depth = down.shape
-    owners = len(packed)
-    per = packed[0].shape[0]
+def low_kernel(rank, attended, marks, *refs):
+    out = refs[-1]
+    rows = attended[...]
+    chosen = marks[...].astype(F32)
+    low = jnp.zeros((rows.shape[0], rank), F32)
+    first = 0
+    for down in refs[:-1]:
+        every = contract(rows, down[...], 1, 1)
+        for y in range(down.shape[0] // rank):
+            part = every[:, y * rank : (y + 1) * rank]
+            low = low + part * chosen[:, first : first + 1]
+            first += 1
+    half = low.shape[0] // 2
+    out[...] = jnp.concatenate([low[:half], low[half:]], axis=1).astype(BF16)
+
+
+def low_partial(attended, marks, downs, rank):
+    rows = attended.shape[0]
     return pl.pallas_call(
-        functools.partial(low_kernel, owners, resident),
-        out_shape=[jax.ShapeDtypeStruct((per, 2 * rank), BF16)] * owners,
+        functools.partial(low_kernel, rank),
+        out_shape=jax.ShapeDtypeStruct((rows // 2, 2 * rank), BF16),
         compiler_params=pltpu.CompilerParams(vmem_limit_bytes=SMALL_VMEM),
         cost_estimate=SMALL_COST,
         name="low",
-    )(down.reshape(resident * rank, depth), *packed)
-
-
-def unpack_kernel(placing, *refs):
-    out = refs[-1]
-    slots = jnp.concatenate([part[...] for part in refs[:-1]], axis=0)
-    low = contract(placing[...], slots, 0, 0)
-    half = low.shape[0] // 2
-    rank = low.shape[1] // 2
-    out[...] = jnp.concatenate([low[:half, :rank], low[half:, :rank]], axis=1).astype(BF16)
-
-
-def unpack(placing, slots):
-    rows = placing.shape[1]
-    return pl.pallas_call(
-        unpack_kernel,
-        out_shape=jax.ShapeDtypeStruct((rows // 2, slots[0].shape[1]), BF16),
-        compiler_params=pltpu.CompilerParams(vmem_limit_bytes=SMALL_VMEM),
-        cost_estimate=SMALL_COST,
-        name="unpack",
-    )(placing, *slots)
-
-
-def combine_kernel(sums, pairs, blocks, marks, *refs):
+    )(attended, marks, *downs)
+
+
+def combine_kernel(sums, blocks, marks, *refs):
     partials = refs[:sums]
-    halves = refs[sums : sums + 2 * pairs]
-    refs = refs[:sums] + refs[sums + 2 * pairs :]
     lows = refs[sums : sums + blocks]
     ups = refs[sums + blocks : -1]
     out = refs[-1]
@@ -412,9 +356,6 @@
     base = partials[0][...].astype(F32)
     for part in partials[1:]:
         base = base + part[...].astype(F32)
-    for j in range(pairs):
-        both = jnp.concatenate([halves[2 * j][...], halves[2 * j + 1][...]], axis=0)
-        base = base + both.astype(F32)
     first = 0
     for up in ups:
         held = up.shape[0] // rank
@@ -426,14 +367,11 @@
     out[...] = base.reshape(out.shape).astype(BF16)
 
 
-def combine(marks, own, partials, halves, lows, ups, steps):
+def combine(marks, own, partials, lows, ups, steps):
     rows, columns = own.shape
-    split = [part for pair in halves for part in pair]
-    inputs = [marks, own, *partials, *split, *lows, *ups]
+    inputs = [marks, own, *partials, *lows, *ups]
     return pl.pallas_call(
-        functools.partial(
-            combine_kernel, 1 + len(partials), len(halves), len(lows)
-        ),
+        functools.partial(combine_kernel, 1 + len(partials), len(lows)),
         out_shape=jax.ShapeDtypeStruct((rows // steps, steps, columns), BF16),
         compiler_params=pltpu.CompilerParams(vmem_limit_bytes=SMALL_VMEM),
         cost_estimate=SMALL_COST,
@@ -473,13 +411,16 @@
     place = lax.axis_index("adapter").reshape(1)
     mine = lax.axis_index("tensor").reshape(1)
 
-    up_rows = adapter_up_weight.reshape(resident * rank, columns)
     top_bit = owners // 2
-    ups = {0: up_rows}
-    ups[top_bit] = swap(up_rows, "adapter", top_bit)
-    ups[1] = swap(up_rows, "adapter", 1)
-
-    attended, placing, marks, first, *packed = attend(
+    ups = {0: adapter_up_weight.reshape(resident * rank, columns)}
+    downs = {0: adapter_down_weight.reshape(resident * rank, -1)}
+    downs[top_bit] = swap(downs[0], "adapter", top_bit)
+    cut = resident * rank // 2
+    far_ups = [{top_bit: swap(ups[0][:cut], "adapter", top_bit)}]
+    for held in (downs, ups):
+        held[1] = swap(held[0], "adapter", 1)
+
+    attended, marks, first = attend(
         queries,
         token_key_rows,
         token_value_rows,
@@ -490,47 +431,42 @@
         place,
         mine,
         request_adapter,
-        owners,
         resident,
         blocks,
         columns,
     )
-    ups[1], attended, first, packed = lax.optimization_barrier(
-        (ups[1], attended, first, packed)
+    ups[1], downs[1], attended, first = lax.optimization_barrier(
+        (ups[1], downs[1], attended, first)
     )
     inward = {blocks - 1: swap(first, "tensor", 1)}
-    arrived = [packed[0]] + [None] * (owners - 1)
-    for k in range(owners - 1, 0, -1):
-        arrived[k] = swap(packed[k], "adapter", k)
     made = project(attended, output_weight_matrix, mine, blocks)
     partials = {blocks - 2 - j: part for j, part in enumerate(made)}
     for k in range(blocks - 3, 1, -2):
         inward[k] = swap(partials[k], "tensor", 1)
-    partials, inward, arrived[1], ups[top_bit] = lax.optimization_barrier(
-        (partials, inward, arrived[1], ups[top_bit])
-    )
+    partials, inward = lax.optimization_barrier((partials, inward))
     outward = []
     for k in range(2, blocks, 2):
         pair = partials[k].astype(F32) + inward[k + 1].astype(F32)
         outward.append(swap(pair.astype(BF16), "tensor", k))
     near = swap(partials[1], "tensor", 1)
-    arrived, near, outward = lax.optimization_barrier((arrived, near, outward))
-    lows = low_partial(arrived, adapter_down_weight)
-    ups, lows = lax.optimization_barrier((ups, lows))
+    near = near.astype(F32) + partials[0].astype(F32)
+    downs[top_bit], far_ups[0], near, outward = lax.optimization_barrier(
+        (downs[top_bit], far_ups[0], near, outward)
+    )
+    forward(downs, "adapter", top_bit // 2)
+    last_ups = ups[0][cut:]
+    last_ups, near = lax.optimization_barrier((last_ups, near))
+    far_ups.append({top_bit: swap(last_ups, "adapter", top_bit)})
+    low = low_partial(attended, marks, [downs[k] for k in range(owners)], rank)
+    low_parts = [low] + [swap(low, "tensor", k) for k in range(1, blocks)]
+    far_ups[1], low_parts = lax.optimization_barrier((far_ups[1], low_parts))
     forward(ups, "adapter", top_bit // 2)
-    returned = [lows[0]] + [swap(lows[k], "adapter", k) for k in range(1, owners)]
-
-    low = unpack(placing, returned)
-    low_parts = [low] + [swap(low, "tensor", k) for k in range(1, blocks)]
-    return combine(
-        marks,
-        partials[0],
-        [near] + outward,
-        [],
-        low_parts,
-        [ups[k] for k in range(owners)],
-        steps,
-    )
+    for held in far_ups:
+        forward(held, "adapter", top_bit // 2)
+    pieces = []
+    for k in range(owners):
+        pieces += [ups[k]] if k < top_bit else [held[k] for held in far_ups]
+    return combine(marks, near, outward, low_parts, pieces, steps)
 
 
 def solution(mesh):

time: 56.9 us -> 54.4 us (0.956)
  waiting for transfers between devices: 18.6 us -> 16.9 us
  other arithmetic: 1.02 us -> 2.02 us
  local copies, waits for them, and re-layouts: 0.98 us -> 0.06 us
    ppermute x15 -> x14, waiting for transfers between devices: 18.6 us -> 16.9 us  [swap(): return lax.ppermute(value, axis, [(i, i ^ k) for i in range(count)])]
    add x0 -> x1, other arithmetic: none -> 1.01 us  [body(): near = near.astype(F32) + partials[0].astype(F32)]
    unnamed x16 -> x8, local copies, waits for them, and re-layouts: 0.98 us -> 0.02 us
    ppermute x15 -> x14, starting transfers between devices: 16.4 us -> 15.9 us  [swap(): return lax.ppermute(value, axis, [(i, i ^ k) for i in range(count)])]
    pallas_call x4 -> x3, Pallas kernels: 13 us -> 12.7 us  [the longest x1 9.14 us: attend(): pl.pallas_call(functools.partial(attend_kernel, blocks - 1, resident, blo...]
  transfers between devices with their start and end apart: 15 -> 14, of which waited for: 8 -> 7; matrix products, arithmetic and copies ran while one was open for 2% -> 4% of each run, Pallas kernels for 29% -> 32%
where the time goes in v6:
time: 54.4 us; the launch traced here: 54.2 us
  Pallas kernels  19.1 us (35%)
  waiting for transfers between devices  16.9 us (31%)
  starting transfers between devices  15.9 us (29%)
  other arithmetic  2.02 us (4%)
    ppermute x14, waiting for transfers between devices, swap(): return lax.ppermute(value, axis, [(i, i ^ k) for i in range(count)])  16.9 us
    ppermute x14, starting transfers between devices, swap(): return lax.ppermute(value, axis, [(i, i ^ k) for i in range(count)])  15.9 us
    pallas_call x1, Pallas kernels, attend(): pl.pallas_call(functools.partial(attend_kernel, blocks - 1, resident, blo...  9.14 us
    pallas_call x1, Pallas kernels, project(): pl.pallas_call(functools.partial(project_kernel, count), grid_spec=pltpu....  6.47 us
    pallas_call x1, Pallas kernels, combine(): pl.pallas_call(functools.partial(combine_kernel, 1 + len(partials), len(l...  1.86 us
    pallas_call x1, Pallas kernels, low_partial(): pl.pallas_call(functools.partial(low_kernel, rank), out_shape=jax.ShapeDt...  1.67 us
  transfers between devices with their start and end apart: 14, of which 7 were waited for; matrix products, arithmetic and copies ran while one was open for 4% of the time, Pallas kernels for 32%

profile of v6, /device:TPU:0, one launch (start us, length us, event | category | flops | bytes accessed | tf_op | source)
XLA Modules:
  0.0 54.2 jit_solution(12917462071391687723)
XLA Ops:
  0.0 0.5 collective-permute-start.3
  0.5 0.1 collective-permute-start.2
  0.5 2.9 %collective-permute-start = (bf16[256,2048]{1,0:T(8,128)(2,1)}, bf16[256,2048]{1,0:T(8,128)(2,1)S(1)}, u32[]{:S(2)}, u32[]{:S(2)}) collective-permute-start(bf16[256,2048]{1,0:T(8,128)(2,1)} %bitcast.10), channel_id=1, source_target_pairs={{0,8},{4,12},{8,0},{12,4},{1,9},{5,13},{9,1},{13,5},{2,10},{6,14},... | collective-permute-start | bytes 3145736 | tf_op jit(solution)/shard_map/ppermute | solution.py:384
  3.5 9.1 %attend.1 = (bf16[128,2048]{1,0:T(8,128)(2,1)}, bf16[128,128]{1,0:T(8,128)(2,1)}, bf16[128,1024]{1,0:T(8,128)(2,1)}) custom-call(s32[64]{0:T(128)} %lengths.1, s32[1]{0:T(128)} %bitcast.place, s32[1]{0:T(128)} %bitcast.1.column.refs_0_, s32[1,64]{1,0:T(1,128)} %bitcast.14, bf16[64,2,2048]{2,1,0:T(2,128)(2,1)} %queries_hbm.1, ...), custom_call_target="tpu_custom_call" | custom-call | flops 1024 | bytes 1024 | tf_op jit(solution)/shard_map/attend/pallas_call | solution.py:220
  12.7 1.6 %collective-permute-start.4 = (bf16[128,1024]{1,0:T(8,128)(2,1)}, bf16[128,1024]{1,0:T(8,128)(2,1)S(1)}, u32[]{:S(2)}, u32[]{:S(2)}) collective-permute-start(bf16[128,1024]{1,0:T(8,128)(2,1)} %get-tuple-element.37), channel_id=1, source_target_pairs={{0,1},{1,0},{2,3},{3,2},{4,5},{5,4},{6,7},{7,6},{8,9},{9,8},{10,11... | collective-permute-start | bytes 786440 | tf_op jit(solution)/shard_map/ppermute | solution.py:384
  14.3 6.5 %project.1 = (bf16[128,1024]{1,0:T(8,128)(2,1)}, bf16[128,1024]{1,0:T(8,128)(2,1)}, bf16[128,1024]{1,0:T(8,128)(2,1)}) custom-call(s32[1]{0:T(128)} %bitcast.1.column.refs_0_, bf16[128,2048]{1,0:T(8,128)(2,1)} %get-tuple-element.33.refs_1_.attended, bf16[2048,4096]{1,0:T(8,128)(2,1)} %refs_2_.1), custom_call_target="tpu_custom_call" | custom-call | flops 1024 | bytes 1024 | tf_op jit(solution)/shard_map/project/pallas_call | solution.py:297
  20.8 0.1 collective-permute-done.4
  20.9 1.6 %collective-permute-start.5 = (bf16[128,1024]{1,0:T(8,128)(2,1)}, bf16[128,1024]{1,0:T(8,128)(2,1)S(1)}, u32[]{:S(2)}, u32[]{:S(2)}) collective-permute-start(bf16[128,1024]{1,0:T(8,128)(2,1)} %get-tuple-element.38), channel_id=1, source_target_pairs={{0,1},{1,0},{2,3},{3,2},{4,5},{5,4},{6,7},{7,6},{8,9},{9,8},{10,11... | collective-permute-start | bytes 786440 | tf_op jit(solution)/shard_map/ppermute | solution.py:384
  22.5 0.6 %collective-permute-start.1 = (bf16[128,1024]{1,0:T(8,128)(2,1)S(1)}, bf16[128,1024]{1,0:T(8,128)(2,1)S(1)}, u32[]{:S(2)}, u32[]{:S(2)}) collective-permute-start(bf16[128,1024]{1,0:T(8,128)(2,1)S(1)} %bitcast.13), channel_id=1, source_target_pairs={{0,8},{4,12},{8,0},{12,4},{1,9},{5,13},{9,1},{13,5},{2,10},{6,14},... | collective-permute-start | bytes 786440 | tf_op jit(solution)/shard_map/ppermute | solution.py:384
  23.1 1.0 %add_convert_fusion = bf16[128,1024]{1,0:T(8,128)(2,1)S(1)} fusion(bf16[128,1024]{1,0:T(8,128)(2,1)S(1)} %collective-permute-done.4, bf16[128,1024]{1,0:T(8,128)(2,1)} %get-tuple-element.40), kind=kLoop, calls=%fused_computation | loop fusion | flops 524288 | bytes 786432 | tf_op jit(solution)/shard_map/convert_element_type | solution.py:450
  24.1 2.7 %collective-permute-start.6 = (bf16[128,1024]{1,0:T(8,128)(2,1)S(1)}, bf16[128,1024]{1,0:T(8,128)(2,1)S(1)}, u32[]{:S(2)}, u32[]{:S(2)}) collective-permute-start(bf16[128,1024]{1,0:T(8,128)(2,1)S(1)} %add_convert_fusion), channel_id=1, source_target_pairs={{0,2},{1,3},{2,0},{3,1},{4,6},{5,7},{6,4},{7,5},{8,10},{9,11},{10,... | collective-permute-start | bytes 786440 | tf_op jit(solution)/shard_map/ppermute | solution.py:384
  26.8 6.5 %collective-permute-done.5 = bf16[128,1024]{1,0:T(8,128)(2,1)S(1)} collective-permute-done((bf16[128,1024]{1,0:T(8,128)(2,1)}, bf16[128,1024]{1,0:T(8,128)(2,1)S(1)}, u32[]{:S(2)}, u32[]{:S(2)}) %collective-permute-start.5) | collective-permute-done | bytes 262176 | tf_op jit(solution)/shard_map/ppermute | solution.py:384
  33.3 1.0 %convert_add_fusion.refs_0_ = f32[128,1024]{1,0:T(8,128)S(1)} fusion(bf16[128,1024]{1,0:T(8,128)(2,1)} %get-tuple-element.39, bf16[128,1024]{1,0:T(8,128)(2,1)S(1)} %collective-permute-done.5), kind=kLoop, calls=%fused_computation.1 | loop fusion | flops 393216 | bytes 1048576 | tf_op jit(solution)/shard_map/add | solution.py:452
  34.3 3.2 %collective-permute-done.6.refs_1_ = bf16[128,1024]{1,0:T(8,128)(2,1)S(1)} collective-permute-done((bf16[128,1024]{1,0:T(8,128)(2,1)S(1)}, bf16[128,1024]{1,0:T(8,128)(2,1)S(1)}, u32[]{:S(2)}, u32[]{:S(2)}) %collective-permute-start.6) | collective-permute-done | bytes 262176 | tf_op jit(solution)/shard_map/ppermute | solution.py:384
  37.5 1.5 %collective-permute-start.7 = (bf16[128,1024]{1,0:T(8,128)(2,1)S(1)}, bf16[128,1024]{1,0:T(8,128)(2,1)S(1)}, u32[]{:S(2)}, u32[]{:S(2)}) collective-permute-start(bf16[128,1024]{1,0:T(8,128)(2,1)S(1)} %bitcast.12), channel_id=1, source_target_pairs={{0,8},{4,12},{8,0},{12,4},{1,9},{5,13},{9,1},{13,5},{2,10},{6,14},... | collective-permute-start | bytes 786440 | tf_op jit(solution)/shard_map/ppermute | solution.py:384
  39.1 1.1 %collective-permute-done.8.refs_3_ = bf16[256,2048]{1,0:T(8,128)(2,1)S(1)} collective-permute-done((bf16[256,2048]{1,0:T(8,128)(2,1)S(1)}, bf16[256,2048]{1,0:T(8,128)(2,1)S(1)}, u32[]{:S(2)}, u32[]{:S(2)}) %collective-permute-start.8) | collective-permute-done | bytes 1048608 | tf_op jit(solution)/shard_map/ppermute | solution.py:384
  40.2 1.7 %low.1.refs_2_ = bf16[64,128]{1,0:T(8,128)(2,1)S(1)} custom-call(bf16[128,2048]{1,0:T(8,128)(2,1)S(1)} %copy-done, bf16[128,128]{1,0:T(8,128)(2,1)S(1)} %copy-done.3, bf16[256,2048]{1,0:T(8,128)(2,1)S(1)} %bitcast.11, bf16[256,2048]{1,0:T(8,128)(2,1)S(1)} %collective-permute-done.3.refs_1_, bf16[256,2048]{1,0:T(8,128)(2,1)S(1)} %collective-permute-done.refs_2_, ...), custom_call_target="tpu_custom_call" | custom-call | flops 1024 | bytes 1024 | tf_op jit(solution)/shard_map/low/pallas_call | solution.py:335
  41.9 0.1 collective-permute-start.9
  41.9 3.3 %collective-permute-start.10 = (bf16[64,128]{1,0:T(8,128)(2,1)S(1)}, bf16[64,128]{1,0:T(8,128)(2,1)S(1)}, u32[]{:S(2)}, u32[]{:S(2)}) collective-permute-start(bf16[64,128]{1,0:T(8,128)(2,1)S(1)} %low.1.refs_2_), channel_id=1, source_target_pairs={{0,2},{1,3},{2,0},{3,1},{4,6},{5,7},{6,4},{7,5},{8,10},{9,11},{10,... | collective-permute-start | bytes 49160 | tf_op jit(solution)/shard_map/ppermute | solution.py:384
  45.2 1.1 %collective-permute-start.11 = (bf16[64,128]{1,0:T(8,128)(2,1)S(1)}, bf16[64,128]{1,0:T(8,128)(2,1)S(1)}, u32[]{:S(2)}, u32[]{:S(2)}) collective-permute-start(bf16[64,128]{1,0:T(8,128)(2,1)S(1)} %low.1.refs_2_), channel_id=1, source_target_pairs={{0,3},{1,2},{2,1},{3,0},{4,7},{5,6},{6,5},{7,4},{8,11},{9,10},{10,... | collective-permute-start | bytes 49160 | tf_op jit(solution)/shard_map/ppermute | solution.py:384
  46.3 0.8 %collective-permute-done.10.refs_4_ = bf16[64,128]{1,0:T(8,128)(2,1)S(1)} collective-permute-done((bf16[64,128]{1,0:T(8,128)(2,1)S(1)}, bf16[64,128]{1,0:T(8,128)(2,1)S(1)}, u32[]{:S(2)}, u32[]{:S(2)}) %collective-permute-start.10) | collective-permute-done | bytes 16416 | tf_op jit(solution)/shard_map/ppermute | solution.py:384
  47.1 3.7 %collective-permute-done.11.refs_5_ = bf16[64,128]{1,0:T(8,128)(2,1)S(1)} collective-permute-done((bf16[64,128]{1,0:T(8,128)(2,1)S(1)}, bf16[64,128]{1,0:T(8,128)(2,1)S(1)}, u32[]{:S(2)}, u32[]{:S(2)}) %collective-permute-start.11) | collective-permute-done | bytes 16416 | tf_op jit(solution)/shard_map/ppermute | solution.py:384
  50.8 1.5 %collective-permute-done.13.refs_11_ = bf16[128,1024]{1,0:T(8,128)(2,1)S(1)} collective-permute-done((bf16[128,1024]{1,0:T(8,128)(2,1)S(1)}, bf16[128,1024]{1,0:T(8,128)(2,1)S(1)}, u32[]{:S(2)}, u32[]{:S(2)}) %collective-permute-start.13) | collective-permute-done | bytes 262176 | tf_op jit(solution)/shard_map/ppermute | solution.py:384
  52.3 1.9 %combine.1 = bf16[64,2,1024]{2,1,0:T(2,128)(2,1)} custom-call(bf16[128,128]{1,0:T(8,128)(2,1)S(1)} %copy-done.3, f32[128,1024]{1,0:T(8,128)S(1)} %convert_add_fusion.refs_0_, bf16[128,1024]{1,0:T(8,128)(2,1)S(1)} %collective-permute-done.6.refs_1_, bf16[64,128]{1,0:T(8,128)(2,1)S(1)} %low.1.refs_2_, bf16[64,128]{1,0:T(8,128)(2,1)S(1)} %collective-permute-done.9.refs_3_, ...), custom_call_target="tpu_custom_call" | custom-call | flops 1024 | bytes 1024 | tf_op jit(solution)/shard_map/combine/pallas_call | solution.py:373
  (19 shorter events, 0.1 us)
Async XLA Ops:
  0.0 12.6 %collective-permute-start.3 = (bf16[256,2048]{1,0:T(8,128)(2,1)}, bf16[256,2048]{1,0:T(8,128)(2,1)S(1)}, u32[]{:S(2)}, u32[]{:S(2)}) collective-permute-start(bf16[256,2048]{1,0:T(8,128)(2,1)} %bitcast.9), channel_id=1, source_target_pairs={{0,4},{4,0},{8,12},{12,8},{1,5},{5,1},{9,13},{13,9},{2,6},{6,2},{1... | collective-permute-start | bytes 3145736 | tf_op jit(solution)/shard_map/ppermute | solution.py:384
  0.5 12.1 %collective-permute-start.2 = (bf16[256,1024]{1,0:T(8,128)(2,1)}, bf16[256,1024]{1,0:T(8,128)(2,1)S(1)}, u32[]{:S(2)}, u32[]{:S(2)}) collective-permute-start(bf16[256,1024]{1,0:T(8,128)(2,1)} %bitcast.7), channel_id=1, source_target_pairs={{0,4},{4,0},{8,12},{12,8},{1,5},{5,1},{9,13},{13,9},{2,6},{6,2},{1... | collective-permute-start | bytes 1572872 | tf_op jit(solution)/shard_map/ppermute | solution.py:384
  0.5 33.8 %collective-permute-start = (bf16[256,2048]{1,0:T(8,128)(2,1)}, bf16[256,2048]{1,0:T(8,128)(2,1)S(1)}, u32[]{:S(2)}, u32[]{:S(2)}) collective-permute-start(bf16[256,2048]{1,0:T(8,128)(2,1)} %bitcast.10), channel_id=1, source_target_pairs={{0,8},{4,12},{8,0},{12,4},{1,9},{5,13},{9,1},{13,5},{2,10},{6,14},... | collective-permute-start | bytes 3145736 | tf_op jit(solution)/shard_map/ppermute | solution.py:384
  12.6 9.8 %copy-start.1 = (bf16[4,64,1024]{2,1,0:T(8,128)(2,1)S(1)}, bf16[4,64,1024]{2,1,0:T(8,128)(2,1)}, u32[]{:S(2)}) copy-start(bf16[4,64,1024]{2,1,0:T(8,128)(2,1)} %param.19) | copy-start | bytes 1572868
  12.6 27.6 %copy-start = (bf16[128,2048]{1,0:T(8,128)(2,1)S(1)}, bf16[128,2048]{1,0:T(8,128)(2,1)}, u32[]{:S(2)}) copy-start(bf16[128,2048]{1,0:T(8,128)(2,1)} %get-tuple-element.33.refs_1_.attended) | copy-start | bytes 1572868
  12.6 27.6 %copy-start.2 = (bf16[4,64,2048]{2,1,0:T(8,128)(2,1)S(1)}, bf16[4,64,2048]{2,1,0:T(8,128)(2,1)}, u32[]{:S(2)}) copy-start(bf16[4,64,2048]{2,1,0:T(8,128)(2,1)} %param.18) | copy-start | bytes 3145732
  12.7 27.5 %copy-start.3 = (bf16[128,128]{1,0:T(8,128)(2,1)S(1)}, bf16[128,128]{1,0:T(8,128)(2,1)}, u32[]{:S(2)}) copy-start(bf16[128,128]{1,0:T(8,128)(2,1)} %get-tuple-element.30.marks) | copy-start | bytes 98308
  12.7 8.2 %collective-permute-start.4 = (bf16[128,1024]{1,0:T(8,128)(2,1)}, bf16[128,1024]{1,0:T(8,128)(2,1)S(1)}, u32[]{:S(2)}, u32[]{:S(2)}) collective-permute-start(bf16[128,1024]{1,0:T(8,128)(2,1)} %get-tuple-element.37), channel_id=1, source_target_pairs={{0,1},{1,0},{2,3},{3,2},{4,5},{5,4},{6,7},{7,6},{8,9},{9,8},{10,11... | collective-permute-start | bytes 786440 | tf_op jit(solution)/shard_map/ppermute | solution.py:384
  20.9 12.4 %collective-permute-start.5 = (bf16[128,1024]{1,0:T(8,128)(2,1)}, bf16[128,1024]{1,0:T(8,128)(2,1)S(1)}, u32[]{:S(2)}, u32[]{:S(2)}) collective-permute-start(bf16[128,1024]{1,0:T(8,128)(2,1)} %get-tuple-element.38), channel_id=1, source_target_pairs={{0,1},{1,0},{2,3},{3,2},{4,5},{5,4},{6,7},{7,6},{8,9},{9,8},{10,11... | collective-permute-start | bytes 786440 | tf_op jit(solution)/shard_map/ppermute | solution.py:384
  22.5 11.8 %collective-permute-start.1 = (bf16[128,1024]{1,0:T(8,128)(2,1)S(1)}, bf16[128,1024]{1,0:T(8,128)(2,1)S(1)}, u32[]{:S(2)}, u32[]{:S(2)}) collective-permute-start(bf16[128,1024]{1,0:T(8,128)(2,1)S(1)} %bitcast.13), channel_id=1, source_target_pairs={{0,8},{4,12},{8,0},{12,4},{1,9},{5,13},{9,1},{13,5},{2,10},{6,14},... | collective-permute-start | bytes 786440 | tf_op jit(solution)/shard_map/ppermute | solution.py:384
  24.1 13.4 %collective-permute-start.6 = (bf16[128,1024]{1,0:T(8,128)(2,1)S(1)}, bf16[128,1024]{1,0:T(8,128)(2,1)S(1)}, u32[]{:S(2)}, u32[]{:S(2)}) collective-permute-start(bf16[128,1024]{1,0:T(8,128)(2,1)S(1)} %add_convert_fusion), channel_id=1, source_target_pairs={{0,2},{1,3},{2,0},{3,1},{4,6},{5,7},{6,4},{7,5},{8,10},{9,11},{10,... | collective-permute-start | bytes 786440 | tf_op jit(solution)/shard_map/ppermute | solution.py:384
  37.5 2.7 %collective-permute-start.8 = (bf16[256,2048]{1,0:T(8,128)(2,1)S(1)}, bf16[256,2048]{1,0:T(8,128)(2,1)S(1)}, u32[]{:S(2)}, u32[]{:S(2)}) collective-permute-start(bf16[256,2048]{1,0:T(8,128)(2,1)S(1)} %collective-permute-done.refs_2_), channel_id=1, source_target_pairs={{0,4},{4,0},{8,12},{12,8},{1,5},{5,1},{9,13},{13,9},{2,6},{6,2},{1... | collective-permute-start | bytes 3145736 | tf_op jit(solution)/shard_map/ppermute | solution.py:384
  37.5 8.8 %collective-permute-start.7 = (bf16[128,1024]{1,0:T(8,128)(2,1)S(1)}, bf16[128,1024]{1,0:T(8,128)(2,1)S(1)}, u32[]{:S(2)}, u32[]{:S(2)}) collective-permute-start(bf16[128,1024]{1,0:T(8,128)(2,1)S(1)} %bitcast.12), channel_id=1, source_target_pairs={{0,8},{4,12},{8,0},{12,4},{1,9},{5,13},{9,1},{13,5},{2,10},{6,14},... | collective-permute-start | bytes 786440 | tf_op jit(solution)/shard_map/ppermute | solution.py:384
  41.9 4.5 %collective-permute-start.9 = (bf16[64,128]{1,0:T(8,128)(2,1)S(1)}, bf16[64,128]{1,0:T(8,128)(2,1)S(1)}, u32[]{:S(2)}, u32[]{:S(2)}) collective-permute-start(bf16[64,128]{1,0:T(8,128)(2,1)S(1)} %low.1.refs_2_), channel_id=1, source_target_pairs={{0,1},{1,0},{2,3},{3,2},{4,5},{5,4},{6,7},{7,6},{8,9},{9,8},{10,11... | collective-permute-start | bytes 49160 | tf_op jit(solution)/shard_map/ppermute | solution.py:384
  41.9 5.1 %collective-permute-start.10 = (bf16[64,128]{1,0:T(8,128)(2,1)S(1)}, bf16[64,128]{1,0:T(8,128)(2,1)S(1)}, u32[]{:S(2)}, u32[]{:S(2)}) collective-permute-start(bf16[64,128]{1,0:T(8,128)(2,1)S(1)} %low.1.refs_2_), channel_id=1, source_target_pairs={{0,2},{1,3},{2,0},{3,1},{4,6},{5,7},{6,4},{7,5},{8,10},{9,11},{10,... | collective-permute-start | bytes 49160 | tf_op jit(solution)/shard_map/ppermute | solution.py:384
  45.2 5.5 %collective-permute-start.11 = (bf16[64,128]{1,0:T(8,128)(2,1)S(1)}, bf16[64,128]{1,0:T(8,128)(2,1)S(1)}, u32[]{:S(2)}, u32[]{:S(2)}) collective-permute-start(bf16[64,128]{1,0:T(8,128)(2,1)S(1)} %low.1.refs_2_), channel_id=1, source_target_pairs={{0,3},{1,2},{2,1},{3,0},{4,7},{5,6},{6,5},{7,4},{8,11},{9,10},{10,... | collective-permute-start | bytes 49160 | tf_op jit(solution)/shard_map/ppermute | solution.py:384
  46.3 4.5 %collective-permute-start.12 = (bf16[128,1024]{1,0:T(8,128)(2,1)S(1)}, bf16[128,1024]{1,0:T(8,128)(2,1)S(1)}, u32[]{:S(2)}, u32[]{:S(2)}) collective-permute-start(bf16[128,1024]{1,0:T(8,128)(2,1)S(1)} %collective-permute-done.1.refs_8_), channel_id=1, source_target_pairs={{0,4},{4,0},{8,12},{12,8},{1,5},{5,1},{9,13},{13,9},{2,6},{6,2},{1... | collective-permute-start | bytes 786440 | tf_op jit(solution)/shard_map/ppermute | solution.py:384
  50.8 1.5 %collective-permute-start.13 = (bf16[128,1024]{1,0:T(8,128)(2,1)S(1)}, bf16[128,1024]{1,0:T(8,128)(2,1)S(1)}, u32[]{:S(2)}, u32[]{:S(2)}) collective-permute-start(bf16[128,1024]{1,0:T(8,128)(2,1)S(1)} %collective-permute-done.7.refs_9_), channel_id=1, source_target_pairs={{0,4},{4,0},{8,12},{12,8},{1,5},{5,1},{9,13},{13,9},{2,6},{6,2},{1... | collective-permute-start | bytes 786440 | tf_op jit(solution)/shard_map/ppermute | solution.py:384

commit v7 on v6

--- a/solution.py
+++ b/solution.py
@@ -450,12 +450,10 @@
         outward.append(swap(pair.astype(BF16), "tensor", k))
     near = swap(partials[1], "tensor", 1)
     near = near.astype(F32) + partials[0].astype(F32)
-    downs[top_bit], far_ups[0], near, outward = lax.optimization_barrier(
-        (downs[top_bit], far_ups[0], near, outward)
-    )
+    downs[top_bit], far_ups[0], inw = lax.optimization_barrier((downs[top_bit], far_ups[0], outward))
+    outward = inw
     forward(downs, "adapter", top_bit // 2)
-    last_ups = ups[0][cut:]
-    last_ups, near = lax.optimization_barrier((last_ups, near))
+    last_ups, outward = lax.optimization_barrier((ups[0][cut:], outward))
     far_ups.append({top_bit: swap(last_ups, "adapter", top_bit)})
     low = low_partial(attended, marks, [downs[k] for k in range(owners)], rank)
     low_parts = [low] + [swap(low, "tensor", k) for k in range(1, blocks)]

time: 54.4 us -> 54 us (level)
  starting transfers between devices: 15.9 us -> 13.5 us
  waiting for transfers between devices: 16.9 us -> 18.9 us
  Pallas kernels: 19.1 us -> 20.1 us
  other arithmetic: 2.02 us -> 1.12 us
    ppermute x14, starting transfers between devices: 15.9 us -> 13.5 us  [swap(): return lax.ppermute(value, axis, [(i, i ^ k) for i in range(count)])]
    ppermute x14, waiting for transfers between devices: 16.9 us -> 18.9 us  [swap(): return lax.ppermute(value, axis, [(i, i ^ k) for i in range(count)])]
    add x1, other arithmetic: 1.01 us -> 0.06 us  [body(): near = near.astype(F32) + partials[0].astype(F32)]
    pallas_call x1, Pallas kernels: 6.47 us -> 7.32 us  [project(): pl.pallas_call(functools.partial(project_kernel, count), grid_spec=pltpu....]
  transfers between devices with their start and end apart: 14 -> 14, of which waited for: 7 -> 6; matrix products, arithmetic and copies ran while one was open for 4% -> 2% of each run, Pallas kernels for 32% -> 34%
where the time goes in v7:
time: 54 us; the launch traced here: 53.8 us
  Pallas kernels  20.1 us (37%)
  waiting for transfers between devices  18.9 us (35%)
  starting transfers between devices  13.5 us (25%)
  other arithmetic  1.12 us (2%)
    ppermute x14, waiting for transfers between devices, swap(): return lax.ppermute(value, axis, [(i, i ^ k) for i in range(count)])  18.9 us
    ppermute x14, starting transfers between devices, swap(): return lax.ppermute(value, axis, [(i, i ^ k) for i in range(count)])  13.5 us
    pallas_call x1, Pallas kernels, attend(): pl.pallas_call(functools.partial(attend_kernel, blocks - 1, resident, blo...  9.27 us
    pallas_call x1, Pallas kernels, project(): pl.pallas_call(functools.partial(project_kernel, count), grid_spec=pltpu....  7.32 us
    pallas_call x1, Pallas kernels, combine(): pl.pallas_call(functools.partial(combine_kernel, 1 + len(partials), len(l...  1.86 us
    pallas_call x1, Pallas kernels, low_partial(): pl.pallas_call(functools.partial(low_kernel, rank), out_shape=jax.ShapeDt...  1.67 us
  transfers between devices with their start and end apart: 14, of which 6 were waited for; matrix products, arithmetic and copies ran while one was open for 2% of the time, Pallas kernels for 34%

profile of v7, /device:TPU:0, one launch (start us, length us, event | category | flops | bytes accessed | tf_op | source)
XLA Modules:
  0.0 53.8 jit_solution(10845914266292801034)
XLA Ops:
  0.0 0.5 collective-permute-start.1
  0.5 0.1 collective-permute-start
  0.5 2.9 %collective-permute-start.4 = (bf16[256,2048]{1,0:T(8,128)(2,1)}, bf16[256,2048]{1,0:T(8,128)(2,1)S(1)}, u32[]{:S(2)}, u32[]{:S(2)}) collective-permute-start(bf16[256,2048]{1,0:T(8,128)(2,1)} %bitcast.10), channel_id=1, source_target_pairs={{0,8},{4,12},{8,0},{12,4},{1,9},{5,13},{9,1},{13,5},{2,10},{6,14},... | collective-permute-start | bytes 3145736 | tf_op jit(solution)/shard_map/ppermute | solution.py:384
  3.5 9.3 %attend.1 = (bf16[128,2048]{1,0:T(8,128)(2,1)}, bf16[128,128]{1,0:T(8,128)(2,1)}, bf16[128,1024]{1,0:T(8,128)(2,1)}) custom-call(s32[64]{0:T(128)} %lengths.1, s32[1]{0:T(128)} %bitcast.place, s32[1]{0:T(128)} %bitcast.1.column.refs_0_, s32[1,64]{1,0:T(1,128)} %bitcast.14, bf16[64,2,2048]{2,1,0:T(2,128)(2,1)} %queries_hbm.1, ...), custom_call_target="tpu_custom_call" | custom-call | flops 1024 | bytes 1024 | tf_op jit(solution)/shard_map/attend/pallas_call | solution.py:220
  12.8 1.6 %collective-permute-start.2 = (bf16[128,1024]{1,0:T(8,128)(2,1)}, bf16[128,1024]{1,0:T(8,128)(2,1)S(1)}, u32[]{:S(2)}, u32[]{:S(2)}) collective-permute-start(bf16[128,1024]{1,0:T(8,128)(2,1)} %get-tuple-element.36), channel_id=1, source_target_pairs={{0,1},{1,0},{2,3},{3,2},{4,5},{5,4},{6,7},{7,6},{8,9},{9,8},{10,11... | collective-permute-start | bytes 786440 | tf_op jit(solution)/shard_map/ppermute | solution.py:384
  14.4 0.0 copy-start.2
  14.5 0.6 %collective-permute-start.5 = (bf16[128,1024]{1,0:T(8,128)(2,1)S(1)}, bf16[128,1024]{1,0:T(8,128)(2,1)S(1)}, u32[]{:S(2)}, u32[]{:S(2)}) collective-permute-start(bf16[128,1024]{1,0:T(8,128)(2,1)S(1)} %bitcast.13), channel_id=1, source_target_pairs={{0,8},{4,12},{8,0},{12,4},{1,9},{5,13},{9,1},{13,5},{2,10},{6,14},... | collective-permute-start | bytes 786440 | tf_op jit(solution)/shard_map/ppermute | solution.py:384
  15.1 7.3 %project.1 = (bf16[128,1024]{1,0:T(8,128)(2,1)}, bf16[128,1024]{1,0:T(8,128)(2,1)}, bf16[128,1024]{1,0:T(8,128)(2,1)}) custom-call(s32[1]{0:T(128)} %bitcast.1.column.refs_0_, bf16[128,2048]{1,0:T(8,128)(2,1)} %get-tuple-element.32.refs_1_.attended, bf16[2048,4096]{1,0:T(8,128)(2,1)} %refs_2_.1), custom_call_target="tpu_custom_call" | custom-call | flops 1024 | bytes 1024 | tf_op jit(solution)/shard_map/project/pallas_call | solution.py:297
  22.4 1.1 %add_convert_fusion = bf16[128,1024]{1,0:T(8,128)(2,1)S(1)} fusion(bf16[128,1024]{1,0:T(8,128)(2,1)S(1)} %collective-permute-done.2, bf16[128,1024]{1,0:T(8,128)(2,1)} %get-tuple-element.39), kind=kLoop, calls=%fused_computation | loop fusion | flops 524288 | bytes 786432 | tf_op jit(solution)/shard_map/convert_element_type | solution.py:450
  23.5 2.7 %collective-permute-start.6 = (bf16[128,1024]{1,0:T(8,128)(2,1)S(1)}, bf16[128,1024]{1,0:T(8,128)(2,1)S(1)}, u32[]{:S(2)}, u32[]{:S(2)}) collective-permute-start(bf16[128,1024]{1,0:T(8,128)(2,1)S(1)} %add_convert_fusion), channel_id=1, source_target_pairs={{0,2},{1,3},{2,0},{3,1},{4,6},{5,7},{6,4},{7,5},{8,10},{9,11},{10,... | collective-permute-start | bytes 786440 | tf_op jit(solution)/shard_map/ppermute | solution.py:384
  26.1 6.5 %collective-permute-done.5.refs_8_ = bf16[128,1024]{1,0:T(8,128)(2,1)S(1)} collective-permute-done((bf16[128,1024]{1,0:T(8,128)(2,1)S(1)}, bf16[128,1024]{1,0:T(8,128)(2,1)S(1)}, u32[]{:S(2)}, u32[]{:S(2)}) %collective-permute-start.5) | collective-permute-done | bytes 262176 | tf_op jit(solution)/shard_map/ppermute | solution.py:384
  32.6 4.7 %collective-permute-done.6.refs_1_ = bf16[128,1024]{1,0:T(8,128)(2,1)S(1)} collective-permute-done((bf16[128,1024]{1,0:T(8,128)(2,1)S(1)}, bf16[128,1024]{1,0:T(8,128)(2,1)S(1)}, u32[]{:S(2)}, u32[]{:S(2)}) %collective-permute-start.6) | collective-permute-done | bytes 262176 | tf_op jit(solution)/shard_map/ppermute | solution.py:384
  37.3 0.0 collective-permute-start.8
  37.3 0.7 %collective-permute-start.7 = (bf16[128,1024]{1,0:T(8,128)(2,1)S(1)}, bf16[128,1024]{1,0:T(8,128)(2,1)S(1)}, u32[]{:S(2)}, u32[]{:S(2)}) collective-permute-start(bf16[128,1024]{1,0:T(8,128)(2,1)S(1)} %bitcast.12), channel_id=1, source_target_pairs={{0,8},{4,12},{8,0},{12,4},{1,9},{5,13},{9,1},{13,5},{2,10},{6,14},... | collective-permute-start | bytes 786440 | tf_op jit(solution)/shard_map/ppermute | solution.py:384
  37.9 2.0 %collective-permute-done.8.refs_3_ = bf16[256,2048]{1,0:T(8,128)(2,1)S(1)} collective-permute-done((bf16[256,2048]{1,0:T(8,128)(2,1)S(1)}, bf16[256,2048]{1,0:T(8,128)(2,1)S(1)}, u32[]{:S(2)}, u32[]{:S(2)}) %collective-permute-start.8) | collective-permute-done | bytes 1048608 | tf_op jit(solution)/shard_map/ppermute | solution.py:384
  39.9 1.7 %low.1.refs_2_ = bf16[64,128]{1,0:T(8,128)(2,1)S(1)} custom-call(bf16[128,2048]{1,0:T(8,128)(2,1)S(1)} %copy-done, bf16[128,128]{1,0:T(8,128)(2,1)S(1)} %copy-done.3, bf16[256,2048]{1,0:T(8,128)(2,1)S(1)} %bitcast.11, bf16[256,2048]{1,0:T(8,128)(2,1)S(1)} %collective-permute-done.1.refs_1_, bf16[256,2048]{1,0:T(8,128)(2,1)S(1)} %collective-permute-done.4.refs_2_, ...), custom_call_target="tpu_custom_call" | custom-call | flops 1024 | bytes 1024 | tf_op jit(solution)/shard_map/low/pallas_call | solution.py:335
  41.6 0.1 collective-permute-start.9
  41.7 3.1 %collective-permute-start.10 = (bf16[64,128]{1,0:T(8,128)(2,1)S(1)}, bf16[64,128]{1,0:T(8,128)(2,1)S(1)}, u32[]{:S(2)}, u32[]{:S(2)}) collective-permute-start(bf16[64,128]{1,0:T(8,128)(2,1)S(1)} %low.1.refs_2_), channel_id=1, source_target_pairs={{0,2},{1,3},{2,0},{3,1},{4,6},{5,7},{6,4},{7,5},{8,10},{9,11},{10,... | collective-permute-start | bytes 49160 | tf_op jit(solution)/shard_map/ppermute | solution.py:384
  44.9 1.2 %collective-permute-start.11 = (bf16[64,128]{1,0:T(8,128)(2,1)S(1)}, bf16[64,128]{1,0:T(8,128)(2,1)S(1)}, u32[]{:S(2)}, u32[]{:S(2)}) collective-permute-start(bf16[64,128]{1,0:T(8,128)(2,1)S(1)} %low.1.refs_2_), channel_id=1, source_target_pairs={{0,3},{1,2},{2,1},{3,0},{4,7},{5,6},{6,5},{7,4},{8,11},{9,10},{10,... | collective-permute-start | bytes 49160 | tf_op jit(solution)/shard_map/ppermute | solution.py:384
  46.1 1.2 %collective-permute-done.9.refs_3_ = bf16[64,128]{1,0:T(8,128)(2,1)S(1)} collective-permute-done((bf16[64,128]{1,0:T(8,128)(2,1)S(1)}, bf16[64,128]{1,0:T(8,128)(2,1)S(1)}, u32[]{:S(2)}, u32[]{:S(2)}) %collective-permute-start.9) | collective-permute-done | bytes 16416 | tf_op jit(solution)/shard_map/ppermute | solution.py:384
  47.3 3.1 %collective-permute-done.11.refs_5_ = bf16[64,128]{1,0:T(8,128)(2,1)S(1)} collective-permute-done((bf16[64,128]{1,0:T(8,128)(2,1)S(1)}, bf16[64,128]{1,0:T(8,128)(2,1)S(1)}, u32[]{:S(2)}, u32[]{:S(2)}) %collective-permute-start.11) | collective-permute-done | bytes 16416 | tf_op jit(solution)/shard_map/ppermute | solution.py:384
  50.4 0.1 convert_add_fusion.refs_0_
  50.5 1.4 %collective-permute-done.13.refs_11_ = bf16[128,1024]{1,0:T(8,128)(2,1)S(1)} collective-permute-done((bf16[128,1024]{1,0:T(8,128)(2,1)S(1)}, bf16[128,1024]{1,0:T(8,128)(2,1)S(1)}, u32[]{:S(2)}, u32[]{:S(2)}) %collective-permute-start.13) | collective-permute-done | bytes 262176 | tf_op jit(solution)/shard_map/ppermute | solution.py:384
  51.9 1.9 %combine.1 = bf16[64,2,1024]{2,1,0:T(2,128)(2,1)} custom-call(bf16[128,128]{1,0:T(8,128)(2,1)S(1)} %copy-done.3, f32[128,1024]{1,0:T(8,128)S(1)} %convert_add_fusion.refs_0_, bf16[128,1024]{1,0:T(8,128)(2,1)S(1)} %collective-permute-done.6.refs_1_, bf16[64,128]{1,0:T(8,128)(2,1)S(1)} %low.1.refs_2_, bf16[64,128]{1,0:T(8,128)(2,1)S(1)} %collective-permute-done.9.refs_3_, ...), custom_call_target="tpu_custom_call" | custom-call | flops 1024 | bytes 1024 | tf_op jit(solution)/shard_map/combine/pallas_call | solution.py:373
  (21 shorter events, 0.1 us)
Async XLA Ops:
  0.0 12.7 %collective-permute-start.1 = (bf16[256,2048]{1,0:T(8,128)(2,1)}, bf16[256,2048]{1,0:T(8,128)(2,1)S(1)}, u32[]{:S(2)}, u32[]{:S(2)}) collective-permute-start(bf16[256,2048]{1,0:T(8,128)(2,1)} %bitcast.9), channel_id=1, source_target_pairs={{0,4},{4,0},{8,12},{12,8},{1,5},{5,1},{9,13},{13,9},{2,6},{6,2},{1... | collective-permute-start | bytes 3145736 | tf_op jit(solution)/shard_map/ppermute | solution.py:384
  0.5 12.3 %collective-permute-start = (bf16[256,1024]{1,0:T(8,128)(2,1)}, bf16[256,1024]{1,0:T(8,128)(2,1)S(1)}, u32[]{:S(2)}, u32[]{:S(2)}) collective-permute-start(bf16[256,1024]{1,0:T(8,128)(2,1)} %bitcast.7), channel_id=1, source_target_pairs={{0,4},{4,0},{8,12},{12,8},{1,5},{5,1},{9,13},{13,9},{2,6},{6,2},{1... | collective-permute-start | bytes 1572872 | tf_op jit(solution)/shard_map/ppermute | solution.py:384
  0.5 32.1 %collective-permute-start.4 = (bf16[256,2048]{1,0:T(8,128)(2,1)}, bf16[256,2048]{1,0:T(8,128)(2,1)S(1)}, u32[]{:S(2)}, u32[]{:S(2)}) collective-permute-start(bf16[256,2048]{1,0:T(8,128)(2,1)} %bitcast.10), channel_id=1, source_target_pairs={{0,8},{4,12},{8,0},{12,4},{1,9},{5,13},{9,1},{13,5},{2,10},{6,14},... | collective-permute-start | bytes 3145736 | tf_op jit(solution)/shard_map/ppermute | solution.py:384
  3.5 10.9 %copy-start.1 = (bf16[4,64,1024]{2,1,0:T(8,128)(2,1)S(1)}, bf16[4,64,1024]{2,1,0:T(8,128)(2,1)}, u32[]{:S(2)}) copy-start(bf16[4,64,1024]{2,1,0:T(8,128)(2,1)} %param.19) | copy-start | bytes 1572868
  12.8 9.7 %collective-permute-start.2 = (bf16[128,1024]{1,0:T(8,128)(2,1)}, bf16[128,1024]{1,0:T(8,128)(2,1)S(1)}, u32[]{:S(2)}, u32[]{:S(2)}) collective-permute-start(bf16[128,1024]{1,0:T(8,128)(2,1)} %get-tuple-element.36), channel_id=1, source_target_pairs={{0,1},{1,0},{2,3},{3,2},{4,5},{5,4},{6,7},{7,6},{8,9},{9,8},{10,11... | collective-permute-start | bytes 786440 | tf_op jit(solution)/shard_map/ppermute | solution.py:384
  14.4 25.5 %copy-start = (bf16[128,2048]{1,0:T(8,128)(2,1)S(1)}, bf16[128,2048]{1,0:T(8,128)(2,1)}, u32[]{:S(2)}) copy-start(bf16[128,2048]{1,0:T(8,128)(2,1)} %get-tuple-element.32.refs_1_.attended) | copy-start | bytes 1572868
  14.4 25.5 %copy-start.2 = (bf16[4,64,2048]{2,1,0:T(8,128)(2,1)S(1)}, bf16[4,64,2048]{2,1,0:T(8,128)(2,1)}, u32[]{:S(2)}) copy-start(bf16[4,64,2048]{2,1,0:T(8,128)(2,1)} %param.18) | copy-start | bytes 3145732
  14.5 25.5 %copy-start.3 = (bf16[128,128]{1,0:T(8,128)(2,1)S(1)}, bf16[128,128]{1,0:T(8,128)(2,1)}, u32[]{:S(2)}) copy-start(bf16[128,128]{1,0:T(8,128)(2,1)} %get-tuple-element.29.marks) | copy-start | bytes 98308
  14.5 18.1 %collective-permute-start.5 = (bf16[128,1024]{1,0:T(8,128)(2,1)S(1)}, bf16[128,1024]{1,0:T(8,128)(2,1)S(1)}, u32[]{:S(2)}, u32[]{:S(2)}) collective-permute-start(bf16[128,1024]{1,0:T(8,128)(2,1)S(1)} %bitcast.13), channel_id=1, source_target_pairs={{0,8},{4,12},{8,0},{12,4},{1,9},{5,13},{9,1},{13,5},{2,10},{6,14},... | collective-permute-start | bytes 786440 | tf_op jit(solution)/shard_map/ppermute | solution.py:384
  22.4 28.0 %copy-start.4 = (bf16[128,1024]{1,0:T(8,128)(2,1)S(1)}, bf16[128,1024]{1,0:T(8,128)(2,1)}, u32[]{:S(2)}) copy-start(bf16[128,1024]{1,0:T(8,128)(2,1)} %get-tuple-element.38) | copy-start | bytes 786436
  23.5 13.8 %collective-permute-start.6 = (bf16[128,1024]{1,0:T(8,128)(2,1)S(1)}, bf16[128,1024]{1,0:T(8,128)(2,1)S(1)}, u32[]{:S(2)}, u32[]{:S(2)}) collective-permute-start(bf16[128,1024]{1,0:T(8,128)(2,1)S(1)} %add_convert_fusion), channel_id=1, source_target_pairs={{0,2},{1,3},{2,0},{3,1},{4,6},{5,7},{6,4},{7,5},{8,10},{9,11},{10,... | collective-permute-start | bytes 786440 | tf_op jit(solution)/shard_map/ppermute | solution.py:384
  37.3 2.7 %collective-permute-start.8 = (bf16[256,2048]{1,0:T(8,128)(2,1)S(1)}, bf16[256,2048]{1,0:T(8,128)(2,1)S(1)}, u32[]{:S(2)}, u32[]{:S(2)}) collective-permute-start(bf16[256,2048]{1,0:T(8,128)(2,1)S(1)} %collective-permute-done.4.refs_2_), channel_id=1, source_target_pairs={{0,4},{4,0},{8,12},{12,8},{1,5},{5,1},{9,13},{13,9},{2,6},{6,2},{1... | collective-permute-start | bytes 3145736 | tf_op jit(solution)/shard_map/ppermute | solution.py:384
  37.3 8.8 %collective-permute-start.7 = (bf16[128,1024]{1,0:T(8,128)(2,1)S(1)}, bf16[128,1024]{1,0:T(8,128)(2,1)S(1)}, u32[]{:S(2)}, u32[]{:S(2)}) collective-permute-start(bf16[128,1024]{1,0:T(8,128)(2,1)S(1)} %bitcast.12), channel_id=1, source_target_pairs={{0,8},{4,12},{8,0},{12,4},{1,9},{5,13},{9,1},{13,5},{2,10},{6,14},... | collective-permute-start | bytes 786440 | tf_op jit(solution)/shard_map/ppermute | solution.py:384
  37.9 12.5 %collective-permute-start.3 = (bf16[128,1024]{1,0:T(8,128)(2,1)}, bf16[128,1024]{1,0:T(8,128)(2,1)S(1)}, u32[]{:S(2)}, u32[]{:S(2)}) collective-permute-start(bf16[128,1024]{1,0:T(8,128)(2,1)} %get-tuple-element.37), channel_id=1, source_target_pairs={{0,1},{1,0},{2,3},{3,2},{4,5},{5,4},{6,7},{7,6},{8,9},{9,8},{10,11... | collective-permute-start | bytes 786440 | tf_op jit(solution)/shard_map/ppermute | solution.py:384
  41.6 5.7 %collective-permute-start.9 = (bf16[64,128]{1,0:T(8,128)(2,1)S(1)}, bf16[64,128]{1,0:T(8,128)(2,1)S(1)}, u32[]{:S(2)}, u32[]{:S(2)}) collective-permute-start(bf16[64,128]{1,0:T(8,128)(2,1)S(1)} %low.1.refs_2_), channel_id=1, source_target_pairs={{0,1},{1,0},{2,3},{3,2},{4,5},{5,4},{6,7},{7,6},{8,9},{9,8},{10,11... | collective-permute-start | bytes 49160 | tf_op jit(solution)/shard_map/ppermute | solution.py:384
  41.7 5.6 %collective-permute-start.10 = (bf16[64,128]{1,0:T(8,128)(2,1)S(1)}, bf16[64,128]{1,0:T(8,128)(2,1)S(1)}, u32[]{:S(2)}, u32[]{:S(2)}) collective-permute-start(bf16[64,128]{1,0:T(8,128)(2,1)S(1)} %low.1.refs_2_), channel_id=1, source_target_pairs={{0,2},{1,3},{2,0},{3,1},{4,6},{5,7},{6,4},{7,5},{8,10},{9,11},{10,... | collective-permute-start | bytes 49160 | tf_op jit(solution)/shard_map/ppermute | solution.py:384
  44.9 5.5 %collective-permute-start.11 = (bf16[64,128]{1,0:T(8,128)(2,1)S(1)}, bf16[64,128]{1,0:T(8,128)(2,1)S(1)}, u32[]{:S(2)}, u32[]{:S(2)}) collective-permute-start(bf16[64,128]{1,0:T(8,128)(2,1)S(1)} %low.1.refs_2_), channel_id=1, source_target_pairs={{0,3},{1,2},{2,1},{3,0},{4,7},{5,6},{6,5},{7,4},{8,11},{9,10},{10,... | collective-permute-start | bytes 49160 | tf_op jit(solution)/shard_map/ppermute | solution.py:384
  46.1 4.4 %collective-permute-start.12 = (bf16[128,1024]{1,0:T(8,128)(2,1)S(1)}, bf16[128,1024]{1,0:T(8,128)(2,1)S(1)}, u32[]{:S(2)}, u32[]{:S(2)}) collective-permute-start(bf16[128,1024]{1,0:T(8,128)(2,1)S(1)} %collective-permute-done.5.refs_8_), channel_id=1, source_target_pairs={{0,4},{4,0},{8,12},{12,8},{1,5},{5,1},{9,13},{13,9},{2,6},{6,2},{1... | collective-permute-start | bytes 786440 | tf_op jit(solution)/shard_map/ppermute | solution.py:384
  50.4 1.5 %collective-permute-start.13 = (bf16[128,1024]{1,0:T(8,128)(2,1)S(1)}, bf16[128,1024]{1,0:T(8,128)(2,1)S(1)}, u32[]{:S(2)}, u32[]{:S(2)}) collective-permute-start(bf16[128,1024]{1,0:T(8,128)(2,1)S(1)} %collective-permute-done.7.refs_9_), channel_id=1, source_target_pairs={{0,4},{4,0},{8,12},{12,8},{1,5},{5,1},{9,13},{13,9},{2,6},{6,2},{1... | collective-permute-start | bytes 786440 | tf_op jit(solution)/shard_map/ppermute | solution.py:384

commit v8 on v7

--- a/solution.py
+++ b/solution.py
@@ -341,8 +341,8 @@
     )(attended, marks, *downs)
 
 
-def combine_kernel(sums, blocks, marks, *refs):
-    partials = refs[:sums]
+def combine_kernel(pairs, blocks, marks, own, *refs):
+    sums = 2 * pairs
     lows = refs[sums : sums + blocks]
     ups = refs[sums + blocks : -1]
     out = refs[-1]
@@ -353,9 +353,10 @@
     low = low.astype(BF16).astype(F32)
     low = jnp.concatenate([low[:, :rank], low[:, rank:]], axis=0)
     chosen = marks[...].astype(F32)
-    base = partials[0][...].astype(F32)
-    for part in partials[1:]:
-        base = base + part[...].astype(F32)
+    base = own[...]
+    for j in range(pairs):
+        both = jnp.concatenate([refs[2 * j][...], refs[2 * j + 1][...]], axis=0)
+        base = base + both.astype(F32)
     first = 0
     for up in ups:
         held = up.shape[0] // rank
@@ -367,11 +368,12 @@
     out[...] = base.reshape(out.shape).astype(BF16)
 
 
-def combine(marks, own, partials, lows, ups, steps):
+def combine(marks, own, halves, lows, ups, steps):
     rows, columns = own.shape
-    inputs = [marks, own, *partials, *lows, *ups]
+    split = [part for pair in halves for part in pair]
+    inputs = [marks, own, *split, *lows, *ups]
     return pl.pallas_call(
-        functools.partial(combine_kernel, 1 + len(partials), len(lows)),
+        functools.partial(combine_kernel, len(halves), len(lows)),
         out_shape=jax.ShapeDtypeStruct((rows // steps, steps, columns), BF16),
         compiler_params=pltpu.CompilerParams(vmem_limit_bytes=SMALL_VMEM),
         cost_estimate=SMALL_COST,
@@ -444,27 +446,32 @@
     for k in range(blocks - 3, 1, -2):
         inward[k] = swap(partials[k], "tensor", 1)
     partials, inward = lax.optimization_barrier((partials, inward))
-    outward = []
+    half = requests * steps // 2
+    top, bottom = [], []
     for k in range(2, blocks, 2):
         pair = partials[k].astype(F32) + inward[k + 1].astype(F32)
-        outward.append(swap(pair.astype(BF16), "tensor", k))
+        pair = pair.astype(BF16)
+        top.append(swap(pair[:half], "tensor", k))
+        bottom.append(swap(pair[half:], "tensor", k))
     near = swap(partials[1], "tensor", 1)
     near = near.astype(F32) + partials[0].astype(F32)
-    downs[top_bit], far_ups[0], inw = lax.optimization_barrier((downs[top_bit], far_ups[0], outward))
-    outward = inw
+    last_ups, far_ups[0] = lax.optimization_barrier((ups[0][cut:], far_ups[0]))
+    far_ups.append({top_bit: swap(last_ups, "adapter", top_bit)})
+    downs[top_bit], far_ups[0], top = lax.optimization_barrier(
+        (downs[top_bit], far_ups[0], top)
+    )
     forward(downs, "adapter", top_bit // 2)
-    last_ups, outward = lax.optimization_barrier((ups[0][cut:], outward))
-    far_ups.append({top_bit: swap(last_ups, "adapter", top_bit)})
+    forward(far_ups[0], "adapter", top_bit // 2)
     low = low_partial(attended, marks, [downs[k] for k in range(owners)], rank)
+    low, bottom, far_ups = lax.optimization_barrier((low, bottom, far_ups))
     low_parts = [low] + [swap(low, "tensor", k) for k in range(1, blocks)]
-    far_ups[1], low_parts = lax.optimization_barrier((far_ups[1], low_parts))
     forward(ups, "adapter", top_bit // 2)
     for held in far_ups:
         forward(held, "adapter", top_bit // 2)
     pieces = []
     for k in range(owners):
         pieces += [ups[k]] if k < top_bit else [held[k] for held in far_ups]
-    return combine(marks, near, outward, low_parts, pieces, steps)
+    return combine(marks, near, [*zip(top, bottom)], low_parts, pieces, steps)
 
 
 def solution(mesh):

time: 54 us -> 56.4 us (1.044)
  starting transfers between devices: 13.5 us -> 20.4 us
  waiting for transfers between devices: 18.9 us -> 14.3 us
    ppermute x14 -> x15, starting transfers between devices: 13.5 us -> 20.4 us  [swap(): return lax.ppermute(value, axis, [(i, i ^ k) for i in range(count)])]
    ppermute x14 -> x15, waiting for transfers between devices: 18.9 us -> 14.3 us  [swap(): return lax.ppermute(value, axis, [(i, i ^ k) for i in range(count)])]
  transfers between devices with their start and end apart: 14 -> 15, of which waited for: 6 -> 5; matrix products, arithmetic and copies ran while one was open for 2% -> 2% of each run, Pallas kernels for 34% -> 33%
where the time goes in v8:
time: 56.4 us; the launch traced here: 56.2 us
  starting transfers between devices  20.4 us (36%)
  Pallas kernels  20.2 us (36%)
  waiting for transfers between devices  14.3 us (25%)
  other arithmetic  1.12 us (2%)
    ppermute x15, starting transfers between devices, swap(): return lax.ppermute(value, axis, [(i, i ^ k) for i in range(count)])  20.4 us
    ppermute x15, waiting for transfers between devices, swap(): return lax.ppermute(value, axis, [(i, i ^ k) for i in range(count)])  14.3 us
    pallas_call x1, Pallas kernels, attend(): pl.pallas_call(functools.partial(attend_kernel, blocks - 1, resident, blo...  9.27 us
    pallas_call x1, Pallas kernels, project(): pl.pallas_call(functools.partial(project_kernel, count), grid_spec=pltpu....  7.34 us
    pallas_call x1, Pallas kernels, combine(): pl.pallas_call(functools.partial(combine_kernel, len(halves), len(lows)),...  1.87 us
    pallas_call x1, Pallas kernels, low_partial(): pl.pallas_call(functools.partial(low_kernel, rank), out_shape=jax.ShapeDt...  1.68 us
  transfers between devices with their start and end apart: 15, of which 5 were waited for; matrix products, arithmetic and copies ran while one was open for 2% of the time, Pallas kernels for 33%

profile of v8, /device:TPU:0, one launch (start us, length us, event | category | flops | bytes accessed | tf_op | source)
XLA Modules:
  0.0 56.2 jit_solution(303597488145957508)
XLA Ops:
  0.0 0.5 collective-permute-start.1
  0.5 0.1 collective-permute-start
  0.5 2.9 %collective-permute-start.4 = (bf16[256,2048]{1,0:T(8,128)(2,1)}, bf16[256,2048]{1,0:T(8,128)(2,1)S(1)}, u32[]{:S(2)}, u32[]{:S(2)}) collective-permute-start(bf16[256,2048]{1,0:T(8,128)(2,1)} %bitcast.10), channel_id=1, source_target_pairs={{0,8},{4,12},{8,0},{12,4},{1,9},{5,13},{9,1},{13,5},{2,10},{6,14},... | collective-permute-start | bytes 3145736 | tf_op jit(solution)/shard_map/ppermute | solution.py:386
  3.5 9.3 %attend.1 = (bf16[128,2048]{1,0:T(8,128)(2,1)}, bf16[128,128]{1,0:T(8,128)(2,1)}, bf16[128,1024]{1,0:T(8,128)(2,1)}) custom-call(s32[64]{0:T(128)} %lengths.1, s32[1]{0:T(128)} %bitcast.place, s32[1]{0:T(128)} %bitcast.1.column.refs_0_, s32[1,64]{1,0:T(1,128)} %bitcast.14, bf16[64,2,2048]{2,1,0:T(2,128)(2,1)} %queries_hbm.1, ...), custom_call_target="tpu_custom_call" | custom-call | flops 1024 | bytes 1024 | tf_op jit(solution)/shard_map/attend/pallas_call | solution.py:220
  12.8 1.6 %collective-permute-start.2 = (bf16[128,1024]{1,0:T(8,128)(2,1)}, bf16[128,1024]{1,0:T(8,128)(2,1)S(1)}, u32[]{:S(2)}, u32[]{:S(2)}) collective-permute-start(bf16[128,1024]{1,0:T(8,128)(2,1)} %get-tuple-element.36), channel_id=1, source_target_pairs={{0,1},{1,0},{2,3},{3,2},{4,5},{5,4},{6,7},{7,6},{8,9},{9,8},{10,11... | collective-permute-start | bytes 786440 | tf_op jit(solution)/shard_map/ppermute | solution.py:386
  14.4 0.0 copy-start.2
  14.5 0.6 %collective-permute-start.5 = (bf16[128,1024]{1,0:T(8,128)(2,1)S(1)}, bf16[128,1024]{1,0:T(8,128)(2,1)S(1)}, u32[]{:S(2)}, u32[]{:S(2)}) collective-permute-start(bf16[128,1024]{1,0:T(8,128)(2,1)S(1)} %bitcast.13), channel_id=1, source_target_pairs={{0,8},{4,12},{8,0},{12,4},{1,9},{5,13},{9,1},{13,5},{2,10},{6,14},... | collective-permute-start | bytes 786440 | tf_op jit(solution)/shard_map/ppermute | solution.py:386
  15.1 7.3 %project.1 = (bf16[128,1024]{1,0:T(8,128)(2,1)}, bf16[128,1024]{1,0:T(8,128)(2,1)}, bf16[128,1024]{1,0:T(8,128)(2,1)}) custom-call(s32[1]{0:T(128)} %bitcast.1.column.refs_0_, bf16[128,2048]{1,0:T(8,128)(2,1)} %get-tuple-element.32.refs_1_.attended, bf16[2048,4096]{1,0:T(8,128)(2,1)} %refs_2_.1), custom_call_target="tpu_custom_call" | custom-call | flops 1024 | bytes 1024 | tf_op jit(solution)/shard_map/project/pallas_call | solution.py:297
  22.4 1.1 %add_convert_fusion = bf16[128,1024]{1,0:T(8,128)(2,1)S(1)} fusion(bf16[128,1024]{1,0:T(8,128)(2,1)S(1)} %collective-permute-done.2, bf16[128,1024]{1,0:T(8,128)(2,1)} %get-tuple-element.40), kind=kLoop, calls=%fused_computation | loop fusion | flops 524288 | bytes 786432 | tf_op jit(solution)/shard_map/convert_element_type | solution.py:453
  23.5 2.7 %collective-permute-start.6 = (bf16[64,1024]{1,0:T(8,128)(2,1)S(1)}, bf16[64,1024]{1,0:T(8,128)(2,1)S(1)}, u32[]{:S(2)}, u32[]{:S(2)}) collective-permute-start(bf16[64,1024]{1,0:T(8,128)(2,1)S(1)} %get-tuple-element.56), channel_id=1, source_target_pairs={{0,2},{1,3},{2,0},{3,1},{4,6},{5,7},{6,4},{7,5},{8,10},{9,11},{10,... | collective-permute-start | bytes 393224 | tf_op jit(solution)/shard_map/ppermute | solution.py:386
  26.2 6.4 %collective-permute-done.5.refs_8_ = bf16[128,1024]{1,0:T(8,128)(2,1)S(1)} collective-permute-done((bf16[128,1024]{1,0:T(8,128)(2,1)S(1)}, bf16[128,1024]{1,0:T(8,128)(2,1)S(1)}, u32[]{:S(2)}, u32[]{:S(2)}) %collective-permute-start.5) | collective-permute-done | bytes 262176 | tf_op jit(solution)/shard_map/ppermute | solution.py:386
  32.6 1.8 %collective-permute-start.10 = (bf16[128,1024]{1,0:T(8,128)(2,1)S(1)}, bf16[128,1024]{1,0:T(8,128)(2,1)S(1)}, u32[]{:S(2)}, u32[]{:S(2)}) collective-permute-start(bf16[128,1024]{1,0:T(8,128)(2,1)S(1)} %bitcast.12), channel_id=1, source_target_pairs={{0,8},{4,12},{8,0},{12,4},{1,9},{5,13},{9,1},{13,5},{2,10},{6,14},... | collective-permute-start | bytes 786440 | tf_op jit(solution)/shard_map/ppermute | solution.py:386
  34.4 0.2 collective-permute-start.9
  34.6 1.6 %collective-permute-start.3 = (bf16[128,1024]{1,0:T(8,128)(2,1)}, bf16[128,1024]{1,0:T(8,128)(2,1)S(1)}, u32[]{:S(2)}, u32[]{:S(2)}) collective-permute-start(bf16[128,1024]{1,0:T(8,128)(2,1)} %get-tuple-element.37), channel_id=1, source_target_pairs={{0,1},{1,0},{2,3},{3,2},{4,5},{5,4},{6,7},{7,6},{8,9},{9,8},{10,11... | collective-permute-start | bytes 786440 | tf_op jit(solution)/shard_map/ppermute | solution.py:386
  36.2 2.6 %collective-permute-start.8 = (bf16[64,1024]{1,0:T(8,128)(2,1)S(1)}, bf16[64,1024]{1,0:T(8,128)(2,1)S(1)}, u32[]{:S(2)}, u32[]{:S(2)}) collective-permute-start(bf16[64,1024]{1,0:T(8,128)(2,1)S(1)} %get-tuple-element.55), channel_id=1, source_target_pairs={{0,2},{1,3},{2,0},{3,1},{4,6},{5,7},{6,4},{7,5},{8,10},{9,11},{10,... | collective-permute-start | bytes 393224 | tf_op jit(solution)/shard_map/ppermute | solution.py:386
  38.8 1.7 %low.1.refs_2_ = bf16[64,128]{1,0:T(8,128)(2,1)S(1)} custom-call(bf16[128,2048]{1,0:T(8,128)(2,1)S(1)} %copy-done, bf16[128,128]{1,0:T(8,128)(2,1)S(1)} %copy-done.3, bf16[256,2048]{1,0:T(8,128)(2,1)S(1)} %bitcast.11, bf16[256,2048]{1,0:T(8,128)(2,1)S(1)} %collective-permute-done.1.refs_1_, bf16[256,2048]{1,0:T(8,128)(2,1)S(1)} %collective-permute-done.4.refs_2_, ...), custom_call_target="tpu_custom_call" | custom-call | flops 1024 | bytes 1024 | tf_op jit(solution)/shard_map/low/pallas_call | solution.py:335
  40.5 0.9 %collective-permute-done.10.refs_9_ = bf16[128,1024]{1,0:T(8,128)(2,1)S(1)} collective-permute-done((bf16[128,1024]{1,0:T(8,128)(2,1)S(1)}, bf16[128,1024]{1,0:T(8,128)(2,1)S(1)}, u32[]{:S(2)}, u32[]{:S(2)}) %collective-permute-start.10) | collective-permute-done | bytes 262176 | tf_op jit(solution)/shard_map/ppermute | solution.py:386
  41.3 3.9 %collective-permute-done.8.refs_1_ = bf16[64,1024]{1,0:T(8,128)(2,1)S(1)} collective-permute-done((bf16[64,1024]{1,0:T(8,128)(2,1)S(1)}, bf16[64,1024]{1,0:T(8,128)(2,1)S(1)}, u32[]{:S(2)}, u32[]{:S(2)}) %collective-permute-start.8) | collective-permute-done | bytes 131104 | tf_op jit(solution)/shard_map/ppermute | solution.py:386
  45.3 3.5 %collective-permute-start.11 = (bf16[64,128]{1,0:T(8,128)(2,1)S(1)}, bf16[64,128]{1,0:T(8,128)(2,1)S(1)}, u32[]{:S(2)}, u32[]{:S(2)}) collective-permute-start(bf16[64,128]{1,0:T(8,128)(2,1)S(1)} %low.1.refs_2_), channel_id=1, source_target_pairs={{0,1},{1,0},{2,3},{3,2},{4,5},{5,4},{6,7},{7,6},{8,9},{9,8},{10,11... | collective-permute-start | bytes 49160 | tf_op jit(solution)/shard_map/ppermute | solution.py:386
  48.8 2.4 %collective-permute-start.13 = (bf16[64,128]{1,0:T(8,128)(2,1)S(1)}, bf16[64,128]{1,0:T(8,128)(2,1)S(1)}, u32[]{:S(2)}, u32[]{:S(2)}) collective-permute-start(bf16[64,128]{1,0:T(8,128)(2,1)S(1)} %low.1.refs_2_), channel_id=1, source_target_pairs={{0,3},{1,2},{2,1},{3,0},{4,7},{5,6},{6,5},{7,4},{8,11},{9,10},{10,... | collective-permute-start | bytes 49160 | tf_op jit(solution)/shard_map/ppermute | solution.py:386
  51.2 0.1 convert_add_fusion.own
  51.3 2.3 %collective-permute-done.12.refs_4_ = bf16[64,128]{1,0:T(8,128)(2,1)S(1)} collective-permute-done((bf16[64,128]{1,0:T(8,128)(2,1)S(1)}, bf16[64,128]{1,0:T(8,128)(2,1)S(1)}, u32[]{:S(2)}, u32[]{:S(2)}) %collective-permute-start.12) | collective-permute-done | bytes 16416 | tf_op jit(solution)/shard_map/ppermute | solution.py:386
  53.6 0.7 %collective-permute-done.13.refs_5_ = bf16[64,128]{1,0:T(8,128)(2,1)S(1)} collective-permute-done((bf16[64,128]{1,0:T(8,128)(2,1)S(1)}, bf16[64,128]{1,0:T(8,128)(2,1)S(1)}, u32[]{:S(2)}, u32[]{:S(2)}) %collective-permute-start.13) | collective-permute-done | bytes 16416 | tf_op jit(solution)/shard_map/ppermute | solution.py:386
  54.3 1.9 %combine.1 = bf16[64,2,1024]{2,1,0:T(2,128)(2,1)} custom-call(bf16[128,128]{1,0:T(8,128)(2,1)S(1)} %copy-done.3, f32[128,1024]{1,0:T(8,128)S(1)} %convert_add_fusion.own, bf16[64,1024]{1,0:T(8,128)(2,1)S(1)} %collective-permute-done.6.refs_0_, bf16[64,1024]{1,0:T(8,128)(2,1)S(1)} %collective-permute-done.8.refs_1_, bf16[64,128]{1,0:T(8,128)(2,1)S(1)} %low.1.refs_2_, ...), custom_call_target="tpu_custom_call" | custom-call | flops 1024 | bytes 1024 | tf_op jit(solution)/shard_map/combine/pallas_call | solution.py:375
  (24 shorter events, 0.1 us)
Async XLA Ops:
  0.0 12.7 %collective-permute-start.1 = (bf16[256,2048]{1,0:T(8,128)(2,1)}, bf16[256,2048]{1,0:T(8,128)(2,1)S(1)}, u32[]{:S(2)}, u32[]{:S(2)}) collective-permute-start(bf16[256,2048]{1,0:T(8,128)(2,1)} %bitcast.9), channel_id=1, source_target_pairs={{0,4},{4,0},{8,12},{12,8},{1,5},{5,1},{9,13},{13,9},{2,6},{6,2},{1... | collective-permute-start | bytes 3145736 | tf_op jit(solution)/shard_map/ppermute | solution.py:386
  0.5 12.3 %collective-permute-start = (bf16[256,1024]{1,0:T(8,128)(2,1)}, bf16[256,1024]{1,0:T(8,128)(2,1)S(1)}, u32[]{:S(2)}, u32[]{:S(2)}) collective-permute-start(bf16[256,1024]{1,0:T(8,128)(2,1)} %bitcast.7), channel_id=1, source_target_pairs={{0,4},{4,0},{8,12},{12,8},{1,5},{5,1},{9,13},{13,9},{2,6},{6,2},{1... | collective-permute-start | bytes 1572872 | tf_op jit(solution)/shard_map/ppermute | solution.py:386
  0.5 32.1 %collective-permute-start.4 = (bf16[256,2048]{1,0:T(8,128)(2,1)}, bf16[256,2048]{1,0:T(8,128)(2,1)S(1)}, u32[]{:S(2)}, u32[]{:S(2)}) collective-permute-start(bf16[256,2048]{1,0:T(8,128)(2,1)} %bitcast.10), channel_id=1, source_target_pairs={{0,8},{4,12},{8,0},{12,4},{1,9},{5,13},{9,1},{13,5},{2,10},{6,14},... | collective-permute-start | bytes 3145736 | tf_op jit(solution)/shard_map/ppermute | solution.py:386
  3.5 10.9 %copy-start.1 = (bf16[4,64,1024]{2,1,0:T(8,128)(2,1)S(1)}, bf16[4,64,1024]{2,1,0:T(8,128)(2,1)}, u32[]{:S(2)}) copy-start(bf16[4,64,1024]{2,1,0:T(8,128)(2,1)} %param.19) | copy-start | bytes 1572868
  12.8 9.7 %collective-permute-start.2 = (bf16[128,1024]{1,0:T(8,128)(2,1)}, bf16[128,1024]{1,0:T(8,128)(2,1)S(1)}, u32[]{:S(2)}, u32[]{:S(2)}) collective-permute-start(bf16[128,1024]{1,0:T(8,128)(2,1)} %get-tuple-element.36), channel_id=1, source_target_pairs={{0,1},{1,0},{2,3},{3,2},{4,5},{5,4},{6,7},{7,6},{8,9},{9,8},{10,11... | collective-permute-start | bytes 786440 | tf_op jit(solution)/shard_map/ppermute | solution.py:386
  14.4 24.3 %copy-start = (bf16[128,2048]{1,0:T(8,128)(2,1)S(1)}, bf16[128,2048]{1,0:T(8,128)(2,1)}, u32[]{:S(2)}) copy-start(bf16[128,2048]{1,0:T(8,128)(2,1)} %get-tuple-element.32.refs_1_.attended) | copy-start | bytes 1572868
  14.4 24.3 %copy-start.2 = (bf16[4,64,2048]{2,1,0:T(8,128)(2,1)S(1)}, bf16[4,64,2048]{2,1,0:T(8,128)(2,1)}, u32[]{:S(2)}) copy-start(bf16[4,64,2048]{2,1,0:T(8,128)(2,1)} %param.18) | copy-start | bytes 3145732
  14.5 24.3 %copy-start.3 = (bf16[128,128]{1,0:T(8,128)(2,1)S(1)}, bf16[128,128]{1,0:T(8,128)(2,1)}, u32[]{:S(2)}) copy-start(bf16[128,128]{1,0:T(8,128)(2,1)} %get-tuple-element.29.marks) | copy-start | bytes 98308
  14.5 18.1 %collective-permute-start.5 = (bf16[128,1024]{1,0:T(8,128)(2,1)S(1)}, bf16[128,1024]{1,0:T(8,128)(2,1)S(1)}, u32[]{:S(2)}, u32[]{:S(2)}) collective-permute-start(bf16[128,1024]{1,0:T(8,128)(2,1)S(1)} %bitcast.13), channel_id=1, source_target_pairs={{0,8},{4,12},{8,0},{12,4},{1,9},{5,13},{9,1},{13,5},{2,10},{6,14},... | collective-permute-start | bytes 786440 | tf_op jit(solution)/shard_map/ppermute | solution.py:386
  22.4 28.8 %copy-start.4 = (bf16[128,1024]{1,0:T(8,128)(2,1)S(1)}, bf16[128,1024]{1,0:T(8,128)(2,1)}, u32[]{:S(2)}) copy-start(bf16[128,1024]{1,0:T(8,128)(2,1)} %get-tuple-element.38) | copy-start | bytes 786436
  23.5 9.1 %collective-permute-start.6 = (bf16[64,1024]{1,0:T(8,128)(2,1)S(1)}, bf16[64,1024]{1,0:T(8,128)(2,1)S(1)}, u32[]{:S(2)}, u32[]{:S(2)}) collective-permute-start(bf16[64,1024]{1,0:T(8,128)(2,1)S(1)} %get-tuple-element.56), channel_id=1, source_target_pairs={{0,2},{1,3},{2,0},{3,1},{4,6},{5,7},{6,4},{7,5},{8,10},{9,11},{10,... | collective-permute-start | bytes 393224 | tf_op jit(solution)/shard_map/ppermute | solution.py:386
  32.6 6.1 %collective-permute-start.7 = (bf16[256,2048]{1,0:T(8,128)(2,1)S(1)}, bf16[256,2048]{1,0:T(8,128)(2,1)S(1)}, u32[]{:S(2)}, u32[]{:S(2)}) collective-permute-start(bf16[256,2048]{1,0:T(8,128)(2,1)S(1)} %collective-permute-done.4.refs_2_), channel_id=1, source_target_pairs={{0,4},{4,0},{8,12},{12,8},{1,5},{5,1},{9,13},{13,9},{2,6},{6,2},{1... | collective-permute-start | bytes 3145736 | tf_op jit(solution)/shard_map/ppermute | solution.py:386
  32.6 8.7 %collective-permute-start.10 = (bf16[128,1024]{1,0:T(8,128)(2,1)S(1)}, bf16[128,1024]{1,0:T(8,128)(2,1)S(1)}, u32[]{:S(2)}, u32[]{:S(2)}) collective-permute-start(bf16[128,1024]{1,0:T(8,128)(2,1)S(1)} %bitcast.12), channel_id=1, source_target_pairs={{0,8},{4,12},{8,0},{12,4},{1,9},{5,13},{9,1},{13,5},{2,10},{6,14},... | collective-permute-start | bytes 786440 | tf_op jit(solution)/shard_map/ppermute | solution.py:386
  34.4 10.8 %collective-permute-start.9 = (bf16[128,1024]{1,0:T(8,128)(2,1)S(1)}, bf16[128,1024]{1,0:T(8,128)(2,1)S(1)}, u32[]{:S(2)}, u32[]{:S(2)}) collective-permute-start(bf16[128,1024]{1,0:T(8,128)(2,1)S(1)} %collective-permute-done.5.refs_8_), channel_id=1, source_target_pairs={{0,4},{4,0},{8,12},{12,8},{1,5},{5,1},{9,13},{13,9},{2,6},{6,2},{1... | collective-permute-start | bytes 786440 | tf_op jit(solution)/shard_map/ppermute | solution.py:386
  34.6 16.6 %collective-permute-start.3 = (bf16[128,1024]{1,0:T(8,128)(2,1)}, bf16[128,1024]{1,0:T(8,128)(2,1)S(1)}, u32[]{:S(2)}, u32[]{:S(2)}) collective-permute-start(bf16[128,1024]{1,0:T(8,128)(2,1)} %get-tuple-element.37), channel_id=1, source_target_pairs={{0,1},{1,0},{2,3},{3,2},{4,5},{5,4},{6,7},{7,6},{8,9},{9,8},{10,11... | collective-permute-start | bytes 786440 | tf_op jit(solution)/shard_map/ppermute | solution.py:386
  36.2 9.1 %collective-permute-start.8 = (bf16[64,1024]{1,0:T(8,128)(2,1)S(1)}, bf16[64,1024]{1,0:T(8,128)(2,1)S(1)}, u32[]{:S(2)}, u32[]{:S(2)}) collective-permute-start(bf16[64,1024]{1,0:T(8,128)(2,1)S(1)} %get-tuple-element.55), channel_id=1, source_target_pairs={{0,2},{1,3},{2,0},{3,1},{4,6},{5,7},{6,4},{7,5},{8,10},{9,11},{10,... | collective-permute-start | bytes 393224 | tf_op jit(solution)/shard_map/ppermute | solution.py:386
  45.3 9.0 %collective-permute-start.14 = (bf16[128,1024]{1,0:T(8,128)(2,1)S(1)}, bf16[128,1024]{1,0:T(8,128)(2,1)S(1)}, u32[]{:S(2)}, u32[]{:S(2)}) collective-permute-start(bf16[128,1024]{1,0:T(8,128)(2,1)S(1)} %collective-permute-done.10.refs_9_), channel_id=1, source_target_pairs={{0,4},{4,0},{8,12},{12,8},{1,5},{5,1},{9,13},{13,9},{2,6},{6,2},{1... | collective-permute-start | bytes 786440 | tf_op jit(solution)/shard_map/ppermute | solution.py:386
  45.3 6.0 %collective-permute-start.11 = (bf16[64,128]{1,0:T(8,128)(2,1)S(1)}, bf16[64,128]{1,0:T(8,128)(2,1)S(1)}, u32[]{:S(2)}, u32[]{:S(2)}) collective-permute-start(bf16[64,128]{1,0:T(8,128)(2,1)S(1)} %low.1.refs_2_), channel_id=1, source_target_pairs={{0,1},{1,0},{2,3},{3,2},{4,5},{5,4},{6,7},{7,6},{8,9},{9,8},{10,11... | collective-permute-start | bytes 49160 | tf_op jit(solution)/shard_map/ppermute | solution.py:386
  48.8 4.8 %collective-permute-start.12 = (bf16[64,128]{1,0:T(8,128)(2,1)S(1)}, bf16[64,128]{1,0:T(8,128)(2,1)S(1)}, u32[]{:S(2)}, u32[]{:S(2)}) collective-permute-start(bf16[64,128]{1,0:T(8,128)(2,1)S(1)} %low.1.refs_2_), channel_id=1, source_target_pairs={{0,2},{1,3},{2,0},{3,1},{4,6},{5,7},{6,4},{7,5},{8,10},{9,11},{10,... | collective-permute-start | bytes 49160 | tf_op jit(solution)/shard_map/ppermute | solution.py:386
  48.8 5.5 %collective-permute-start.13 = (bf16[64,128]{1,0:T(8,128)(2,1)S(1)}, bf16[64,128]{1,0:T(8,128)(2,1)S(1)}, u32[]{:S(2)}, u32[]{:S(2)}) collective-permute-start(bf16[64,128]{1,0:T(8,128)(2,1)S(1)} %low.1.refs_2_), channel_id=1, source_target_pairs={{0,3},{1,2},{2,1},{3,0},{4,7},{5,6},{6,5},{7,4},{8,11},{9,10},{10,... | collective-permute-start | bytes 49160 | tf_op jit(solution)/shard_map/ppermute | solution.py:386

commit v9 on v7

--- a/solution.py
+++ b/solution.py
@@ -415,7 +415,7 @@
     ups = {0: adapter_up_weight.reshape(resident * rank, columns)}
     downs = {0: adapter_down_weight.reshape(resident * rank, -1)}
     downs[top_bit] = swap(downs[0], "adapter", top_bit)
-    cut = resident * rank // 2
+    cut = (resident - 1) * rank
     far_ups = [{top_bit: swap(ups[0][:cut], "adapter", top_bit)}]
     for held in (downs, ups):
         held[1] = swap(held[0], "adapter", 1)
@@ -456,8 +456,8 @@
     last_ups, outward = lax.optimization_barrier((ups[0][cut:], outward))
     far_ups.append({top_bit: swap(last_ups, "adapter", top_bit)})
     low = low_partial(attended, marks, [downs[k] for k in range(owners)], rank)
+    far_ups, low = lax.optimization_barrier((far_ups, low))
     low_parts = [low] + [swap(low, "tensor", k) for k in range(1, blocks)]
-    far_ups[1], low_parts = lax.optimization_barrier((far_ups[1], low_parts))
     forward(ups, "adapter", top_bit // 2)
     for held in far_ups:
         forward(held, "adapter", top_bit // 2)

time: 54 us -> 51.8 us (0.959)
  waiting for transfers between devices: 18.9 us -> 16.9 us
    ppermute x14, waiting for transfers between devices: 18.9 us -> 16.9 us  [swap(): return lax.ppermute(value, axis, [(i, i ^ k) for i in range(count)])]
  transfers between devices with their start and end apart: 14 -> 14, of which waited for: 6 -> 6; matrix products, arithmetic and copies ran while one was open for 2% -> 2% of each run, Pallas kernels for 34% -> 35%
where the time goes in v9:
time: 51.8 us; the launch traced here: 51.6 us
  Pallas kernels  20 us (39%)
  waiting for transfers between devices  16.9 us (33%)
  starting transfers between devices  13.4 us (26%)
  other arithmetic  1.12 us (2%)
    ppermute x14, waiting for transfers between devices, swap(): return lax.ppermute(value, axis, [(i, i ^ k) for i in range(count)])  16.9 us
    ppermute x14, starting transfers between devices, swap(): return lax.ppermute(value, axis, [(i, i ^ k) for i in range(count)])  13.4 us
    pallas_call x1, Pallas kernels, attend(): pl.pallas_call(functools.partial(attend_kernel, blocks - 1, resident, blo...  9.27 us
    pallas_call x1, Pallas kernels, project(): pl.pallas_call(functools.partial(project_kernel, count), grid_spec=pltpu....  7.34 us
    pallas_call x1, Pallas kernels, combine(): pl.pallas_call(functools.partial(combine_kernel, 1 + len(partials), len(l...  1.75 us
    pallas_call x1, Pallas kernels, low_partial(): pl.pallas_call(functools.partial(low_kernel, rank), out_shape=jax.ShapeDt...  1.68 us
    convert_element_type x1, other arithmetic, body(): outward.append(swap(pair.astype(BF16), 'tensor', k))  1.06 us
  transfers between devices with their start and end apart: 14, of which 6 were waited for; matrix products, arithmetic and copies ran while one was open for 2% of the time, Pallas kernels for 35%

profile of v9, /device:TPU:0, one launch (start us, length us, event | category | flops | bytes accessed | tf_op | source)
XLA Modules:
  0.0 51.6 jit_solution(3900992467289856870)
XLA Ops:
  0.0 0.5 collective-permute-start.1
  0.5 0.1 collective-permute-start
  0.5 2.9 %collective-permute-start.4 = (bf16[256,2048]{1,0:T(8,128)(2,1)}, bf16[256,2048]{1,0:T(8,128)(2,1)S(1)}, u32[]{:S(2)}, u32[]{:S(2)}) collective-permute-start(bf16[256,2048]{1,0:T(8,128)(2,1)} %bitcast.11), channel_id=1, source_target_pairs={{0,8},{4,12},{8,0},{12,4},{1,9},{5,13},{9,1},{13,5},{2,10},{6,14},... | collective-permute-start | bytes 3145736 | tf_op jit(solution)/shard_map/ppermute | solution.py:384
  3.5 9.3 %attend.1 = (bf16[128,2048]{1,0:T(8,128)(2,1)}, bf16[128,128]{1,0:T(8,128)(2,1)}, bf16[128,1024]{1,0:T(8,128)(2,1)}) custom-call(s32[64]{0:T(128)} %lengths.1, s32[1]{0:T(128)} %bitcast.place, s32[1]{0:T(128)} %bitcast.1.column.refs_0_, s32[1,64]{1,0:T(1,128)} %bitcast.14, bf16[64,2,2048]{2,1,0:T(2,128)(2,1)} %queries_hbm.1, ...), custom_call_target="tpu_custom_call" | custom-call | flops 1024 | bytes 1024 | tf_op jit(solution)/shard_map/attend/pallas_call | solution.py:220
  12.8 1.6 %collective-permute-start.2 = (bf16[128,1024]{1,0:T(8,128)(2,1)}, bf16[128,1024]{1,0:T(8,128)(2,1)S(1)}, u32[]{:S(2)}, u32[]{:S(2)}) collective-permute-start(bf16[128,1024]{1,0:T(8,128)(2,1)} %get-tuple-element.34), channel_id=1, source_target_pairs={{0,1},{1,0},{2,3},{3,2},{4,5},{5,4},{6,7},{7,6},{8,9},{9,8},{10,11... | collective-permute-start | bytes 786440 | tf_op jit(solution)/shard_map/ppermute | solution.py:384
  14.5 0.6 %collective-permute-start.5 = (bf16[192,1024]{1,0:T(8,128)(2,1)S(1)}, bf16[192,1024]{1,0:T(8,128)(2,1)S(1)}, u32[]{:S(2)}, u32[]{:S(2)}) collective-permute-start(bf16[192,1024]{1,0:T(8,128)(2,1)S(1)} %bitcast.13), channel_id=1, source_target_pairs={{0,8},{4,12},{8,0},{12,4},{1,9},{5,13},{9,1},{13,5},{2,10},{6,14},... | collective-permute-start | bytes 1179656 | tf_op jit(solution)/shard_map/ppermute | solution.py:384
  15.1 7.3 %project.1 = (bf16[128,1024]{1,0:T(8,128)(2,1)}, bf16[128,1024]{1,0:T(8,128)(2,1)}, bf16[128,1024]{1,0:T(8,128)(2,1)}) custom-call(s32[1]{0:T(128)} %bitcast.1.column.refs_0_, bf16[128,2048]{1,0:T(8,128)(2,1)} %get-tuple-element.30.refs_1_.attended, bf16[2048,4096]{1,0:T(8,128)(2,1)} %refs_2_.1), custom_call_target="tpu_custom_call" | custom-call | flops 1024 | bytes 1024 | tf_op jit(solution)/shard_map/project/pallas_call | solution.py:297
  22.4 1.1 %add_convert_fusion = bf16[128,1024]{1,0:T(8,128)(2,1)S(1)} fusion(bf16[128,1024]{1,0:T(8,128)(2,1)S(1)} %collective-permute-done.2, bf16[128,1024]{1,0:T(8,128)(2,1)} %get-tuple-element.37), kind=kLoop, calls=%fused_computation | loop fusion | flops 524288 | bytes 786432 | tf_op jit(solution)/shard_map/convert_element_type | solution.py:450
  23.5 2.7 %collective-permute-start.6 = (bf16[128,1024]{1,0:T(8,128)(2,1)S(1)}, bf16[128,1024]{1,0:T(8,128)(2,1)S(1)}, u32[]{:S(2)}, u32[]{:S(2)}) collective-permute-start(bf16[128,1024]{1,0:T(8,128)(2,1)S(1)} %add_convert_fusion), channel_id=1, source_target_pairs={{0,2},{1,3},{2,0},{3,1},{4,6},{5,7},{6,4},{7,5},{8,10},{9,11},{10,... | collective-permute-start | bytes 786440 | tf_op jit(solution)/shard_map/ppermute | solution.py:384
  26.2 9.3 %collective-permute-done.5.refs_8_ = bf16[192,1024]{1,0:T(8,128)(2,1)S(1)} collective-permute-done((bf16[192,1024]{1,0:T(8,128)(2,1)S(1)}, bf16[192,1024]{1,0:T(8,128)(2,1)S(1)}, u32[]{:S(2)}, u32[]{:S(2)}) %collective-permute-start.5) | collective-permute-done | bytes 393248 | tf_op jit(solution)/shard_map/ppermute | solution.py:384
  35.4 1.9 %collective-permute-done.6.refs_1_ = bf16[128,1024]{1,0:T(8,128)(2,1)S(1)} collective-permute-done((bf16[128,1024]{1,0:T(8,128)(2,1)S(1)}, bf16[128,1024]{1,0:T(8,128)(2,1)S(1)}, u32[]{:S(2)}, u32[]{:S(2)}) %collective-permute-start.6) | collective-permute-done | bytes 262176 | tf_op jit(solution)/shard_map/ppermute | solution.py:384
  37.3 0.0 collective-permute-start.8
  37.3 0.7 %collective-permute-start.7 = (bf16[64,1024]{1,0:T(8,128)(2,1)S(1)}, bf16[64,1024]{1,0:T(8,128)(2,1)S(1)}, u32[]{:S(2)}, u32[]{:S(2)}) collective-permute-start(bf16[64,1024]{1,0:T(8,128)(2,1)S(1)} %slice_bitcast_fusion), channel_id=1, source_target_pairs={{0,8},{4,12},{8,0},{12,4},{1,9},{5,13},{9,1},{13,5},{2,10},{6,14},... | collective-permute-start | bytes 393224 | tf_op jit(solution)/shard_map/ppermute | solution.py:384
  38.0 0.8 %collective-permute-start.3 = (bf16[128,1024]{1,0:T(8,128)(2,1)}, bf16[128,1024]{1,0:T(8,128)(2,1)S(1)}, u32[]{:S(2)}, u32[]{:S(2)}) collective-permute-start(bf16[128,1024]{1,0:T(8,128)(2,1)} %get-tuple-element.35), channel_id=1, source_target_pairs={{0,1},{1,0},{2,3},{3,2},{4,5},{5,4},{6,7},{7,6},{8,9},{9,8},{10,11... | collective-permute-start | bytes 786440 | tf_op jit(solution)/shard_map/ppermute | solution.py:384
  38.8 1.1 %collective-permute-done.8.refs_3_ = bf16[256,2048]{1,0:T(8,128)(2,1)S(1)} collective-permute-done((bf16[256,2048]{1,0:T(8,128)(2,1)S(1)}, bf16[256,2048]{1,0:T(8,128)(2,1)S(1)}, u32[]{:S(2)}, u32[]{:S(2)}) %collective-permute-start.8) | collective-permute-done | bytes 1048608 | tf_op jit(solution)/shard_map/ppermute | solution.py:384
  40.0 1.7 %low.1.refs_2_ = bf16[64,128]{1,0:T(8,128)(2,1)S(1)} custom-call(bf16[128,2048]{1,0:T(8,128)(2,1)S(1)} %copy-done, bf16[128,128]{1,0:T(8,128)(2,1)S(1)} %copy-done.3, bf16[256,2048]{1,0:T(8,128)(2,1)S(1)} %bitcast.12, bf16[256,2048]{1,0:T(8,128)(2,1)S(1)} %collective-permute-done.1.refs_1_, bf16[256,2048]{1,0:T(8,128)(2,1)S(1)} %collective-permute-done.4.refs_2_, ...), custom_call_target="tpu_custom_call" | custom-call | flops 1024 | bytes 1024 | tf_op jit(solution)/shard_map/low/pallas_call | solution.py:335
  41.6 1.6 %collective-permute-done.7.refs_9_ = bf16[64,1024]{1,0:T(8,128)(2,1)S(1)} collective-permute-done((bf16[64,1024]{1,0:T(8,128)(2,1)S(1)}, bf16[64,1024]{1,0:T(8,128)(2,1)S(1)}, u32[]{:S(2)}, u32[]{:S(2)}) %collective-permute-start.7) | collective-permute-done | bytes 131104 | tf_op jit(solution)/shard_map/ppermute | solution.py:384
  43.3 1.0 %collective-permute-start.10 = (bf16[64,128]{1,0:T(8,128)(2,1)S(1)}, bf16[64,128]{1,0:T(8,128)(2,1)S(1)}, u32[]{:S(2)}, u32[]{:S(2)}) collective-permute-start(bf16[64,128]{1,0:T(8,128)(2,1)S(1)} %low.1.refs_2_), channel_id=1, source_target_pairs={{0,2},{1,3},{2,0},{3,1},{4,6},{5,7},{6,4},{7,5},{8,10},{9,11},{10,... | collective-permute-start | bytes 49160 | tf_op jit(solution)/shard_map/ppermute | solution.py:384
  44.3 1.7 %collective-permute-start.11 = (bf16[64,128]{1,0:T(8,128)(2,1)S(1)}, bf16[64,128]{1,0:T(8,128)(2,1)S(1)}, u32[]{:S(2)}, u32[]{:S(2)}) collective-permute-start(bf16[64,128]{1,0:T(8,128)(2,1)S(1)} %low.1.refs_2_), channel_id=1, source_target_pairs={{0,3},{1,2},{2,1},{3,0},{4,7},{5,6},{6,5},{7,4},{8,11},{9,10},{10,... | collective-permute-start | bytes 49160 | tf_op jit(solution)/shard_map/ppermute | solution.py:384
  45.9 0.8 %collective-permute-start.9 = (bf16[64,128]{1,0:T(8,128)(2,1)S(1)}, bf16[64,128]{1,0:T(8,128)(2,1)S(1)}, u32[]{:S(2)}, u32[]{:S(2)}) collective-permute-start(bf16[64,128]{1,0:T(8,128)(2,1)S(1)} %low.1.refs_2_), channel_id=1, source_target_pairs={{0,1},{1,0},{2,3},{3,2},{4,5},{5,4},{6,7},{7,6},{8,9},{9,8},{10,11... | collective-permute-start | bytes 49160 | tf_op jit(solution)/shard_map/ppermute | solution.py:384
  46.8 0.1 convert_add_fusion.refs_0_
  46.8 1.1 %collective-permute-done.10.refs_4_ = bf16[64,128]{1,0:T(8,128)(2,1)S(1)} collective-permute-done((bf16[64,128]{1,0:T(8,128)(2,1)S(1)}, bf16[64,128]{1,0:T(8,128)(2,1)S(1)}, u32[]{:S(2)}, u32[]{:S(2)}) %collective-permute-start.10) | collective-permute-done | bytes 16416 | tf_op jit(solution)/shard_map/ppermute | solution.py:384
  47.9 1.9 %collective-permute-done.11.refs_5_ = bf16[64,128]{1,0:T(8,128)(2,1)S(1)} collective-permute-done((bf16[64,128]{1,0:T(8,128)(2,1)S(1)}, bf16[64,128]{1,0:T(8,128)(2,1)S(1)}, u32[]{:S(2)}, u32[]{:S(2)}) %collective-permute-start.11) | collective-permute-done | bytes 16416 | tf_op jit(solution)/shard_map/ppermute | solution.py:384
  49.8 1.7 %combine.1 = bf16[64,2,1024]{2,1,0:T(2,128)(2,1)} custom-call(bf16[128,128]{1,0:T(8,128)(2,1)S(1)} %copy-done.3, f32[128,1024]{1,0:T(8,128)S(1)} %convert_add_fusion.refs_0_, bf16[128,1024]{1,0:T(8,128)(2,1)S(1)} %collective-permute-done.6.refs_1_, bf16[64,128]{1,0:T(8,128)(2,1)S(1)} %low.1.refs_2_, bf16[64,128]{1,0:T(8,128)(2,1)S(1)} %collective-permute-done.9.refs_3_, ...), custom_call_target="tpu_custom_call" | custom-call | flops 1024 | bytes 1024 | tf_op jit(solution)/shard_map/combine/pallas_call | solution.py:373
  (22 shorter events, 0.1 us)
Async XLA Ops:
  0.0 12.7 %collective-permute-start.1 = (bf16[256,2048]{1,0:T(8,128)(2,1)}, bf16[256,2048]{1,0:T(8,128)(2,1)S(1)}, u32[]{:S(2)}, u32[]{:S(2)}) collective-permute-start(bf16[256,2048]{1,0:T(8,128)(2,1)} %bitcast.10), channel_id=1, source_target_pairs={{0,4},{4,0},{8,12},{12,8},{1,5},{5,1},{9,13},{13,9},{2,6},{6,2},{1... | collective-permute-start | bytes 3145736 | tf_op jit(solution)/shard_map/ppermute | solution.py:384
  0.5 12.3 %collective-permute-start = (bf16[256,1024]{1,0:T(8,128)(2,1)}, bf16[256,1024]{1,0:T(8,128)(2,1)S(1)}, u32[]{:S(2)}, u32[]{:S(2)}) collective-permute-start(bf16[256,1024]{1,0:T(8,128)(2,1)} %bitcast.8), channel_id=1, source_target_pairs={{0,4},{4,0},{8,12},{12,8},{1,5},{5,1},{9,13},{13,9},{2,6},{6,2},{1... | collective-permute-start | bytes 1572872 | tf_op jit(solution)/shard_map/ppermute | solution.py:384
  0.5 34.9 %collective-permute-start.4 = (bf16[256,2048]{1,0:T(8,128)(2,1)}, bf16[256,2048]{1,0:T(8,128)(2,1)S(1)}, u32[]{:S(2)}, u32[]{:S(2)}) collective-permute-start(bf16[256,2048]{1,0:T(8,128)(2,1)} %bitcast.11), channel_id=1, source_target_pairs={{0,8},{4,12},{8,0},{12,4},{1,9},{5,13},{9,1},{13,5},{2,10},{6,14},... | collective-permute-start | bytes 3145736 | tf_op jit(solution)/shard_map/ppermute | solution.py:384
  3.5 10.9 %copy-start.1 = (bf16[4,64,1024]{2,1,0:T(8,128)(2,1)S(1)}, bf16[4,64,1024]{2,1,0:T(8,128)(2,1)}, u32[]{:S(2)}) copy-start(bf16[4,64,1024]{2,1,0:T(8,128)(2,1)} %param.19) | copy-start | bytes 1572868
  12.8 9.7 %collective-permute-start.2 = (bf16[128,1024]{1,0:T(8,128)(2,1)}, bf16[128,1024]{1,0:T(8,128)(2,1)S(1)}, u32[]{:S(2)}, u32[]{:S(2)}) collective-permute-start(bf16[128,1024]{1,0:T(8,128)(2,1)} %get-tuple-element.34), channel_id=1, source_target_pairs={{0,1},{1,0},{2,3},{3,2},{4,5},{5,4},{6,7},{7,6},{8,9},{9,8},{10,11... | collective-permute-start | bytes 786440 | tf_op jit(solution)/shard_map/ppermute | solution.py:384
  14.4 25.5 %copy-start = (bf16[128,2048]{1,0:T(8,128)(2,1)S(1)}, bf16[128,2048]{1,0:T(8,128)(2,1)}, u32[]{:S(2)}) copy-start(bf16[128,2048]{1,0:T(8,128)(2,1)} %get-tuple-element.30.refs_1_.attended) | copy-start | bytes 1572868
  14.4 25.5 %copy-start.2 = (bf16[4,64,2048]{2,1,0:T(8,128)(2,1)S(1)}, bf16[4,64,2048]{2,1,0:T(8,128)(2,1)}, u32[]{:S(2)}) copy-start(bf16[4,64,2048]{2,1,0:T(8,128)(2,1)} %param.18) | copy-start | bytes 3145732
  14.4 25.5 %copy-start.3 = (bf16[128,128]{1,0:T(8,128)(2,1)S(1)}, bf16[128,128]{1,0:T(8,128)(2,1)}, u32[]{:S(2)}) copy-start(bf16[128,128]{1,0:T(8,128)(2,1)} %get-tuple-element.27.marks) | copy-start | bytes 98308
  14.5 21.0 %collective-permute-start.5 = (bf16[192,1024]{1,0:T(8,128)(2,1)S(1)}, bf16[192,1024]{1,0:T(8,128)(2,1)S(1)}, u32[]{:S(2)}, u32[]{:S(2)}) collective-permute-start(bf16[192,1024]{1,0:T(8,128)(2,1)S(1)} %bitcast.13), channel_id=1, source_target_pairs={{0,8},{4,12},{8,0},{12,4},{1,9},{5,13},{9,1},{13,5},{2,10},{6,14},... | collective-permute-start | bytes 1179656 | tf_op jit(solution)/shard_map/ppermute | solution.py:384
  22.4 24.4 %copy-start.4 = (bf16[128,1024]{1,0:T(8,128)(2,1)S(1)}, bf16[128,1024]{1,0:T(8,128)(2,1)}, u32[]{:S(2)}) copy-start(bf16[128,1024]{1,0:T(8,128)(2,1)} %get-tuple-element.36) | copy-start | bytes 786436
  23.5 13.8 %collective-permute-start.6 = (bf16[128,1024]{1,0:T(8,128)(2,1)S(1)}, bf16[128,1024]{1,0:T(8,128)(2,1)S(1)}, u32[]{:S(2)}, u32[]{:S(2)}) collective-permute-start(bf16[128,1024]{1,0:T(8,128)(2,1)S(1)} %add_convert_fusion), channel_id=1, source_target_pairs={{0,2},{1,3},{2,0},{3,1},{4,6},{5,7},{6,4},{7,5},{8,10},{9,11},{10,... | collective-permute-start | bytes 786440 | tf_op jit(solution)/shard_map/ppermute | solution.py:384
  37.3 2.7 %collective-permute-start.8 = (bf16[256,2048]{1,0:T(8,128)(2,1)S(1)}, bf16[256,2048]{1,0:T(8,128)(2,1)S(1)}, u32[]{:S(2)}, u32[]{:S(2)}) collective-permute-start(bf16[256,2048]{1,0:T(8,128)(2,1)S(1)} %collective-permute-done.4.refs_2_), channel_id=1, source_target_pairs={{0,4},{4,0},{8,12},{12,8},{1,5},{5,1},{9,13},{13,9},{2,6},{6,2},{1... | collective-permute-start | bytes 3145736 | tf_op jit(solution)/shard_map/ppermute | solution.py:384
  37.3 6.0 %collective-permute-start.7 = (bf16[64,1024]{1,0:T(8,128)(2,1)S(1)}, bf16[64,1024]{1,0:T(8,128)(2,1)S(1)}, u32[]{:S(2)}, u32[]{:S(2)}) collective-permute-start(bf16[64,1024]{1,0:T(8,128)(2,1)S(1)} %slice_bitcast_fusion), channel_id=1, source_target_pairs={{0,8},{4,12},{8,0},{12,4},{1,9},{5,13},{9,1},{13,5},{2,10},{6,14},... | collective-permute-start | bytes 393224 | tf_op jit(solution)/shard_map/ppermute | solution.py:384
  38.0 8.8 %collective-permute-start.3 = (bf16[128,1024]{1,0:T(8,128)(2,1)}, bf16[128,1024]{1,0:T(8,128)(2,1)S(1)}, u32[]{:S(2)}, u32[]{:S(2)}) collective-permute-start(bf16[128,1024]{1,0:T(8,128)(2,1)} %get-tuple-element.35), channel_id=1, source_target_pairs={{0,1},{1,0},{2,3},{3,2},{4,5},{5,4},{6,7},{7,6},{8,9},{9,8},{10,11... | collective-permute-start | bytes 786440 | tf_op jit(solution)/shard_map/ppermute | solution.py:384
  43.3 6.6 %collective-permute-start.12 = (bf16[192,1024]{1,0:T(8,128)(2,1)S(1)}, bf16[192,1024]{1,0:T(8,128)(2,1)S(1)}, u32[]{:S(2)}, u32[]{:S(2)}) collective-permute-start(bf16[192,1024]{1,0:T(8,128)(2,1)S(1)} %collective-permute-done.5.refs_8_), channel_id=1, source_target_pairs={{0,4},{4,0},{8,12},{12,8},{1,5},{5,1},{9,13},{13,9},{2,6},{6,2},{1... | collective-permute-start | bytes 1179656 | tf_op jit(solution)/shard_map/ppermute | solution.py:384
  43.3 4.6 %collective-permute-start.10 = (bf16[64,128]{1,0:T(8,128)(2,1)S(1)}, bf16[64,128]{1,0:T(8,128)(2,1)S(1)}, u32[]{:S(2)}, u32[]{:S(2)}) collective-permute-start(bf16[64,128]{1,0:T(8,128)(2,1)S(1)} %low.1.refs_2_), channel_id=1, source_target_pairs={{0,2},{1,3},{2,0},{3,1},{4,6},{5,7},{6,4},{7,5},{8,10},{9,11},{10,... | collective-permute-start | bytes 49160 | tf_op jit(solution)/shard_map/ppermute | solution.py:384
  44.3 5.6 %collective-permute-start.11 = (bf16[64,128]{1,0:T(8,128)(2,1)S(1)}, bf16[64,128]{1,0:T(8,128)(2,1)S(1)}, u32[]{:S(2)}, u32[]{:S(2)}) collective-permute-start(bf16[64,128]{1,0:T(8,128)(2,1)S(1)} %low.1.refs_2_), channel_id=1, source_target_pairs={{0,3},{1,2},{2,1},{3,0},{4,7},{5,6},{6,5},{7,4},{8,11},{9,10},{10,... | collective-permute-start | bytes 49160 | tf_op jit(solution)/shard_map/ppermute | solution.py:384
  45.9 3.9 %collective-permute-start.9 = (bf16[64,128]{1,0:T(8,128)(2,1)S(1)}, bf16[64,128]{1,0:T(8,128)(2,1)S(1)}, u32[]{:S(2)}, u32[]{:S(2)}) collective-permute-start(bf16[64,128]{1,0:T(8,128)(2,1)S(1)} %low.1.refs_2_), channel_id=1, source_target_pairs={{0,1},{1,0},{2,3},{3,2},{4,5},{5,4},{6,7},{7,6},{8,9},{9,8},{10,11... | collective-permute-start | bytes 49160 | tf_op jit(solution)/shard_map/ppermute | solution.py:384
  46.8 3.1 %collective-permute-start.13 = (bf16[64,1024]{1,0:T(8,128)(2,1)S(1)}, bf16[64,1024]{1,0:T(8,128)(2,1)S(1)}, u32[]{:S(2)}, u32[]{:S(2)}) collective-permute-start(bf16[64,1024]{1,0:T(8,128)(2,1)S(1)} %collective-permute-done.7.refs_9_), channel_id=1, source_target_pairs={{0,4},{4,0},{8,12},{12,8},{1,5},{5,1},{9,13},{13,9},{2,6},{6,2},{1... | collective-permute-start | bytes 393224 | tf_op jit(solution)/shard_map/ppermute | solution.py:384

commit v10 on v9

--- a/solution.py
+++ b/solution.py
@@ -13,6 +13,7 @@
 NEGATIVE = -1e30
 LANES = 128
 KERNEL_VMEM = 56 * 1024 * 1024
+PROJECT_VMEM = 50 * 1024 * 1024
 SMALL_COST = pl.CostEstimate(flops=1024, bytes_accessed=1024, transcendentals=0)
 SMALL_VMEM = 16 * 1024 * 1024
 
@@ -308,7 +309,7 @@
             ],
         ),
         out_shape=[jax.ShapeDtypeStruct((rows, columns), BF16)] * count,
-        compiler_params=pltpu.CompilerParams(vmem_limit_bytes=KERNEL_VMEM),
+        compiler_params=pltpu.CompilerParams(vmem_limit_bytes=PROJECT_VMEM),
         cost_estimate=SMALL_COST,
         name="project",
     )(column, attended, weight)

time: 51.8 us -> 51.8 us (level)
  starting transfers between devices: 13.4 us -> 15.7 us
  Pallas kernels: 20 us -> 18.3 us
  local copies, waits for them, and re-layouts: 0.06 us -> 1.09 us
  other arithmetic: 1.12 us -> 0.13 us
    ppermute x14, starting transfers between devices: 13.4 us -> 15.7 us  [swap(): return lax.ppermute(value, axis, [(i, i ^ k) for i in range(count)])]
    pallas_call x1, Pallas kernels: 7.34 us -> 5.56 us  [project(): pl.pallas_call(functools.partial(project_kernel, count), grid_spec=pltpu....]
    unnamed x10 -> x8, local copies, waits for them, and re-layouts: 0.02 us -> 1.05 us
    convert_element_type x1, other arithmetic: 1.06 us -> 0.07 us  [body(): outward.append(swap(pair.astype(BF16), 'tensor', k))]
    ppermute x14, waiting for transfers between devices: 16.9 us -> 16.4 us  [swap(): return lax.ppermute(value, axis, [(i, i ^ k) for i in range(count)])]
  transfers between devices with their start and end apart: 14 -> 14, of which waited for: 6 -> 5; matrix products, arithmetic and copies ran while one was open for 2% -> 0% of each run, Pallas kernels for 35% -> 32%
where the time goes in v10:
time: 51.8 us; the launch traced here: 51.6 us
  Pallas kernels  18.3 us (35%)
  waiting for transfers between devices  16.4 us (32%)
  starting transfers between devices  15.7 us (30%)
  local copies, waits for them, and re-layouts  1.09 us (2%)
    ppermute x14, waiting for transfers between devices, swap(): return lax.ppermute(value, axis, [(i, i ^ k) for i in range(count)])  16.4 us
    ppermute x14, starting transfers between devices, swap(): return lax.ppermute(value, axis, [(i, i ^ k) for i in range(count)])  15.7 us
    pallas_call x1, Pallas kernels, attend(): pl.pallas_call(functools.partial(attend_kernel, blocks - 1, resident, blo...  9.27 us
    pallas_call x1, Pallas kernels, project(): pl.pallas_call(functools.partial(project_kernel, count), grid_spec=pltpu....  5.56 us
    pallas_call x1, Pallas kernels, combine(): pl.pallas_call(functools.partial(combine_kernel, 1 + len(partials), len(l...  1.75 us
    pallas_call x1, Pallas kernels, low_partial(): pl.pallas_call(functools.partial(low_kernel, rank), out_shape=jax.ShapeDt...  1.67 us
    unnamed x8, local copies, waits for them, and re-layouts  1.05 us
  transfers between devices with their start and end apart: 14, of which 5 were waited for; matrix products, arithmetic and copies ran while one was open for 0% of the time, Pallas kernels for 32%

profile of v10, /device:TPU:0, one launch (start us, length us, event | category | flops | bytes accessed | tf_op | source)
XLA Modules:
  0.0 51.6 jit_solution(10086367504601237654)
XLA Ops:
  0.0 0.5 collective-permute-start.1
  0.5 0.1 collective-permute-start
  0.5 2.9 %collective-permute-start.4 = (bf16[256,2048]{1,0:T(8,128)(2,1)}, bf16[256,2048]{1,0:T(8,128)(2,1)S(1)}, u32[]{:S(2)}, u32[]{:S(2)}) collective-permute-start(bf16[256,2048]{1,0:T(8,128)(2,1)} %bitcast.11), channel_id=1, source_target_pairs={{0,8},{4,12},{8,0},{12,4},{1,9},{5,13},{9,1},{13,5},{2,10},{6,14},... | collective-permute-start | bytes 3145736 | tf_op jit(solution)/shard_map/ppermute | solution.py:385
  3.5 9.3 %attend.1 = (bf16[128,2048]{1,0:T(8,128)(2,1)}, bf16[128,128]{1,0:T(8,128)(2,1)}, bf16[128,1024]{1,0:T(8,128)(2,1)}) custom-call(s32[64]{0:T(128)} %lengths.1, s32[1]{0:T(128)} %bitcast.place, s32[1]{0:T(128)} %bitcast.1.column.refs_0_, s32[1,64]{1,0:T(1,128)} %bitcast.14, bf16[64,2,2048]{2,1,0:T(2,128)(2,1)} %queries_hbm.1, ...), custom_call_target="tpu_custom_call" | custom-call | flops 1024 | bytes 1024 | tf_op jit(solution)/shard_map/attend/pallas_call | solution.py:221
  12.8 1.6 %collective-permute-start.2 = (bf16[128,1024]{1,0:T(8,128)(2,1)}, bf16[128,1024]{1,0:T(8,128)(2,1)S(1)}, u32[]{:S(2)}, u32[]{:S(2)}) collective-permute-start(bf16[128,1024]{1,0:T(8,128)(2,1)} %get-tuple-element.34), channel_id=1, source_target_pairs={{0,1},{1,0},{2,3},{3,2},{4,5},{5,4},{6,7},{7,6},{8,9},{9,8},{10,11... | collective-permute-start | bytes 786440 | tf_op jit(solution)/shard_map/ppermute | solution.py:385
  14.4 0.6 %collective-permute-start.5 = (bf16[192,1024]{1,0:T(8,128)(2,1)S(1)}, bf16[192,1024]{1,0:T(8,128)(2,1)S(1)}, u32[]{:S(2)}, u32[]{:S(2)}) collective-permute-start(bf16[192,1024]{1,0:T(8,128)(2,1)S(1)} %bitcast.13), channel_id=1, source_target_pairs={{0,8},{4,12},{8,0},{12,4},{1,9},{5,13},{9,1},{13,5},{2,10},{6,14},... | collective-permute-start | bytes 1179656 | tf_op jit(solution)/shard_map/ppermute | solution.py:385
  15.0 1.0 %copy-done = bf16[128,2048]{1,0:T(8,128)(2,1)S(1)} copy-done((bf16[128,2048]{1,0:T(8,128)(2,1)S(1)}, bf16[128,2048]{1,0:T(8,128)(2,1)}, u32[]{:S(2)}) %copy-start) | copy-done | bytes 524312
  16.1 5.6 %project.1 = (bf16[128,1024]{1,0:T(8,128)(2,1)S(1)}, bf16[128,1024]{1,0:T(8,128)(2,1)S(1)}, bf16[128,1024]{1,0:T(8,128)(2,1)S(1)}) custom-call(s32[1]{0:T(128)} %bitcast.1.column.refs_0_, bf16[128,2048]{1,0:T(8,128)(2,1)S(1)} %copy-done, bf16[2048,4096]{1,0:T(8,128)(2,1)} %refs_2_.1), custom_call_target="tpu_custom_call" | custom-call | flops 1024 | bytes 1024 | tf_op jit(solution)/shard_map/project/pallas_call | solution.py:298
  21.6 0.1 add_convert_fusion
  21.7 2.7 %collective-permute-start.6 = (bf16[128,1024]{1,0:T(8,128)(2,1)S(1)}, bf16[128,1024]{1,0:T(8,128)(2,1)S(1)}, u32[]{:S(2)}, u32[]{:S(2)}) collective-permute-start(bf16[128,1024]{1,0:T(8,128)(2,1)S(1)} %add_convert_fusion), channel_id=1, source_target_pairs={{0,2},{1,3},{2,0},{3,1},{4,6},{5,7},{6,4},{7,5},{8,10},{9,11},{10,... | collective-permute-start | bytes 786440 | tf_op jit(solution)/shard_map/ppermute | solution.py:385
  24.4 11.0 %collective-permute-done.5.refs_8_ = bf16[192,1024]{1,0:T(8,128)(2,1)S(1)} collective-permute-done((bf16[192,1024]{1,0:T(8,128)(2,1)S(1)}, bf16[192,1024]{1,0:T(8,128)(2,1)S(1)}, u32[]{:S(2)}, u32[]{:S(2)}) %collective-permute-start.5) | collective-permute-done | bytes 393248 | tf_op jit(solution)/shard_map/ppermute | solution.py:385
  35.4 0.3 collective-permute-done.6.refs_1_
  35.7 0.0 collective-permute-start.8
  35.7 1.5 %collective-permute-start.7 = (bf16[64,1024]{1,0:T(8,128)(2,1)S(1)}, bf16[64,1024]{1,0:T(8,128)(2,1)S(1)}, u32[]{:S(2)}, u32[]{:S(2)}) collective-permute-start(bf16[64,1024]{1,0:T(8,128)(2,1)S(1)} %slice_bitcast_fusion), channel_id=1, source_target_pairs={{0,8},{4,12},{8,0},{12,4},{1,9},{5,13},{9,1},{13,5},{2,10},{6,14},... | collective-permute-start | bytes 393224 | tf_op jit(solution)/shard_map/ppermute | solution.py:385
  37.3 1.6 %collective-permute-start.3 = (bf16[128,1024]{1,0:T(8,128)(2,1)S(1)}, bf16[128,1024]{1,0:T(8,128)(2,1)S(1)}, u32[]{:S(2)}, u32[]{:S(2)}) collective-permute-start(bf16[128,1024]{1,0:T(8,128)(2,1)S(1)} %get-tuple-element.35), channel_id=1, source_target_pairs={{0,1},{1,0},{2,3},{3,2},{4,5},{5,4},{6,7},{7,6},{8,9},{9,8},{10,11... | collective-permute-start | bytes 786440 | tf_op jit(solution)/shard_map/ppermute | solution.py:385
  38.8 1.7 %low.1.refs_2_ = bf16[64,128]{1,0:T(8,128)(2,1)S(1)} custom-call(bf16[128,2048]{1,0:T(8,128)(2,1)S(1)} %copy-done, bf16[128,128]{1,0:T(8,128)(2,1)S(1)} %copy-done.3, bf16[256,2048]{1,0:T(8,128)(2,1)S(1)} %bitcast.12, bf16[256,2048]{1,0:T(8,128)(2,1)S(1)} %collective-permute-done.1.refs_1_, bf16[256,2048]{1,0:T(8,128)(2,1)S(1)} %collective-permute-done.4.refs_2_, ...), custom_call_target="tpu_custom_call" | custom-call | flops 1024 | bytes 1024 | tf_op jit(solution)/shard_map/low/pallas_call | solution.py:336
  40.5 1.2 %collective-permute-done.7.refs_9_ = bf16[64,1024]{1,0:T(8,128)(2,1)S(1)} collective-permute-done((bf16[64,1024]{1,0:T(8,128)(2,1)S(1)}, bf16[64,1024]{1,0:T(8,128)(2,1)S(1)}, u32[]{:S(2)}, u32[]{:S(2)}) %collective-permute-start.7) | collective-permute-done | bytes 131104 | tf_op jit(solution)/shard_map/ppermute | solution.py:385
  41.7 2.6 %collective-permute-start.10 = (bf16[64,128]{1,0:T(8,128)(2,1)S(1)}, bf16[64,128]{1,0:T(8,128)(2,1)S(1)}, u32[]{:S(2)}, u32[]{:S(2)}) collective-permute-start(bf16[64,128]{1,0:T(8,128)(2,1)S(1)} %low.1.refs_2_), channel_id=1, source_target_pairs={{0,2},{1,3},{2,0},{3,1},{4,6},{5,7},{6,4},{7,5},{8,10},{9,11},{10,... | collective-permute-start | bytes 49160 | tf_op jit(solution)/shard_map/ppermute | solution.py:385
  44.3 1.3 %collective-permute-start.11 = (bf16[64,128]{1,0:T(8,128)(2,1)S(1)}, bf16[64,128]{1,0:T(8,128)(2,1)S(1)}, u32[]{:S(2)}, u32[]{:S(2)}) collective-permute-start(bf16[64,128]{1,0:T(8,128)(2,1)S(1)} %low.1.refs_2_), channel_id=1, source_target_pairs={{0,3},{1,2},{2,1},{3,0},{4,7},{5,6},{6,5},{7,4},{8,11},{9,10},{10,... | collective-permute-start | bytes 49160 | tf_op jit(solution)/shard_map/ppermute | solution.py:385
  45.6 0.2 collective-permute-start.9
  45.8 0.1 convert_add_fusion.refs_0_
  45.9 0.4 collective-permute-done.10.refs_4_
  46.3 3.5 %collective-permute-done.11.refs_5_ = bf16[64,128]{1,0:T(8,128)(2,1)S(1)} collective-permute-done((bf16[64,128]{1,0:T(8,128)(2,1)S(1)}, bf16[64,128]{1,0:T(8,128)(2,1)S(1)}, u32[]{:S(2)}, u32[]{:S(2)}) %collective-permute-start.11) | collective-permute-done | bytes 16416 | tf_op jit(solution)/shard_map/ppermute | solution.py:385
  49.8 1.8 %combine.1 = bf16[64,2,1024]{2,1,0:T(2,128)(2,1)} custom-call(bf16[128,128]{1,0:T(8,128)(2,1)S(1)} %copy-done.3, f32[128,1024]{1,0:T(8,128)S(1)} %convert_add_fusion.refs_0_, bf16[128,1024]{1,0:T(8,128)(2,1)S(1)} %collective-permute-done.6.refs_1_, bf16[64,128]{1,0:T(8,128)(2,1)S(1)} %low.1.refs_2_, bf16[64,128]{1,0:T(8,128)(2,1)S(1)} %collective-permute-done.9.refs_3_, ...), custom_call_target="tpu_custom_call" | custom-call | flops 1024 | bytes 1024 | tf_op jit(solution)/shard_map/combine/pallas_call | solution.py:374
  (20 shorter events, 0.1 us)
Async XLA Ops:
  0.0 12.7 %collective-permute-start.1 = (bf16[256,2048]{1,0:T(8,128)(2,1)}, bf16[256,2048]{1,0:T(8,128)(2,1)S(1)}, u32[]{:S(2)}, u32[]{:S(2)}) collective-permute-start(bf16[256,2048]{1,0:T(8,128)(2,1)} %bitcast.10), channel_id=1, source_target_pairs={{0,4},{4,0},{8,12},{12,8},{1,5},{5,1},{9,13},{13,9},{2,6},{6,2},{1... | collective-permute-start | bytes 3145736 | tf_op jit(solution)/shard_map/ppermute | solution.py:385
  0.5 12.3 %collective-permute-start = (bf16[256,1024]{1,0:T(8,128)(2,1)}, bf16[256,1024]{1,0:T(8,128)(2,1)S(1)}, u32[]{:S(2)}, u32[]{:S(2)}) collective-permute-start(bf16[256,1024]{1,0:T(8,128)(2,1)} %bitcast.8), channel_id=1, source_target_pairs={{0,4},{4,0},{8,12},{12,8},{1,5},{5,1},{9,13},{13,9},{2,6},{6,2},{1... | collective-permute-start | bytes 1572872 | tf_op jit(solution)/shard_map/ppermute | solution.py:385
  0.5 34.9 %collective-permute-start.4 = (bf16[256,2048]{1,0:T(8,128)(2,1)}, bf16[256,2048]{1,0:T(8,128)(2,1)S(1)}, u32[]{:S(2)}, u32[]{:S(2)}) collective-permute-start(bf16[256,2048]{1,0:T(8,128)(2,1)} %bitcast.11), channel_id=1, source_target_pairs={{0,8},{4,12},{8,0},{12,4},{1,9},{5,13},{9,1},{13,5},{2,10},{6,14},... | collective-permute-start | bytes 3145736 | tf_op jit(solution)/shard_map/ppermute | solution.py:385
  3.5 10.9 %copy-start.1 = (bf16[4,64,1024]{2,1,0:T(8,128)(2,1)S(1)}, bf16[4,64,1024]{2,1,0:T(8,128)(2,1)}, u32[]{:S(2)}) copy-start(bf16[4,64,1024]{2,1,0:T(8,128)(2,1)} %param.19) | copy-start | bytes 1572868
  12.8 8.9 %collective-permute-start.2 = (bf16[128,1024]{1,0:T(8,128)(2,1)}, bf16[128,1024]{1,0:T(8,128)(2,1)S(1)}, u32[]{:S(2)}, u32[]{:S(2)}) collective-permute-start(bf16[128,1024]{1,0:T(8,128)(2,1)} %get-tuple-element.34), channel_id=1, source_target_pairs={{0,1},{1,0},{2,3},{3,2},{4,5},{5,4},{6,7},{7,6},{8,9},{9,8},{10,11... | collective-permute-start | bytes 786440 | tf_op jit(solution)/shard_map/ppermute | solution.py:385
  14.4 21.0 %collective-permute-start.5 = (bf16[192,1024]{1,0:T(8,128)(2,1)S(1)}, bf16[192,1024]{1,0:T(8,128)(2,1)S(1)}, u32[]{:S(2)}, u32[]{:S(2)}) collective-permute-start(bf16[192,1024]{1,0:T(8,128)(2,1)S(1)} %bitcast.13), channel_id=1, source_target_pairs={{0,8},{4,12},{8,0},{12,4},{1,9},{5,13},{9,1},{13,5},{2,10},{6,14},... | collective-permute-start | bytes 1179656 | tf_op jit(solution)/shard_map/ppermute | solution.py:385
  15.0 1.0 %copy-start = (bf16[128,2048]{1,0:T(8,128)(2,1)S(1)}, bf16[128,2048]{1,0:T(8,128)(2,1)}, u32[]{:S(2)}) copy-start(bf16[128,2048]{1,0:T(8,128)(2,1)} %get-tuple-element.30.refs_1_.attended) | copy-start | bytes 1572868
  16.1 22.8 %copy-start.2 = (bf16[4,64,2048]{2,1,0:T(8,128)(2,1)S(1)}, bf16[4,64,2048]{2,1,0:T(8,128)(2,1)}, u32[]{:S(2)}) copy-start(bf16[4,64,2048]{2,1,0:T(8,128)(2,1)} %param.18) | copy-start | bytes 3145732
  16.1 22.8 %copy-start.3 = (bf16[128,128]{1,0:T(8,128)(2,1)S(1)}, bf16[128,128]{1,0:T(8,128)(2,1)}, u32[]{:S(2)}) copy-start(bf16[128,128]{1,0:T(8,128)(2,1)} %get-tuple-element.27.marks) | copy-start | bytes 98308
  21.7 14.0 %collective-permute-start.6 = (bf16[128,1024]{1,0:T(8,128)(2,1)S(1)}, bf16[128,1024]{1,0:T(8,128)(2,1)S(1)}, u32[]{:S(2)}, u32[]{:S(2)}) collective-permute-start(bf16[128,1024]{1,0:T(8,128)(2,1)S(1)} %add_convert_fusion), channel_id=1, source_target_pairs={{0,2},{1,3},{2,0},{3,1},{4,6},{5,7},{6,4},{7,5},{8,10},{9,11},{10,... | collective-permute-start | bytes 786440 | tf_op jit(solution)/shard_map/ppermute | solution.py:385
  35.7 3.2 %collective-permute-start.8 = (bf16[256,2048]{1,0:T(8,128)(2,1)S(1)}, bf16[256,2048]{1,0:T(8,128)(2,1)S(1)}, u32[]{:S(2)}, u32[]{:S(2)}) collective-permute-start(bf16[256,2048]{1,0:T(8,128)(2,1)S(1)} %collective-permute-done.4.refs_2_), channel_id=1, source_target_pairs={{0,4},{4,0},{8,12},{12,8},{1,5},{5,1},{9,13},{13,9},{2,6},{6,2},{1... | collective-permute-start | bytes 3145736 | tf_op jit(solution)/shard_map/ppermute | solution.py:385
  35.7 6.0 %collective-permute-start.7 = (bf16[64,1024]{1,0:T(8,128)(2,1)S(1)}, bf16[64,1024]{1,0:T(8,128)(2,1)S(1)}, u32[]{:S(2)}, u32[]{:S(2)}) collective-permute-start(bf16[64,1024]{1,0:T(8,128)(2,1)S(1)} %slice_bitcast_fusion), channel_id=1, source_target_pairs={{0,8},{4,12},{8,0},{12,4},{1,9},{5,13},{9,1},{13,5},{2,10},{6,14},... | collective-permute-start | bytes 393224 | tf_op jit(solution)/shard_map/ppermute | solution.py:385
  37.3 8.6 %collective-permute-start.3 = (bf16[128,1024]{1,0:T(8,128)(2,1)S(1)}, bf16[128,1024]{1,0:T(8,128)(2,1)S(1)}, u32[]{:S(2)}, u32[]{:S(2)}) collective-permute-start(bf16[128,1024]{1,0:T(8,128)(2,1)S(1)} %get-tuple-element.35), channel_id=1, source_target_pairs={{0,1},{1,0},{2,3},{3,2},{4,5},{5,4},{6,7},{7,6},{8,9},{9,8},{10,11... | collective-permute-start | bytes 786440 | tf_op jit(solution)/shard_map/ppermute | solution.py:385
  41.7 8.1 %collective-permute-start.12 = (bf16[192,1024]{1,0:T(8,128)(2,1)S(1)}, bf16[192,1024]{1,0:T(8,128)(2,1)S(1)}, u32[]{:S(2)}, u32[]{:S(2)}) collective-permute-start(bf16[192,1024]{1,0:T(8,128)(2,1)S(1)} %collective-permute-done.5.refs_8_), channel_id=1, source_target_pairs={{0,4},{4,0},{8,12},{12,8},{1,5},{5,1},{9,13},{13,9},{2,6},{6,2},{1... | collective-permute-start | bytes 1179656 | tf_op jit(solution)/shard_map/ppermute | solution.py:385
  41.7 4.6 %collective-permute-start.10 = (bf16[64,128]{1,0:T(8,128)(2,1)S(1)}, bf16[64,128]{1,0:T(8,128)(2,1)S(1)}, u32[]{:S(2)}, u32[]{:S(2)}) collective-permute-start(bf16[64,128]{1,0:T(8,128)(2,1)S(1)} %low.1.refs_2_), channel_id=1, source_target_pairs={{0,2},{1,3},{2,0},{3,1},{4,6},{5,7},{6,4},{7,5},{8,10},{9,11},{10,... | collective-permute-start | bytes 49160 | tf_op jit(solution)/shard_map/ppermute | solution.py:385
  44.3 5.5 %collective-permute-start.11 = (bf16[64,128]{1,0:T(8,128)(2,1)S(1)}, bf16[64,128]{1,0:T(8,128)(2,1)S(1)}, u32[]{:S(2)}, u32[]{:S(2)}) collective-permute-start(bf16[64,128]{1,0:T(8,128)(2,1)S(1)} %low.1.refs_2_), channel_id=1, source_target_pairs={{0,3},{1,2},{2,1},{3,0},{4,7},{5,6},{6,5},{7,4},{8,11},{9,10},{10,... | collective-permute-start | bytes 49160 | tf_op jit(solution)/shard_map/ppermute | solution.py:385
  45.6 4.2 %collective-permute-start.9 = (bf16[64,128]{1,0:T(8,128)(2,1)S(1)}, bf16[64,128]{1,0:T(8,128)(2,1)S(1)}, u32[]{:S(2)}, u32[]{:S(2)}) collective-permute-start(bf16[64,128]{1,0:T(8,128)(2,1)S(1)} %low.1.refs_2_), channel_id=1, source_target_pairs={{0,1},{1,0},{2,3},{3,2},{4,5},{5,4},{6,7},{7,6},{8,9},{9,8},{10,11... | collective-permute-start | bytes 49160 | tf_op jit(solution)/shard_map/ppermute | solution.py:385
  45.8 4.0 %collective-permute-start.13 = (bf16[64,1024]{1,0:T(8,128)(2,1)S(1)}, bf16[64,1024]{1,0:T(8,128)(2,1)S(1)}, u32[]{:S(2)}, u32[]{:S(2)}) collective-permute-start(bf16[64,1024]{1,0:T(8,128)(2,1)S(1)} %collective-permute-done.7.refs_9_), channel_id=1, source_target_pairs={{0,4},{4,0},{8,12},{12,8},{1,5},{5,1},{9,13},{13,9},{2,6},{6,2},{1... | collective-permute-start | bytes 393224 | tf_op jit(solution)/shard_map/ppermute | solution.py:385
